TPU v7x, 32 devices: a whole 2x2x4 slice. The times are simulated.
32 devices in a mesh: section: 2 (over x), dp: 16 (over z, y, core).
Axes of the slice: x: 2, y: 2, z: 4, core: 2. Of those that a mesh axis runs over, the one named last changes fastest.
Arguments:
- tokens: bfloat16 [2, 16, 1024, 512], P(None, 'dp'), may hold values from -6 to 6
- cotangent: bfloat16 [2, 2, 16, 1024, 512], P('section', None, 'dp'), may hold values from -6 to 6
- w_qkv: float32 [2, 512, 1536], P('section', 'dp'), may hold values from -0.25 to 0.25
- w_out: float32 [2, 512, 512], P('section', 'dp'), may hold values from -1 to 1
- w_gates: float32 [2, 2, 512, 512], P('section', None, 'dp'), may hold values from -0.25 to 0.25
- w_up: float32 [2, 512, 2048], P('section', 'dp'), may hold values from -0.25 to 0.25
- w_down: float32 [2, 2048, 512], P('section', 'dp'), may hold values from -0.125 to 0.125
- norm_gains: float32 [2, 2, 512], P('section', None, 'dp'), may hold values from 0.5 to 1.5
- gate_biases: float32 [2, 2, 512], P('section', None, 'dp'), may hold values from -4 to 4
Outputs:
- block_outputs: bfloat16 [2, 2, 16, 1024, 512], P('section', None, 'dp')
- input_grads: float32 [2, 2, 16, 1024, 512], P('section', None, 'dp')
- grad_qkv: float32 [2, 512, 1536], P('section', 'dp')
- grad_out: float32 [2, 512, 512], P('section', 'dp')
- grad_gates: float32 [2, 2, 512, 512], P('section', None, 'dp')
- grad_up: float32 [2, 512, 2048], P('section', 'dp')
- grad_down: float32 [2, 2048, 512], P('section', 'dp')
- grad_gains: float32 [2, 2, 512], P('section', None, 'dp')
- grad_biases: float32 [2, 2, 512], P('section', None, 'dp')
All inputs are finite; a program needn't handle non-finite values.
Results may differ from a plain program's by a relative error of at most 0.015.
Values may be sent and summed in bfloat16 or wider, within the bound.
No kernel may reach another device: no remote copies, remote signals or barrier semaphores. Data moves between devices by JAX's collectives and lax.ppermute only.
A program may use at most 576 MiB of HBM per device.

v0:
```python
import jax
import jax.numpy as jnp
from jax import lax
from jax.sharding import PartitionSpec as P

H = 8
HD = 64
FF = 2048


root_term = 0.7978845608
cube_term = 0.044715


def shifted(value, axis, steps):
    count = lax.axis_size(axis)
    leading, last = (max(0, -steps), min(count, count - steps))
    return lax.ppermute(value, axis, [(source, source + steps) for source in range(leading, last)])


def layer_norm(values, gain):
    average = jnp.mean(values, axis=-1, keepdims=True)
    centred = values - average
    spread = jnp.mean(centred * centred, axis=-1, keepdims=True)
    return centred * lax.rsqrt(spread + 1e-05) * gain


def smooth(hidden):
    return (
        0.5 * hidden * (1.0 + jnp.tanh(root_term * (hidden + cube_term * hidden * hidden * hidden)))
    )


def smooth_slope(hidden):
    inner = jnp.tanh(root_term * (hidden + cube_term * hidden * hidden * hidden))
    return 0.5 * (1.0 + inner) + 0.5 * hidden * (1.0 - inner * inner) * root_term * (
        1.0 + 3.0 * cube_term * hidden * hidden
    )


def dense(left, right):
    return jnp.dot(left, right, preferred_element_type=jnp.float32)


def cross(left, right):
    return lax.dot_general(
        left, right, (((0,), (0,)), ((), ())), preferred_element_type=jnp.float32
    )


def against(left, right):
    return lax.dot_general(
        left, right, (((1,), (1,)), ((), ())), preferred_element_type=jnp.float32
    )


def score_block(query, keyed, start):
    scores = jnp.einsum("sqhd,skhd->shqk", query, keyed, preferred_element_type=jnp.float32) * 0.125
    places = start + jnp.arange(query.shape[1])
    causal = places[:, None] >= jnp.arange(keyed.shape[1])[None, :]
    return jnp.where(causal, scores, -1e30)


def attend_forward(query, keyed, valued):
    length = query.shape[1]
    block = min(512, length)
    pieces = []
    totals = []
    for index in range(length // block):
        start = index * block
        finish = start + block
        scores = score_block(query[:, start:finish], keyed[:, :finish], start)
        highest = jnp.max(scores, axis=-1, keepdims=True)
        weights = jnp.exp(scores - highest)
        total = jnp.sum(weights, axis=-1, keepdims=True)
        probs = (weights / total).astype(jnp.bfloat16)
        pieces.append(
            jnp.einsum(
                "shqk,skhd->sqhd", probs, valued[:, :finish], preferred_element_type=jnp.float32
            )
        )
        totals.append((highest + jnp.log(total))[..., 0])
    return (jnp.concatenate(pieces, axis=1), jnp.concatenate(totals, axis=2))


def attend_backward(query, keyed, valued, normal, grad_out):
    length = query.shape[1]
    block = min(512, length)
    query_grads = []
    key_grad = jnp.zeros(keyed.shape, jnp.float32)
    value_grad = jnp.zeros(valued.shape, jnp.float32)
    for index in range(length // block):
        start = index * block
        finish = start + block
        scores = score_block(query[:, start:finish], keyed[:, :finish], start)
        probs = jnp.exp(scores - normal[:, :, start:finish, None])
        low_probs = probs.astype(jnp.bfloat16)
        piece = grad_out[:, start:finish]
        value_grad = value_grad.at[:, :finish].add(
            jnp.einsum("shqk,sqhd->skhd", low_probs, piece, preferred_element_type=jnp.float32)
        )
        prob_grad = jnp.einsum(
            "sqhd,skhd->shqk", piece, valued[:, :finish], preferred_element_type=jnp.float32
        )
        score_grad = probs * (prob_grad - jnp.sum(prob_grad * probs, axis=-1, keepdims=True))
        score_low = (score_grad * 0.125).astype(jnp.bfloat16)
        query_grads.append(
            jnp.einsum(
                "shqk,skhd->sqhd", score_low, keyed[:, :finish], preferred_element_type=jnp.float32
            )
        )
        key_grad = key_grad.at[:, :finish].add(
            jnp.einsum(
                "shqk,sqhd->skhd",
                score_low,
                query[:, start:finish],
                preferred_element_type=jnp.float32,
            )
        )
    query_grad = jnp.concatenate(query_grads, axis=1)
    return (
        query_grad.astype(jnp.bfloat16),
        key_grad.astype(jnp.bfloat16),
        value_grad.astype(jnp.bfloat16),
    )


def forward(inputs, weights):
    w_qkv, w_out, w_gates, w_up, w_down, gains, biases = weights
    seqs, length, width = inputs.shape
    flat = inputs.reshape(-1, width)
    normed = layer_norm(flat, gains[0].astype(jnp.float32)).astype(jnp.bfloat16)
    mixed = dense(normed, w_qkv).astype(jnp.bfloat16).reshape(seqs, length, 3, H, HD)
    attended, normal = attend_forward(mixed[:, :, 0], mixed[:, :, 1], mixed[:, :, 2])
    attended = attended.reshape(-1, width).astype(jnp.bfloat16)
    branch = dense(attended, w_out)
    opening = jax.nn.sigmoid(dense(normed, w_gates[0]) + biases[0].astype(jnp.float32))
    middle = flat + opening * branch
    second = layer_norm(middle, gains[1].astype(jnp.float32)).astype(jnp.bfloat16)
    hidden = dense(second, w_up)
    active = smooth(hidden).astype(jnp.bfloat16)
    feed = dense(active, w_down)
    closing = jax.nn.sigmoid(dense(second, w_gates[1]) + biases[1].astype(jnp.float32))
    result = middle + closing * feed
    kept = (
        flat,
        normed,
        mixed,
        normal,
        attended,
        branch,
        opening,
        middle,
        second,
        hidden,
        active,
        feed,
        closing,
    )
    return (result.reshape(seqs, length, width), kept)


def backward(grad_result, kept, weights):
    w_qkv, w_out, w_gates, w_up, w_down, gains, biases = weights
    (
        flat,
        normed,
        mixed,
        normal,
        attended,
        branch,
        opening,
        middle,
        second,
        hidden,
        active,
        feed,
        closing,
    ) = kept
    seqs, length, width = grad_result.shape
    grad_middle = grad_result.reshape(-1, width)
    feed_grad = (grad_middle * closing).astype(jnp.bfloat16)
    close_grad = (grad_middle * feed * closing * (1.0 - closing)).astype(jnp.bfloat16)
    down_grad = cross(active, feed_grad)
    active_grad = against(feed_grad, w_down)
    hidden_grad = (active_grad * smooth_slope(hidden)).astype(jnp.bfloat16)
    up_grad = cross(second, hidden_grad)
    close_weight = cross(second, close_grad)
    second_grad = against(hidden_grad, w_up) + against(close_grad, w_gates[1])
    ignored, pullback = jax.vjp(layer_norm, middle, gains[1].astype(jnp.float32))
    middle_part, gain_second = pullback(second_grad)
    grad_middle = grad_middle + middle_part
    branch_grad = (grad_middle * opening).astype(jnp.bfloat16)
    open_grad = (grad_middle * branch * opening * (1.0 - opening)).astype(jnp.bfloat16)
    out_grad = cross(attended, branch_grad)
    attended_grad = against(branch_grad, w_out).astype(jnp.bfloat16).reshape(seqs, length, H, HD)
    open_weight = cross(normed, open_grad)
    query_grad, key_grad, value_grad = attend_backward(
        mixed[:, :, 0], mixed[:, :, 1], mixed[:, :, 2], normal, attended_grad
    )
    mixed_grad = jnp.stack([query_grad, key_grad, value_grad], axis=2).reshape(-1, 3 * width)
    qkv_grad = cross(normed, mixed_grad)
    normed_grad = against(mixed_grad, w_qkv) + against(open_grad, w_gates[0])
    ignored, pullback = jax.vjp(layer_norm, flat, gains[0].astype(jnp.float32))
    flat_part, gain_first = pullback(normed_grad)
    grad_input = (grad_middle + flat_part).reshape(seqs, length, width)
    bias_grads = jnp.stack(
        [
            jnp.sum(open_grad.astype(jnp.float32), axis=0),
            jnp.sum(close_grad.astype(jnp.float32), axis=0),
        ]
    )
    grads = (
        qkv_grad,
        out_grad,
        jnp.stack([open_weight, close_weight]),
        up_grad,
        down_grad,
        jnp.stack([gain_first, gain_second]),
        bias_grads,
    )
    return (grad_input, grads)


def empty_forward(inputs):
    seqs, length, width = inputs.shape
    rows = seqs * length
    wide = FF
    floats = jnp.zeros((rows, width), jnp.float32)
    halves = jnp.zeros((rows, width), jnp.bfloat16)
    kept = (
        floats,
        halves,
        jnp.zeros((seqs, length, 3, H, HD), jnp.bfloat16),
        jnp.zeros((seqs, H, length), jnp.float32),
        halves,
        floats,
        floats,
        floats,
        halves,
        jnp.zeros((rows, wide), jnp.float32),
        jnp.zeros((rows, wide), jnp.bfloat16),
        floats,
        floats,
    )
    return (jnp.zeros((seqs, length, width), jnp.float32), kept)


def empty_backward(grad, weights):
    grads = tuple((jnp.zeros(weight.shape, jnp.float32) for weight in weights))
    return (jnp.zeros(grad.shape, jnp.float32), grads)


def per_device(tokens, cotangent, w_qkv, w_out, w_gates, w_up, w_down, norm_gains, gate_biases):
    first = lax.axis_index("section") == 0
    gathered = (
        lax.all_gather(w_qkv.astype(jnp.bfloat16), "dp", axis=1, tiled=True),
        lax.all_gather(w_out.astype(jnp.bfloat16), "dp", axis=1, tiled=True),
        lax.all_gather(w_gates.astype(jnp.bfloat16), "dp", axis=2, tiled=True),
        lax.all_gather(w_up.astype(jnp.bfloat16), "dp", axis=1, tiled=True),
        lax.all_gather(w_down.astype(jnp.bfloat16), "dp", axis=1, tiled=True),
        lax.all_gather(norm_gains.astype(jnp.bfloat16), "dp", axis=2, tiled=True),
        lax.all_gather(gate_biases.astype(jnp.bfloat16), "dp", axis=2, tiled=True),
    )
    weights = tuple((whole[0] for whole in gathered))
    number = tokens.shape[0]

    def run_forward(inputs):
        return forward(inputs, weights)

    def skip_forward(inputs):
        return empty_forward(inputs)

    received = jnp.zeros(tokens.shape[1:], jnp.bfloat16)
    outputs = []
    caches = []
    for tick in range(number + 1):
        own = tokens[min(tick, number - 1)]
        inputs = jnp.where(first, own, received).astype(jnp.float32)
        live = jnp.where(first, tick < number, tick >= 1)
        result, kept = lax.cond(live, run_forward, skip_forward, inputs)
        rounded = result.astype(jnp.bfloat16)
        outputs.append(rounded)
        caches.append(kept)
        if tick < number:
            received = shifted(rounded, "section", 1)
    block = jnp.stack([jnp.where(first, outputs[m], outputs[m + 1]) for m in range(number)])[None]

    def skip_backward(grad):
        return empty_backward(grad, weights)

    returned = jnp.zeros(tokens.shape[1:], jnp.bfloat16)
    input_parts = []
    totals = None
    for tick in range(number + 1):
        early_cache = caches[max(tick - 1, 0)]
        late_cache = caches[min(tick + 1, number)]

        def use_early(grad, early_cache=early_cache):
            return backward(grad, early_cache, weights)

        def use_late(grad, late_cache=late_cache):
            return backward(grad, late_cache, weights)

        seed = jnp.where(first, cotangent[0, max(tick - 1, 0)], cotangent[0, min(tick, number - 1)])
        grad_result = seed.astype(jnp.float32) + returned.astype(jnp.float32)
        valid = jnp.where(first, tick >= 1, tick < number)
        which = jnp.where(valid, jnp.where(first, 1, 2), 0).astype(jnp.int32)
        grad_input, grads = lax.switch(which, (skip_backward, use_early, use_late), grad_result)
        grads = tuple((grad[None] for grad in grads))
        input_parts.append(grad_input)
        shares = (
            lax.psum_scatter(grads[0], "dp", scatter_dimension=1, tiled=True),
            lax.psum_scatter(grads[1], "dp", scatter_dimension=1, tiled=True),
            lax.psum_scatter(grads[2], "dp", scatter_dimension=2, tiled=True),
            lax.psum_scatter(grads[3], "dp", scatter_dimension=1, tiled=True),
            lax.psum_scatter(grads[4], "dp", scatter_dimension=1, tiled=True),
            lax.psum_scatter(grads[5], "dp", scatter_dimension=2, tiled=True),
            lax.psum_scatter(grads[6], "dp", scatter_dimension=2, tiled=True),
        )
        if totals is None:
            totals = tuple(shares)
        else:
            totals = tuple((total + share for total, share in zip(totals, shares)))
        if tick < number:
            returned = shifted(grad_input.astype(jnp.bfloat16), "section", -1)
    in_grads = jnp.stack(
        [jnp.where(first, input_parts[m + 1], input_parts[m]) for m in range(number)]
    )[None]
    return (
        block,
        in_grads,
        totals[0],
        totals[1],
        totals[2],
        totals[3],
        totals[4],
        totals[5],
        totals[6],
    )


def solution(mesh):
    placed = (
        P(None, "dp", None, None),
        P("section", None, "dp", None, None),
        P("section", "dp", None),
        P("section", "dp", None),
        P("section", None, "dp", None),
        P("section", "dp", None),
        P("section", "dp", None),
        P("section", None, "dp"),
        P("section", None, "dp"),
    )
    return jax.shard_map(
        per_device,
        mesh=mesh,
        in_specs=placed,
        out_specs=(
            P("section", None, "dp", None, None),
            P("section", None, "dp", None, None),
            P("section", "dp", None),
            P("section", "dp", None),
            P("section", None, "dp", None),
            P("section", "dp", None),
            P("section", "dp", None),
            P("section", None, "dp"),
            P("section", None, "dp"),
        ),
        check_vma=False,
    )
```

profile of v0, /device:TPU:0, one launch (start us, length us, event | category | flops | bytes accessed | tf_op | source)
XLA Modules:
  0.0 1604.6 jit_solution(12289562402650910641)
XLA Ops:
  16.3 23.8 %all_gather.21 = bf16[1,2,512]{1,0,2:T(2,128)(2,1)S(1)} all-gather(bf16[1,2,32]{1,0,2:T(2,128)(2,1)S(1)} %copy.546), channel_id=1, replica_groups=mesh['section'=2,'dp'=16] {'dp'}, dimensions={2}, use_global_device_ids=true | all-gather | bytes 2176 | tf_op jit(solution)/shard_map/all_gather | solution.py:262
  40.2 18.4 %all_gather.25 = bf16[1,2,512]{1,0,2:T(2,128)(2,1)S(1)} all-gather(bf16[1,2,32]{1,0,2:T(2,128)(2,1)S(1)} %copy.548), channel_id=1, replica_groups=mesh['section'=2,'dp'=16] {'dp'}, dimensions={2}, use_global_device_ids=true | all-gather | bytes 2176 | tf_op jit(solution)/shard_map/all_gather | solution.py:263
  58.8 21.7 %all_gather.23 = bf16[1,512,512]{2,1,0:T(8,128)(2,1)} all-gather(bf16[1,32,512]{2,1,0:T(8,128)(2,1)S(1)} %convert_element_type.653), channel_id=1, replica_groups=mesh['section'=2,'dp'=16] {'dp'}, dimensions={1}, use_global_device_ids=true | all-gather | bytes 557056 | tf_op jit(solution)/shard_map/all_gather | solution.py:258
  94.1 43.1 %all-gather.9.cloned.1.call-done = bf16[1,512,2048]{2,1,0:T(8,128)(2,1)} async-done(((bf16[1,32,2048]{2,1,0:T(8,128)(2,1)}), bf16[1,512,2048]{2,1,0:T(8,128)(2,1)}) %all-gather.9.cloned.1.call-update) | async-done | bytes 2097168 | tf_op jit(solution)/shard_map/all_gather | solution.py:260
  137.1 42.8 %all-gather.11.cloned.1.call-done = bf16[1,2048,512]{2,1,0:T(8,128)(2,1)} async-done(((bf16[1,128,512]{2,1,0:T(8,128)(2,1)}), bf16[1,2048,512]{2,1,0:T(8,128)(2,1)}) %all-gather.11.cloned.1.call-update) | async-done | bytes 2097168 | tf_op jit(solution)/shard_map/all_gather | solution.py:261
  179.9 78.2 %conditional.5 = (f32[1024,512]{0,1:T(8,128)}, bf16[1024,512]{0,1:T(8,128)(2,1)}, bf16[1,1024,3,8,64]{1,4,3,2,0:T(8,128)(2,1)S(1)}, f32[1,8,1024]{2,1,0:T(8,128)...) conditional(s32[]{:T(128)} %convert_element_type.648, ...), branch_computations={%region_0.1_spmd, %region_1.10_spmd.clone} | conditional | flops 9246609408 | bytes 248949168 | solution.py:281
  348.3 16.2 %conditional.7 = (f32[1,1024,512]{2,1,0:T(8,128)}, f32[2,512]{1,0:T(2,128)S(1)}, f32[2,512]{1,0:T(2,128)S(1)}, f32[512,1536]{1,0:T(8,128)}, f32[512,512]{1,0:T(8...) conditional(s32[]{:T(128)} %clamp.10, () %tuple.204, ...), branch_computations={%region_28.29_spmd, %region_29.44_spmd, %region_44.59_spmd} | conditional | flops 19260542976 | bytes 750103168 | solution.py:309
  368.8 213.8 %collective-permute-done.2 = bf16[1,1024,512]{2,1,0:T(8,128)(2,1)} collective-permute-done((bf16[1,1024,512]{2,1,0:T(8,128)(2,1)}, bf16[1,1024,512]{2,1,0:T(8,128)(2,1)}, u32[]{:S(2)}, u32[]{:S(2)}) %collective-permute-start.2) | collective-permute-done | bytes 1048608 | tf_op jit(solution)/shard_map/ppermute | solution.py:18
  586.2 26.3 %conditional.6 = (f32[1024,512]{0,1:T(8,128)S(1)}, bf16[1024,512]{0,1:T(8,128)(2,1)}, bf16[1,1024,3,8,64]{1,4,3,2,0:T(8,128)(2,1)}, f32[1,8,1024]{2,1,0:T(8,128)...) conditional(s32[]{:T(128)} %convert_element_type.676, ...), branch_computations={%region_18.19_spmd, %region_19.28_spmd} | conditional | flops 9243463680 | bytes 198617360 | solution.py:281
  613.5 231.1 %conditional.8 = (f32[1,1024,512]{2,1,0:T(8,128)}, f32[2,512]{1,0:T(2,128)S(1)}, f32[2,512]{1,0:T(2,128)S(1)}, f32[512,1536]{1,0:T(8,128)}, f32[512,512]{1,0:T(8...) conditional(s32[]{:T(128)} %clamp.9, () %tuple.203, ...), branch_computations={%region_59.60_spmd, %region_60.75_spmd, %region_75.90_spmd} | conditional | flops 19260542976 | bytes 699771456 | solution.py:309
  725.1 14.5 fusion.337
  765.3 22.7 %fusion.346 = bf16[1,512,1,8,64]{1,4,3,2,0:T(8,128)(2,1)} fusion(f32[8,512,1024]{2,1,0:T(8,128)} %copy-done.63, f32[8,512,1024]{2,1,0:T(8,128)} %fusion.352, bf16[1,1024,3,8,64]{1,4,3,2,0:T(8,128)(2,1)} %get-tuple-element.739), kind=kOutput, calls=%fused_computation.421 | convolution fusion | flops 558109696 | bytes 68681728 | tf_op jit(solution)/shard_map/cond/branch_1_fun/shqk,skhd->sqhd/dot_general | solution.py:108
  788.0 23.2 %fusion.328 = bf16[1,1024,1,8,64]{1,4,3,2,0:T(8,128)(2,1)} fusion(f32[8,512,1024]{2,1,0:T(8,128)} %copy-done.63, f32[8,512,1024]{2,1,0:T(8,128)} %fusion.352, f32[1,512,8,64]{1,3,2,0:T(8,128)} %fusion.337, bf16[1,1024,8,64]{1,3,2,0:T(8,128)(2,1)} %copy-done.136), kind=kOutput, calls=%fused_computation.412 | convolution fusion | flops 558896128 | bytes 69730304 | tf_op jit(solution)/shard_map/cond/branch_1_fun/shqk,sqhd->skhd/dot_general | solution.py:113
  848.7 67.4 %collective-permute-done.3 = bf16[1,1024,512]{2,1,0:T(8,128)(2,1)} collective-permute-done((bf16[1,1024,512]{2,1,0:T(8,128)(2,1)}, bf16[1,1024,512]{2,1,0:T(8,128)(2,1)}, u32[]{:S(2)}, u32[]{:S(2)}) %collective-permute-start.3) | collective-permute-done | bytes 1048608 | tf_op jit(solution)/shard_map/ppermute | solution.py:18
  919.3 218.2 %conditional.9 = (f32[2,512]{1,0:T(2,128)S(1)}, f32[2,512]{1,0:T(2,128)S(1)}, f32[1,1024,512]{1,2,0:T(8,128)}, f32[512,1536]{1,0:T(8,128)}, f32[512,512]{1,0:T(8...) conditional(s32[]{:T(128)} %clamp.11, () %tuple.209, ...), branch_computations={%region_90.91_spmd, %region_91.106_spmd, %region_106.121_spmd} | conditional | flops 19260542976 | bytes 762686016 | solution.py:309
  1018.4 14.5 fusion.569
  1057.4 25.3 %fusion.578 = bf16[1,512,1,8,64]{1,4,3,2,0:T(8,128)(2,1)} fusion(f32[8,512,1024]{2,1,0:T(8,128)} %copy-done.65, f32[8,512,1024]{2,1,0:T(8,128)} %fusion.584, bf16[1,1024,3,8,64]{1,4,3,2,0:T(8,128)(2,1)S(1)} %copy-done.4), kind=kOutput, calls=%fused_computation.689 | convolution fusion | flops 558109696 | bytes 68681728 | tf_op jit(solution)/shard_map/cond/branch_1_fun/shqk,skhd->sqhd/dot_general | solution.py:108
  1082.7 22.6 %fusion.560 = bf16[1,1024,1,8,64]{1,4,3,2,0:T(8,128)(2,1)S(1)} fusion(f32[8,512,1024]{2,1,0:T(8,128)} %copy-done.65, f32[8,512,1024]{2,1,0:T(8,128)} %fusion.584, f32[1,512,8,64]{1,3,2,0:T(8,128)} %fusion.569, bf16[1,1024,8,64]{1,3,2,0:T(8,128)(2,1)} %copy-done.140), kind=kOutput, calls=%fused_computation.680 | convolution fusion | flops 558896128 | bytes 69730304 | tf_op jit(solution)/shard_map/cond/branch_1_fun/shqk,sqhd->skhd/dot_general | solution.py:113
  1194.5 55.6 %reduce-scatter.24.cloned.1.call-done = f32[32,2]{1,0:T(8,128)} async-done(((f32[512,2]{1,0:T(8,128)}), f32[32,2]{1,0:T(8,128)}) %reduce-scatter.24.cloned.1.call-update) | async-done | bytes 272
  1251.5 59.3 %reduce-scatter.14.cloned.1.call-done = f32[1,32,512]{2,1,0:T(8,128)} async-done(((f32[1,512,512]{2,1,0:T(8,128)}), f32[1,32,512]{2,1,0:T(8,128)}) %reduce-scatter.14.cloned.1.call-update) | async-done | bytes 65552 | tf_op jit(solution)/shard_map/reduce_scatter | solution.py:314
  1310.8 65.4 %reduce-scatter.16.cloned.1.call-done = f32[1,2,32,512]{3,2,1,0:T(8,128)} async-done(((f32[1,2,512,512]{3,2,1,0:T(8,128)}), f32[1,2,32,512]{3,2,1,0:T(8,128)}) %reduce-scatter.16.cloned.1.call-update) | async-done | bytes 131088 | tf_op jit(solution)/shard_map/reduce_scatter | solution.py:315
  1376.2 69.6 %reduce-scatter.12.cloned.1.call-done = f32[1,32,1536]{2,1,0:T(8,128)} async-done(((f32[1,512,1536]{2,1,0:T(8,128)}), f32[1,32,1536]{2,1,0:T(8,128)}) %reduce-scatter.12.cloned.1.call-update) | async-done | bytes 196624 | tf_op jit(solution)/shard_map/reduce_scatter | solution.py:313
  1445.8 75.6 %reduce-scatter.18.cloned.1.call-done = f32[1,32,2048]{2,1,0:T(8,128)} async-done(((f32[1,512,2048]{2,1,0:T(8,128)}), f32[1,32,2048]{2,1,0:T(8,128)}) %reduce-scatter.18.cloned.1.call-update) | async-done | bytes 262160 | tf_op jit(solution)/shard_map/reduce_scatter | solution.py:316
  1521.4 76.5 %reduce-scatter.20.cloned.1.call-done = f32[1,128,512]{2,1,0:T(8,128)} async-done(((f32[1,2048,512]{2,1,0:T(8,128)}), f32[1,128,512]{2,1,0:T(8,128)}) %reduce-scatter.20.cloned.1.call-update) | async-done | bytes 262160 | tf_op jit(solution)/shard_map/reduce_scatter | solution.py:317
  (485 shorter events, 594.6 us)
Async XLA Ops:
  7.2 73.3 %all-gather.7.cloned.1.call-start = ((), (), s32[]{:S(2)}) async-start(), calls=%async_computation.8 | async-start | bytes 1114112 | tf_op jit(solution)/shard_map/all_gather | solution.py:259
  8.8 85.3 %all-gather.5.cloned.1.call-start = ((), (), s32[]{:S(2)}) async-start(), calls=%async_computation.7 | async-start | bytes 1671168 | tf_op jit(solution)/shard_map/all_gather | solution.py:257
  10.4 126.7 %all-gather.9.cloned.1.call-start = ((), (), s32[]{:S(2)}) async-start(), calls=%async_computation.9 | async-start | bytes 2228224 | tf_op jit(solution)/shard_map/all_gather | solution.py:260
  12.1 167.8 %all-gather.11.cloned.1.call-start = ((), (), s32[]{:S(2)}) async-start(), calls=%async_computation.10 | async-start | bytes 2228224 | tf_op jit(solution)/shard_map/all_gather | solution.py:261
  13.8 1179.4 %reduce-scatter.22.cloned.1.call-start = ((), (), s32[]{:S(2)}) async-start(), calls=%async_computation.16 | async-start | bytes 278528
  40.1 139.8 %copy-start.118 = (bf16[1,2,512]{1,0,2:T(2,128)(2,1)}, bf16[1,2,512]{1,0,2:T(2,128)(2,1)S(1)}, u32[]{:S(2)}) copy-start(bf16[1,2,512]{1,0,2:T(2,128)(2,1)S(1)} %all_gather.21) | copy-start | bytes 6148
  58.8 121.2 %copy-start.181 = (bf16[1,2,512]{2,1,0:T(2,128)(2,1)}, bf16[1,2,512]{2,1,0:T(2,128)(2,1)S(1)}, u32[]{:S(2)}) copy-start(bf16[1,2,512]{2,1,0:T(2,128)(2,1)S(1)} %copy.549) | copy-start | bytes 6148
  258.2 90.1 %copy-start.179 = (f32[1,8,1024]{2,1,0:T(8,128)}, f32[1,8,1024]{2,1,0:T(8,128)S(1)}, u32[]{:S(2)}) copy-start(f32[1,8,1024]{2,1,0:T(8,128)S(1)} %get-tuple-element.878) | copy-start | bytes 98308
  258.2 24.7 %collective-permute-start = (bf16[1,1024,512]{1,2,0:T(8,128)(2,1)}, bf16[1,1024,512]{1,2,0:T(8,128)(2,1)}, u32[]{:S(2)}, u32[]{:S(2)}) collective-permute-start(bf16[1,1024,512]{1,2,0:T(8,128)(2,1)} %get-tuple-element.871), channel_id=1, source_target_pairs={{0,16},{1,17},{2,18},{3,19},{4,20},{5,21},{6,22},{7,23},{8,24},{9,... | collective-permute-start | bytes 3145736 | tf_op jit(solution)/shard_map/ppermute | solution.py:18
  339.7 28.9 %collective-permute-start.1 = (bf16[1,1024,512]{1,2,0:T(8,128)(2,1)}, bf16[1,1024,512]{1,2,0:T(8,128)(2,1)}, u32[]{:S(2)}, u32[]{:S(2)}) collective-permute-start(bf16[1,1024,512]{1,2,0:T(8,128)(2,1)} %get-tuple-element.1894), channel_id=1, source_target_pairs={{0,16},{1,17},{2,18},{3,19},{4,20},{5,21},{6,22},{7,23},{8,24},{9,... | collective-permute-start | bytes 3145736 | tf_op jit(solution)/shard_map/ppermute | solution.py:18
  367.3 215.4 %collective-permute-start.2 = (bf16[1,1024,512]{2,1,0:T(8,128)(2,1)}, bf16[1,1024,512]{2,1,0:T(8,128)(2,1)}, u32[]{:S(2)}, u32[]{:S(2)}) collective-permute-start(bf16[1,1024,512]{2,1,0:T(8,128)(2,1)} %convert_element_type.684), channel_id=1, source_target_pairs={{16,0},{17,1},{18,2},{19,3},{20,4},{21,5},{22,6},{23,7},{24,8},{25... | collective-permute-start | bytes 3145736 | tf_op jit(solution)/shard_map/ppermute | solution.py:18
  368.8 217.5 %copy-start.18 = (bf16[1,2,512,512]{3,2,1,0:T(8,128)(2,1)S(1)}, bf16[1,2,512,512]{3,2,1,0:T(8,128)(2,1)}, u32[]{:S(2)}) copy-start(bf16[1,2,512,512]{3,2,1,0:T(8,128)(2,1)} %all-gather.7.cloned.1.call-done) | copy-start | bytes 3145732
  368.8 217.5 %copy-start.182 = (bf16[1,2,512]{2,1,0:T(2,128)(2,1)S(1)}, bf16[1,2,512]{2,1,0:T(2,128)(2,1)}, u32[]{:S(2)}) copy-start(bf16[1,2,512]{2,1,0:T(2,128)(2,1)} %copy-done.181) | copy-start | bytes 6148
  844.6 74.6 %copy-start.187 = (f32[2,512]{1,0:T(2,128)}, f32[2,512]{1,0:T(2,128)S(1)}, u32[]{:S(2)}) copy-start(f32[2,512]{1,0:T(2,128)S(1)} %get-tuple-element.921) | copy-start | bytes 12292
  844.7 74.6 %copy-start.188 = (f32[2,512]{1,0:T(2,128)}, f32[2,512]{1,0:T(2,128)S(1)}, u32[]{:S(2)}) copy-start(f32[2,512]{1,0:T(2,128)S(1)} %get-tuple-element.918) | copy-start | bytes 12292
  847.4 68.7 %collective-permute-start.3 = (bf16[1,1024,512]{2,1,0:T(8,128)(2,1)}, bf16[1,1024,512]{2,1,0:T(8,128)(2,1)}, u32[]{:S(2)}, u32[]{:S(2)}) collective-permute-start(bf16[1,1024,512]{2,1,0:T(8,128)(2,1)} %convert_element_type.688), channel_id=1, source_target_pairs={{16,0},{17,1},{18,2},{19,3},{20,4},{21,5},{22,6},{23,7},{24,8},{25... | collective-permute-start | bytes 3145736 | tf_op jit(solution)/shard_map/ppermute | solution.py:18
  919.3 218.2 %copy-start.186 = (f32[2,512]{1,0:T(2,128)S(1)}, f32[2,512]{1,0:T(2,128)}, u32[]{:S(2)}) copy-start(f32[2,512]{1,0:T(2,128)} %copy-done.185) | copy-start | bytes 12292
  919.3 219.8 %copy-start.184 = (f32[2,512]{1,0:T(2,128)S(1)}, f32[2,512]{1,0:T(2,128)}, u32[]{:S(2)}) copy-start(f32[2,512]{1,0:T(2,128)} %copy-done.183) | copy-start | bytes 12292
  1139.1 111.1 %reduce-scatter.24.cloned.1.call-start = ((), (), s32[]{:S(2)}) async-start(), calls=%async_computation.17 | async-start | bytes 278528
  1140.7 170.1 %reduce-scatter.14.cloned.1.call-start = ((), (), s32[]{:S(2)}) async-start(), calls=%async_computation.12 | async-start | bytes 1114112 | tf_op jit(solution)/shard_map/reduce_scatter | solution.py:314
  1144.0 232.2 %reduce-scatter.16.cloned.1.call-start = ((), (), s32[]{:S(2)}) async-start(), calls=%async_computation.13 | async-start | bytes 2228224 | tf_op jit(solution)/shard_map/reduce_scatter | solution.py:315
  1149.1 296.7 %reduce-scatter.12.cloned.1.call-start = ((), (), s32[]{:S(2)}) async-start(), calls=%async_computation.11 | async-start | bytes 3342336 | tf_op jit(solution)/shard_map/reduce_scatter | solution.py:313
  1155.6 365.8 %reduce-scatter.18.cloned.1.call-start = ((), (), s32[]{:S(2)}) async-start(), calls=%async_computation.14 | async-start | bytes 4456448 | tf_op jit(solution)/shard_map/reduce_scatter | solution.py:316
  1164.0 433.9 %reduce-scatter.20.cloned.1.call-start = ((), (), s32[]{:S(2)}) async-start(), calls=%async_computation.15 | async-start | bytes 4456448 | tf_op jit(solution)/shard_map/reduce_scatter | solution.py:317
  (98 other events, 674.9 us)
Sparse Core Ops, SparseCore 0:
  10.8 41.1 all-gather.6
  54.8 39.2 all-gather.4
  96.8 40.2 all-gather.8
  139.7 40.1 all-gather.10
  1139.2 53.1 reduce-scatter.21
  1195.8 54.3 reduce-scatter.23
  1254.4 56.3 reduce-scatter.13
  1315.6 60.6 reduce-scatter.15
  1380.6 65.1 reduce-scatter.11
  1450.1 71.2 reduce-scatter.17
  1526.3 71.5 reduce-scatter.19
where the time goes:
time: 1620 us; the launch traced here: 1600 us
  waiting for transfers between devices  789 us (49%)
  matrix products  373 us (23%)
  local copies, waits for them, and re-layouts  160 us (10%)
  other arithmetic  153 us (9%)
  blocking collectives  63.8 us (4%)
  loops' own time  39.8 us (2%)
    ppermute x4, waiting for transfers between devices, shifted(): lax.ppermute(value, axis, [(source, source + steps) for source in range(l...  288 us
    reduce_scatter x1, waiting for transfers between devices, per_device(): lax.psum_scatter(grads[4], 'dp', scatter_dimension=1, tiled=True)  76.5 us
    dot_general x4, matrix products, attend_backward(): jnp.einsum('shqk,skhd->sqhd', score_low, keyed[:, :finish], preferred_ele...  76.3 us
    reduce_scatter x1, waiting for transfers between devices, per_device(): lax.psum_scatter(grads[3], 'dp', scatter_dimension=1, tiled=True)  75.6 us
    dot_general x4, matrix products, attend_backward(): jnp.einsum('shqk,sqhd->skhd', score_low, query[:, start:finish], preferre...  74.8 us
    reduce_scatter x1, waiting for transfers between devices, per_device(): lax.psum_scatter(grads[0], 'dp', scatter_dimension=1, tiled=True)  69.6 us
    reduce_scatter x1, waiting for transfers between devices, per_device(): lax.psum_scatter(grads[2], 'dp', scatter_dimension=2, tiled=True)  65.4 us
    another operation x33, local copies, waits for them, and re-layouts  62.1 us
  transfers between devices with their start and end apart: 15, of which 12 were waited for; matrix products, arithmetic and copies ran while one was open for 6% of the time, Pallas kernels for 0%

commit v1 on v0

v1 whole, which is shorter than its diff:
```python
import functools

import jax
import jax.numpy as jnp
from jax import lax
from jax.experimental import pallas as pl
from jax.experimental.pallas import tpu as pltpu
from jax.sharding import PartitionSpec as P

HD = 64
ROWS = 256
bf16 = jnp.bfloat16
f32 = jnp.float32
root_term = 0.7978845608
cube_term = 0.044715
VMEM = 56 * 1024 * 1024
PARTS = 16
UNIT = 32
FIRST = 3 * UNIT + 16
REST = 11 * UNIT


def dense(left, right):
    return jnp.dot(left, right, preferred_element_type=f32)


def cross(left, right):
    return lax.dot_general(left, right, (((0,), (0,)), ((), ())), preferred_element_type=f32)


def against(left, right):
    return lax.dot_general(left, right, (((1,), (1,)), ((), ())), preferred_element_type=f32)


def normalise(values):
    centred = values - jnp.mean(values, axis=-1, keepdims=True)
    spread = jnp.mean(centred * centred, axis=-1, keepdims=True)
    scale = lax.rsqrt(spread + 1e-05)
    return centred * scale, scale


def norm_back(grad, hat, scale, gain):
    spread = grad * gain
    first = jnp.mean(spread, axis=-1, keepdims=True)
    second = jnp.mean(spread * hat, axis=-1, keepdims=True)
    return scale * (spread - first - hat * second)


def struct(shape, dtype):
    return jax.ShapeDtypeStruct(shape, dtype)


def rows_of(width):
    return pl.BlockSpec((ROWS, width), lambda i, place: (i, 0))


def whole(*shape):
    return pl.BlockSpec(shape, lambda i, place: (0,) * len(shape))


def call(kernel, grid, in_specs, out_specs, out_shape, scratch=(), flops=0, moved=0):
    return pl.pallas_call(
        kernel,
        grid_spec=pltpu.PrefetchScalarGridSpec(
            num_scalar_prefetch=1, grid=grid, in_specs=in_specs, out_specs=out_specs, scratch_shapes=list(scratch)
        ),
        out_shape=out_shape,
        compiler_params=pltpu.CompilerParams(dimension_semantics=("arbitrary",), vmem_limit_bytes=VMEM),
        cost_estimate=pl.CostEstimate(flops=flops, bytes_accessed=moved, transcendentals=0),
    )


def fetches(place, sources, target, sems, cuts):
    copies = []
    for number, (start, stop) in enumerate(cuts):
        group = []
        for index, source in enumerate(sources):
            for slot in range(4):
                part = ((place[0] - slot) & 3) * 4 + (place[1] ^ (index & 1)) * 2 + (place[2] ^ (index >> 1))
                group.append(
                    pltpu.make_async_copy(
                        source.at[slot, pl.ds(start, stop - start)],
                        target.at[part, pl.ds(start, stop - start)],
                        sems.at[number],
                    )
                )
        copies.append(group)
    return copies


def unit(ref, at):
    return ref[:, at * UNIT : (at + 1) * UNIT, :].reshape(PARTS * UNIT, ref.shape[2])


def down_part(ref, at):
    return ref[at * 4 : at * 4 + 4, 7 * UNIT : 11 * UNIT, :].reshape(16 * UNIT, ref.shape[2])


ANY4 = [pl.BlockSpec(memory_space=pl.ANY)] * 4
REST_CUTS = ((0, 3 * UNIT), (3 * UNIT, 7 * UNIT), (7 * UNIT, 11 * UNIT))


def qkv_kernel(place, x_ref, w0, w1, w2, w3, n_ref, q_ref, k_ref, v_ref, vec_ref, buf, sems):
    copies = fetches(place, (w0, w1, w2, w3), buf, sems, ((0, FIRST),))[0]

    @pl.when(pl.program_id(0) == 0)
    def _():
        for copy in copies:
            copy.start()
        for copy in copies:
            copy.wait()
        vec_ref[...] = jnp.sum(buf[:, 3 * UNIT : 3 * UNIT + 16, :].astype(f32), axis=0)

    hat, _ = normalise(x_ref[...].astype(f32))
    n1 = (hat * vec_ref[0:1, :]).astype(bf16)
    n_ref[...] = n1
    q_ref[...] = (dense(n1, unit(buf, 0)).astype(bf16) * 0.125).astype(bf16)
    k_ref[...] = dense(n1, unit(buf, 1)).astype(bf16)
    v_ref[...] = dense(n1, unit(buf, 2)).astype(bf16)


def qkv_forward(place, x, weights):
    length, width = x.shape
    row = rows_of(width)
    return call(
        qkv_kernel,
        (length // ROWS,),
        [row] + ANY4,
        [row] * 4 + [whole(16, width)],
        [struct((length, width), bf16)] * 4 + [struct((16, width), f32)],
        [pltpu.VMEM((PARTS, FIRST, width), bf16), pltpu.SemaphoreType.DMA((1,))],
        flops=2 * length * width * 3 * width,
        moved=8_000_000,
    )(place, x, *weights)


def attend_kernel(block, place, q_ref, k_ref, v_ref, o_ref, s_ref):
    length = q_ref.shape[0]
    lane = lax.broadcasted_iota(jnp.int32, (block, 128), 1)
    row = lax.broadcasted_iota(jnp.int32, (block, block), 0)
    col = lax.broadcasted_iota(jnp.int32, (block, block), 1)
    for index in range(length // block):
        start, stop = index * block, (index + 1) * block
        q = q_ref[start:stop, :]
        outs, logs = [], []
        for head in range(2):
            mine = (lane >= head * HD) & (lane < (head + 1) * HD)
            own = jnp.where(mine, q, jnp.zeros_like(q))
            scores = against(own, k_ref[:stop, :])
            last = jnp.where(row >= col, scores[:, start:], -1e30)
            scores = jnp.concatenate([scores[:, :start], last], axis=1) if start else last
            highest = jnp.max(scores, axis=1, keepdims=True)
            weights = jnp.exp(scores - highest)
            total = jnp.sum(weights, axis=1, keepdims=True)
            outs.append(dense(weights.astype(bf16), v_ref[:stop, :]) * (1.0 / total))
            logs.append(highest + jnp.log(total))
        o_ref[start:stop, :] = jnp.where(lane < HD, outs[0], outs[1]).astype(bf16)
        s_ref[start:stop, :] = jnp.where(lane < HD, logs[0], logs[1])


def attend_forward(place, q, k, v, block=256):
    length, width = q.shape
    pair = pl.BlockSpec((length, 128), lambda i, place: (0, i))
    return call(
        functools.partial(attend_kernel, block),
        (width // 128,),
        [pair] * 3,
        [pair, pair],
        [struct((length, width), bf16), struct((length, width), f32)],
        flops=12_000_000_000,
        moved=6_000_000,
    )(place, q, k, v)


def feed_kernel(place, x_ref, n1_ref, o_ref, vec_ref, w0, w1, w2, w3,
                y_ref, n2_ref, scale_ref, ga_ref, ta_ref, h_ref, slope_ref, gf_ref, tf_ref, buf, sems):
    copies = fetches(place, (w0, w1, w2, w3), buf, sems, REST_CUTS)
    at_first = pl.program_id(0) == 0

    @pl.when(at_first)
    def _():
        for group in copies:
            for copy in group:
                copy.start()
        for group in copies:
            for copy in group:
                copy.wait()

    branch = dense(o_ref[...], unit(buf, 0))
    opening = jax.nn.sigmoid(dense(n1_ref[...], unit(buf, 1)) + vec_ref[2:3, :])
    gated = opening * branch
    middle = x_ref[...].astype(f32) + gated
    ga_ref[...] = opening.astype(bf16)
    ta_ref[...] = (gated * (1.0 - opening)).astype(bf16)
    hat, scale = normalise(middle)
    n2 = (hat * vec_ref[1:2, :]).astype(bf16)
    n2_ref[...] = n2
    scale_ref[...] = scale
    feed = None
    for at in range(4):
        cut = slice(at * 512, at * 512 + 512)
        u = dense(n2, unit(buf, 3 + at))
        square = u * u
        inner = jnp.tanh(u * (root_term + (root_term * cube_term) * square))
        half = 0.5 + 0.5 * inner
        active = (u * half).astype(bf16)
        h_ref[:, cut] = active
        slope = half + u * (0.5 - 0.5 * inner * inner) * (root_term + (3.0 * root_term * cube_term) * square)
        slope_ref[:, cut] = slope.astype(bf16)
        part = dense(active, down_part(buf, at))
        feed = part if feed is None else feed + part
    closing = jax.nn.sigmoid(dense(n2, unit(buf, 2)) + vec_ref[3:4, :])
    gated = closing * feed
    gf_ref[...] = closing.astype(bf16)
    tf_ref[...] = (gated * (1.0 - closing)).astype(bf16)
    y_ref[...] = (middle + gated).astype(bf16)


def feed_forward(place, x, n1, o, vec, weights):
    length, width = x.shape
    wide = 4 * width
    row, half = rows_of(width), struct((length, width), bf16)
    big, bigs = rows_of(wide), struct((length, wide), bf16)
    return call(
        feed_kernel,
        (length // ROWS,),
        [row, row, row, whole(16, width)] + ANY4,
        [row, row, rows_of(1), row, row, big, big, row, row],
        [half, half, struct((length, 1), f32), half, half, bigs, bigs, half, half],
        [pltpu.VMEM((PARTS, REST, width), bf16), pltpu.SemaphoreType.DMA((3,))],
        flops=2 * length * width * (3 * width + 2 * wide),
        moved=24_000_000,
    )(place, x, n1, o, vec, *weights)


def feed_back_kernel(extra, place, *refs):
    at = 1 + extra
    e_refs = refs[:at]
    n2_ref, scale_ref, ga_ref, ta_ref, slope_ref, gf_ref, tf_ref, vec_ref, w0, w1, w2, w3 = refs[at : at + 12]
    dm_ref, df_ref, dzf_ref, du_ref, da_ref, dza_ref, do_ref, small_ref, buf, sems = refs[at + 12 :]
    copies = fetches(place, (w0, w1, w2, w3), buf, sems, REST_CUTS)
    at_first = pl.program_id(0) == 0

    @pl.when(at_first)
    def _():
        for group in copies:
            for copy in group:
                copy.start()
        for group in copies:
            for copy in group:
                copy.wait()

    e = e_refs[0][...].astype(f32)
    for ref in e_refs[1:]:
        e = e + ref[...].astype(f32)
    df = (e * gf_ref[...].astype(f32)).astype(bf16)
    dzf = (e * tf_ref[...].astype(f32)).astype(bf16)
    df_ref[...] = df
    dzf_ref[...] = dzf
    dn2 = against(dzf, unit(buf, 2))
    for at in range(4):
        cut = slice(at * 512, at * 512 + 512)
        dh = against(df, down_part(buf, at))
        du = (dh * slope_ref[:, cut].astype(f32)).astype(bf16)
        du_ref[:, cut] = du
        dn2 = dn2 + against(du, unit(buf, 3 + at))
    gain = vec_ref[1:2, :]
    hat = n2_ref[...].astype(f32) * (1.0 / gain)
    dm = e + norm_back(dn2, hat, scale_ref[...], gain)
    dm_ref[...] = dm
    da = (dm * ga_ref[...].astype(f32)).astype(bf16)
    dza = (dm * ta_ref[...].astype(f32)).astype(bf16)
    da_ref[...] = da
    dza_ref[...] = dza
    do_ref[...] = against(da, unit(buf, 0)).astype(bf16)
    sums = jnp.concatenate(
        [jnp.sum(part, axis=0, keepdims=True) for part in (dn2 * hat, dza.astype(f32), dzf.astype(f32))]
        + [jnp.zeros((5, e.shape[1]), f32)],
        axis=0,
    )

    @pl.when(at_first)
    def _():
        small_ref[...] = sums

    @pl.when(pl.program_id(0) > 0)
    def _():
        small_ref[...] += sums


def feed_back(place, es, n2, scale, ga, ta, slope, gf, tf, vec, weights):
    length, width = n2.shape
    wide = 4 * width
    row, half = rows_of(width), struct((length, width), bf16)
    big, bigs = rows_of(wide), struct((length, wide), bf16)
    return call(
        functools.partial(feed_back_kernel, len(es) - 1),
        (length // ROWS,),
        [row] * len(es) + [row, rows_of(1), row, row, big, row, row, whole(16, width)] + ANY4,
        [row, row, row, big, row, row, row, whole(8, width)],
        [struct((length, width), f32), half, half, bigs, half, half, half, struct((8, width), f32)],
        [pltpu.VMEM((PARTS, REST, width), bf16), pltpu.SemaphoreType.DMA((3,))],
        flops=2 * length * width * (2 * width + 2 * wide),
        moved=24_000_000,
    )(place, *es, n2, scale, ga, ta, slope, gf, tf, vec, *weights)


def split3(value):
    first = value.astype(bf16)
    rest = value - first.astype(f32)
    second = rest.astype(bf16)
    third = (rest - second.astype(f32)).astype(bf16)
    return first, second, third


def attend_back_kernel(block, place, q_ref, k_ref, v_ref, o_ref, s_ref, do_ref, dq_ref, dk_ref, dv_ref,
                       q_s, k_s, v_s, do_s, acc):
    length = q_ref.shape[0]
    lane = lax.broadcasted_iota(jnp.int32, (length, 128), 1)
    row = lax.broadcasted_iota(jnp.int32, (block, block), 0)
    col = lax.broadcasted_iota(jnp.int32, (block, block), 1)
    q, k, v, do = q_ref[...], k_ref[...], v_ref[...], do_ref[...]
    zero = jnp.zeros_like(q)
    product = do.astype(f32) * o_ref[...].astype(f32)
    for head in range(2):
        low = head * HD
        other = (1 - head) * HD
        mine = (lane >= low) & (lane < low + HD)
        logs = -s_ref[:, low : low + 1]
        delta = -jnp.sum(jnp.where(mine, product, 0.0), axis=1, keepdims=True)
        one = jnp.where((lane >= other) & (lane < other + 3), jnp.ones_like(q), zero)
        q_aug, do_aug = jnp.where(mine, q, zero), jnp.where(mine, do, zero)
        for at, (part, piece) in enumerate(zip(split3(logs), split3(delta))):
            here = lane == other + at
            q_aug = jnp.where(here, part, q_aug)
            do_aug = jnp.where(here, piece, do_aug)
        q_s[head] = q_aug
        do_s[head] = do_aug
        k_s[head] = jnp.where(mine, k, one)
        v_s[head] = jnp.where(mine, v, one)
    for index in range(length // block):
        start, stop = index * block, (index + 1) * block
        kgrads, vgrads = [], []
        for head in range(2):
            kb, vb = k_s[head, start:stop, :], v_s[head, start:stop, :]
            scores = against(kb, q_s[head, start:, :])
            first = jnp.where(row <= col, scores[:, :block], -1e30)
            scores = jnp.concatenate([first, scores[:, block:]], axis=1) if stop < length else first
            probs = jnp.exp(scores)
            grads = (probs * against(vb, do_s[head, start:, :])).astype(bf16)
            vgrads.append(dense(probs.astype(bf16), do_ref[start:, :]))
            kgrads.append(dense(grads, q_ref[start:, :]))
            part = cross(grads, kb)
            if index == 0:
                acc[head] = part
            else:
                acc[head, start:, :] += part
        half = lane[:block] < HD
        dk_ref[start:stop, :] = jnp.where(half, kgrads[0], kgrads[1]).astype(bf16)
        dv_ref[start:stop, :] = jnp.where(half, vgrads[0], vgrads[1]).astype(bf16)
    dq_ref[...] = (jnp.where(lane < HD, acc[0], acc[1]) * 0.125).astype(bf16)


def attend_back(place, q, k, v, o, s, do, block=256):
    length, width = q.shape
    pair = pl.BlockSpec((length, 128), lambda i, place: (0, i))
    return call(
        functools.partial(attend_back_kernel, block),
        (width // 128,),
        [pair] * 6,
        [pair] * 3,
        [struct((length, width), bf16)] * 3,
        [pltpu.VMEM((2, length, 128), bf16)] * 4 + [pltpu.VMEM((2, length, 128), f32)],
        flops=20_000_000_000,
        moved=10_000_000,
    )(place, q, k, v, o, s, do)


def qkv_back_kernel(place, x_ref, dm_ref, dq_ref, dk_ref, dv_ref, dza_ref, vec_ref, w0, w1, w2, w3, r0, r1, r2, r3,
                    dx_ref, low_ref, small_ref, buf, gate, sems):
    copies = fetches(place, (w0, w1, w2, w3), buf, sems, ((0, 3 * UNIT),))[0]
    for index, source in enumerate((r0, r1, r2, r3)):
        for slot in range(4):
            part = ((place[0] - slot) & 3) * 4 + (place[1] ^ (index & 1)) * 2 + (place[2] ^ (index >> 1))
            copies.append(pltpu.make_async_copy(source.at[slot, pl.ds(UNIT, UNIT)], gate.at[part], sems.at[1]))
    at_first = pl.program_id(0) == 0

    @pl.when(at_first)
    def _():
        for copy in copies:
            copy.start()
        for copy in copies:
            copy.wait()

    dn = against(dza_ref[...], gate[...].reshape(PARTS * UNIT, gate.shape[2]))
    for at, ref in enumerate((dq_ref, dk_ref, dv_ref)):
        dn = dn + against(ref[...], unit(buf, at))
    hat, scale = normalise(x_ref[...].astype(f32))
    dx = dm_ref[...] + norm_back(dn, hat, scale, vec_ref[0:1, :])
    dx_ref[...] = dx
    low_ref[...] = dx.astype(bf16)
    sums = jnp.concatenate([jnp.sum(dn * hat, axis=0, keepdims=True), jnp.zeros((7, dx.shape[1]), f32)], axis=0)

    @pl.when(at_first)
    def _():
        small_ref[...] = sums

    @pl.when(pl.program_id(0) > 0)
    def _():
        small_ref[...] += sums


def qkv_back(place, x, dm, dq, dk, dv, dza, vec, weights, rest):
    length, width = x.shape
    row = rows_of(width)
    return call(
        qkv_back_kernel,
        (length // ROWS,),
        [row] * 6 + [whole(16, width)] + ANY4 + ANY4,
        [row, row, whole(8, width)],
        [struct((length, width), f32), struct((length, width), bf16), struct((8, width), f32)],
        [pltpu.VMEM((PARTS, 3 * UNIT, width), bf16), pltpu.VMEM((PARTS, UNIT, width), bf16), pltpu.SemaphoreType.DMA((2,))],
        flops=2 * length * width * 4 * width,
        moved=12_000_000,
    )(place, x, dm, dq, dk, dv, dza, vec, *weights, *rest)


def put(place, keep, send, values, rows, first):
    for y in range(2):
        low, high = (values[(y * 2 + c) * rows : (y * 2 + c + 1) * rows] for c in range(2))
        at = place[1] ^ y
        swap = place[2] == 1
        keep[at, 0, first : first + rows, :] = jnp.where(swap, high, low)
        send[at, 0, first : first + rows, :] = jnp.where(swap, low, high)


def rest_grad_kernel(place, o_ref, n1_ref, n2_ref, h_ref, da_ref, dza_ref, dzf_ref, du_ref, df_ref, keep, send):
    put(place, keep, send, cross(o_ref[...], da_ref[...]).astype(bf16), UNIT, 0)
    put(place, keep, send, cross(n1_ref[...], dza_ref[...]).astype(bf16), UNIT, UNIT)
    put(place, keep, send, cross(n2_ref[...], dzf_ref[...]).astype(bf16), UNIT, 2 * UNIT)
    up = cross(n2_ref[...], du_ref[...]).astype(bf16)
    for at in range(4):
        put(place, keep, send, up[:, at * 512 : at * 512 + 512], UNIT, (3 + at) * UNIT)
    put(place, keep, send, cross(h_ref[...], df_ref[...]).astype(bf16), 4 * UNIT, 7 * UNIT)


def rest_grad(place, o, n1, n2, h, da, dza, dzf, du, df):
    length, width = o.shape
    wide = h.shape[1]
    cols = pl.BlockSpec((length, width // 4), lambda i, place: (0, i))
    wides = pl.BlockSpec((length, wide // 4), lambda i, place: (0, i))
    out = pl.BlockSpec((2, 1, REST, width), lambda i, place: (0, (i - place[0]) & 3, 0, 0))
    return call(
        rest_grad_kernel,
        (4,),
        [cols] * 3 + [wides] + [whole(length, width)] * 3 + [whole(length, wide), whole(length, width)],
        [out, out],
        [struct((2, 4, REST, width), bf16)] * 2,
        flops=2 * length * width * (3 * width + 2 * wide),
        moved=26_000_000,
    )(place, o, n1, n2, h, da, dza, dzf, du, df)


def first_grad_kernel(place, n1_ref, dq_ref, dk_ref, dv_ref, s1_ref, s2_ref, keep, send):
    for at, ref in enumerate((dq_ref, dk_ref, dv_ref)):
        put(place, keep, send, cross(n1_ref[...], ref[...]).astype(bf16), UNIT, at * UNIT)
    small = jnp.concatenate([s1_ref[0:1, :], s2_ref[0:3, :], jnp.zeros((12, n1_ref.shape[1] * 4), f32)], axis=0).astype(bf16)
    for y in range(2):
        keep[y, 0, 3 * UNIT :, :] = small
        send[y, 0, 3 * UNIT :, :] = small


def first_grad(place, n1, dq, dk, dv, small1, small2):
    length, width = n1.shape
    cols = pl.BlockSpec((length, width // 4), lambda i, place: (0, i))
    out = pl.BlockSpec((2, 1, FIRST, width), lambda i, place: (0, (i - place[0]) & 3, 0, 0))
    return call(
        first_grad_kernel,
        (4,),
        [cols] + [whole(length, width)] * 3 + [whole(8, width)] * 2,
        [out, out],
        [struct((2, 4, FIRST, width), bf16)] * 2,
        flops=2 * length * width * 3 * width,
        moved=9_000_000,
    )(place, n1, dq, dk, dv, small1, small2)


def moved_z(value, steps):
    count = lax.axis_size("dp")
    return lax.ppermute(value, "dp", [(d, (d + 4 * steps) % count) for d in range(count)])


def swapped(value, bit):
    return lax.ppermute(value, "dp", [(d, d ^ bit) for d in range(lax.axis_size("dp"))])


def crossed(value, sources=(0, 1)):
    return lax.ppermute(value, "section", [(s, 1 - s) for s in sources])


def spread(block):
    own = jnp.stack([block] + [moved_z(block, k) for k in (1, 2, 3)])
    beside = swapped(own, 2)
    return own, beside, swapped(own, 1), swapped(beside, 1)


def spread_whole(blocks):
    blocks = blocks.reshape(4, 2, 2, *blocks.shape[1:])
    blocks = jnp.stack([blocks[0], blocks[3], blocks[2], blocks[1]])
    return tuple(blocks[:, index & 1, index >> 1] for index in range(4))


def gather_whole(values, axis):
    values = lax.all_gather(values.astype(bf16), "dp", axis=axis, tiled=True)
    return lax.all_gather(values, "section", axis=0, tiled=True)


def split_rows(matrix, cols):
    rows, width = matrix.shape[0] // PARTS, matrix.shape[1] // cols
    return matrix.reshape(PARTS, rows, cols, width).transpose(0, 2, 1, 3).reshape(PARTS, cols * rows, width)


def merge_rows(blocks, cols):
    rows, width = blocks.shape[1] // cols, blocks.shape[2]
    return blocks.reshape(PARTS, cols, rows, width).transpose(0, 2, 1, 3).reshape(PARTS * rows, cols * width)


def weights_whole(w_qkv, w_out, w_gates, w_up, w_down, gains, biases):
    w_qkv, w_out, w_up, w_down = (gather_whole(w, 1) for w in (w_qkv, w_out, w_up, w_down))
    w_gates, gains, biases = (gather_whole(w, 2) for w in (w_gates, gains, biases))
    heads, tails = [], []
    for layer in range(2):
        lines = jnp.concatenate([gains[layer], biases[layer], jnp.zeros((12, gains.shape[2]), bf16)], axis=0)
        lines = jnp.concatenate([lines[None], jnp.zeros((PARTS - 1, *lines.shape), bf16)], axis=0)
        heads.append(spread_whole(jnp.concatenate([split_rows(w_qkv[layer], 3), lines], axis=1)))
        parts = [w_out[layer], w_gates[layer, 0], w_gates[layer, 1]]
        parts = [split_rows(part, 1) for part in parts] + [split_rows(w_up[layer], 4), split_rows(w_down[layer], 1)]
        tails.append(spread_whole(jnp.concatenate(parts, axis=1)))
    return heads, tails


def collect_whole(early, rest):
    early, rest = (jnp.stack(pair).transpose(2, 1, 0, 3, 4).reshape(PARTS, *pair[0].shape[2:]) for pair in (early, rest))
    parts = [merge_rows(early[:, : 3 * UNIT], 3)]
    parts += [merge_rows(rest[:, :UNIT], 1)]
    parts += [jnp.stack([merge_rows(rest[:, at * UNIT : (at + 1) * UNIT], 1) for at in (1, 2)])]
    parts += [merge_rows(rest[:, 3 * UNIT : 7 * UNIT], 4), merge_rows(rest[:, 7 * UNIT :], 1)]
    lines = early[0, 3 * UNIT : 3 * UNIT + 4]
    parts += [lines[0:2], lines[2:4]]
    axes = (0, 0, 1, 0, 0, 1, 1)
    parts = [lax.psum_scatter(part.astype(f32), "dp", scatter_dimension=axis, tiled=True) for part, axis in zip(parts, axes)]
    return [lax.psum(part, "section")[None] for part in parts]


def collect(keep, send):
    got = swapped(send, 1)
    away = (keep[1].astype(f32) + got[1].astype(f32)).astype(bf16)
    near = keep[0].astype(f32) + got[0].astype(f32)
    got = swapped(away, 2)
    near = near + got.astype(f32)
    total = near[0]
    for k in (1, 2, 3):
        total = total + moved_z(near[k].astype(bf16), k).astype(f32)
    return total


def packed_first(w_qkv, gains, biases, index):
    rows, width = w_qkv.shape[1], 512
    qkv = [w_qkv[0][:, at * width : (at + 1) * width] for at in range(3)]
    count = width // rows
    lines = jnp.concatenate([gains[0], biases[0]], axis=0)
    lines = jnp.where(jnp.arange(width)[None, :] // rows == index, jnp.tile(lines, (1, count)), 0.0)
    return jnp.concatenate(qkv + [lines, jnp.zeros((12, width), f32)], axis=0).astype(bf16)


def packed_rest(w_out, w_gates, w_up, w_down):
    width = w_out.shape[2]
    ups = [w_up[0][:, at * width : (at + 1) * width] for at in range(4)]
    return jnp.concatenate([w_out[0], w_gates[0, 0], w_gates[0, 1]] + ups + [w_down[0]], axis=0).astype(bf16)


def per_device(tokens, cotangent, w_qkv, w_out, w_gates, w_up, w_down, norm_gains, gate_biases):
    section = lax.axis_index("section")
    index = lax.axis_index("dp")
    count = lax.axis_size("dp")
    fast = count == PARTS
    number, length, width = tokens.shape[0], tokens.shape[2], tokens.shape[3]
    first = section == 0

    def pick(own, other):
        return jnp.where(first, own, other), jnp.where(first, other, own)

    if not fast:
        place = jnp.zeros((3,), jnp.int32)
        heads, tails = weights_whole(w_qkv, w_out, w_gates, w_up, w_down, norm_gains, gate_biases)
    else:
        place = jnp.stack([index // 4, (index // 2) & 1, index & 1]).astype(jnp.int32)
        head = packed_first(w_qkv, norm_gains, gate_biases, index)
        tail = packed_rest(w_out, w_gates, w_up, w_down)
        heads = [spread(block) for block in pick(head, crossed(head))]
        tails = [spread(block) for block in pick(tail, crossed(tail))]
    x = jnp.where(first, tokens[0, 0], tokens[1, 0])
    seeds = [cotangent[0, m, 0] for m in range(2)]
    seeds = pick(jnp.where(first, seeds[0], seeds[1]), crossed(jnp.where(first, seeds[1], seeds[0])))

    kept = []
    value = x
    for layer in range(2):
        n1, q, k, v, vec = qkv_forward(place, value, heads[layer])
        o, s = attend_forward(place, q, k, v)
        y, n2, scale, ga, ta, h, slope, gf, tf = feed_forward(place, value, n1, o, vec, tails[layer])
        kept.append((value, n1, q, k, v, vec, o, s, n2, scale, ga, ta, h, slope, gf, tf))
        value = y
    y0, y1 = kept[1][0], value
    mine, theirs = pick(y0, y1)
    theirs = crossed(theirs)
    block = jnp.stack([jnp.where(first, mine, theirs), jnp.where(first, theirs, mine)])[None, :, None]

    extra = []
    results = {}
    for layer in (1, 0):
        value, n1, q, k, v, vec, o, s, n2, scale, ga, ta, h, slope, gf, tf = kept[layer]
        dm, df, dzf, du, da, dza, do, small2 = feed_back(
            place, [seeds[layer]] + extra, n2, scale, ga, ta, slope, gf, tf, vec, tails[layer]
        )
        rest = rest_grad(place, o, n1, n2, h, da, dza, dzf, du, df)
        if fast:
            rest = collect(*rest)
        dq, dk, dv = attend_back(place, q, k, v, o, s, do)
        dx, low, small1 = qkv_back(place, value, dm, dq, dk, dv, dza, vec, heads[layer], tails[layer])
        early = first_grad(place, n1, dq, dk, dv, small1, small2)
        extra = [low]
        if fast:
            early = collect(*early)
            sums = [part + crossed(part.astype(bf16), (1 - layer,)).astype(f32) for part in (early, rest)]
        else:
            sums = collect_whole(early, rest)
        results[layer] = (dx, crossed(low, (1 - layer,)), *sums)

    dx = jnp.where(first, results[0][0], results[1][0])
    other = jnp.where(first, results[0][1], results[1][1]).astype(f32)
    in_grads = jnp.stack([jnp.where(first, dx, other), jnp.where(first, other, dx)])[None, :, None]
    if not fast:
        return (block, in_grads, *(jnp.where(first, one, two) for one, two in zip(results[0][2:], results[1][2:])))
    early = jnp.where(first, results[0][2], results[1][2])
    rest = jnp.where(first, results[0][3], results[1][3])
    lines = lax.dynamic_slice(early, (3 * UNIT, index * UNIT), (4, UNIT))
    return (
        block,
        in_grads,
        jnp.concatenate([early[at * UNIT : (at + 1) * UNIT] for at in range(3)], axis=1)[None],
        rest[:UNIT][None],
        rest[UNIT : 3 * UNIT].reshape(1, 2, UNIT, width),
        jnp.concatenate([rest[(3 + at) * UNIT : (4 + at) * UNIT] for at in range(4)], axis=1)[None],
        rest[7 * UNIT :][None],
        lines[None, 0:2],
        lines[None, 2:4],
    )


def solution(mesh):
    placed = (
        P(None, "dp", None, None),
        P("section", None, "dp", None, None),
        P("section", "dp", None),
        P("section", "dp", None),
        P("section", None, "dp", None),
        P("section", "dp", None),
        P("section", "dp", None),
        P("section", None, "dp"),
        P("section", None, "dp"),
    )
    return jax.shard_map(
        per_device,
        mesh=mesh,
        in_specs=placed,
        out_specs=(P("section", None, "dp", None, None), P("section", None, "dp", None, None)) + placed[2:],
        check_vma=False,
    )
```

time: 1620 us -> 533 us (0.33)
  waiting for transfers between devices: 789 us -> 161 us
  matrix products: 373 us -> 0 us
  Pallas kernels: 0 us -> 216 us
  local copies, waits for them, and re-layouts: 160 us -> 7.16 us
  other arithmetic: 153 us -> 29.5 us
  starting transfers between devices: 11.5 us -> 107 us
  blocking collectives: 63.8 us -> 0 us
  loops' own time: 39.8 us -> 0 us
    dot_general x64 -> x0, matrix products: 373 us -> none  [the longest x4 76.3 us: attend_backward(): jnp.einsum('shqk,skhd->sqhd', score_low, keyed[:, :finish], preferred_ele...]
    reduce_scatter x5 -> x0, waiting for transfers between devices: 346 us -> none  [the longest x1 76.5 us: per_device(): lax.psum_scatter(grads[4], 'dp', scatter_dimension=1, tiled=True)]
    pallas_call x0 -> x16, Pallas kernels: none -> 216 us  [the longest x2 41.5 us: attend_back(): call(functools.partial(attend_back_kernel, block), (width // 128,), [pair...]
    ppermute x4 -> x54, waiting for transfers between devices: 288 us -> 161 us  [the longest x24 68 us: moved_z(): lax.ppermute(value, 'dp', [(d, (d + 4 * steps) % count) for d in range(co...]
    all_gather x4 -> x0, waiting for transfers between devices: 99.5 us -> none  [the longest x1 43.1 us: per_device(): lax.all_gather(w_up.astype(jnp.bfloat16), 'dp', axis=1, tiled=True)]
    ppermute x4 -> x54, starting transfers between devices: 11 us -> 107 us  [the longest x24 73.5 us: moved_z(): lax.ppermute(value, 'dp', [(d, (d + 4 * steps) % count) for d in range(co...]
    all_gather x3 -> x0, blocking collectives: 63.8 us -> none  [the longest x1 23.8 us: per_device(): lax.all_gather(norm_gains.astype(jnp.bfloat16), 'dp', axis=2, tiled=True)]
    another operation x33 -> x2, local copies, waits for them, and re-layouts: 62.1 us -> 0.1 us  [packed_first(): jnp.tile(lines, (1, count))]
  transfers between devices with their start and end apart: 15 -> 54, of which waited for: 12 -> 21; matrix products, arithmetic and copies ran while one was open for 6% -> 5% of each run, Pallas kernels for 0% -> 29%
where the time goes in v1:
time: 533 us; the launch traced here: 522 us
  Pallas kernels  216 us (41%)
  waiting for transfers between devices  161 us (30%)
  starting transfers between devices  107 us (20%)
  other arithmetic  29.5 us (6%)
  local copies, waits for them, and re-layouts  7.16 us (1%)
    ppermute x24, starting transfers between devices, moved_z(): lax.ppermute(value, 'dp', [(d, (d + 4 * steps) % count) for d in range(co...  73.5 us
    ppermute x24, waiting for transfers between devices, moved_z(): lax.ppermute(value, 'dp', [(d, (d + 4 * steps) % count) for d in range(co...  68 us
    ppermute x20, waiting for transfers between devices, swapped(): lax.ppermute(value, 'dp', [(d, d ^ bit) for d in range(lax.axis_size('dp'...  50.9 us
    ppermute x10, waiting for transfers between devices, crossed(): return lax.ppermute(value, 'section', [(s, 1 - s) for s in sources])  41.7 us
    pallas_call x2, Pallas kernels, attend_back(): call(functools.partial(attend_back_kernel, block), (width // 128,), [pair...  41.5 us
    pallas_call x2, Pallas kernels, feed_forward(): call(feed_kernel, (length // ROWS,), [row, row, row, whole(16, width)] +...  36.2 us
    pallas_call x2, Pallas kernels, feed_back(): call(functools.partial(feed_back_kernel, len(es) - 1), (length // ROWS,),...  33.5 us
    pallas_call x2, Pallas kernels, attend_forward(): call(functools.partial(attend_kernel, block), (width // 128,), [pair] * 3...  31.7 us
  transfers between devices with their start and end apart: 54, of which 21 were waited for; matrix products, arithmetic and copies ran while one was open for 5% of the time, Pallas kernels for 29%

profile of v1, /device:TPU:0, one launch (start us, length us, event | category | flops | bytes accessed | tf_op | source)
XLA Modules:
  0.0 522.1 jit_solution(11542433293888639642)
XLA Ops:
  30.0 20.0 %collective-permute-start.2 = (bf16[112,512]{1,0:T(8,128)(2,1)S(1)}, bf16[112,512]{1,0:T(8,128)(2,1)S(1)}, u32[]{:S(2)}, u32[]{:S(2)}) collective-permute-start(bf16[112,512]{1,0:T(8,128)(2,1)S(1)} %get-tuple-element.191), channel_id=1, source_target_pairs={{0,8},{1,9},{2,10},{3,11},{4,12},{5,13},{6,14},{7,15},{8,0},{9,1},... | collective-permute-start | bytes 344072 | tf_op jit(solution)/shard_map/ppermute | solution.py:490
  66.2 14.1 %collective-permute-done.14 = bf16[112,512]{1,0:T(8,128)(2,1)S(1)} collective-permute-done((bf16[112,512]{1,0:T(8,128)(2,1)S(1)}, bf16[112,512]{1,0:T(8,128)(2,1)S(1)}, u32[]{:S(2)}, u32[]{:S(2)}) %collective-permute-start.14) | collective-permute-done | bytes 114720 | tf_op jit(solution)/shard_map/ppermute | solution.py:490
  92.3 8.5 %collective-permute-start.21 = (bf16[352,512]{1,0:T(8,128)(2,1)}, bf16[352,512]{1,0:T(8,128)(2,1)}, u32[]{:S(2)}, u32[]{:S(2)}) collective-permute-start(bf16[352,512]{1,0:T(8,128)(2,1)} %get-tuple-element.179), channel_id=1, source_target_pairs={{0,8},{1,9},{2,10},{3,11},{4,12},{5,13},{6,14},{7,15},{8,0},{9,1},... | collective-permute-start | bytes 1081352 | tf_op jit(solution)/shard_map/ppermute | solution.py:490
  107.6 10.5 %collective-permute-done.21 = bf16[352,512]{1,0:T(8,128)(2,1)} collective-permute-done((bf16[352,512]{1,0:T(8,128)(2,1)}, bf16[352,512]{1,0:T(8,128)(2,1)}, u32[]{:S(2)}, u32[]{:S(2)}) %collective-permute-start.21) | collective-permute-done | bytes 360480 | tf_op jit(solution)/shard_map/ppermute | solution.py:490
  131.0 7.3 %shard_map.160 = (bf16[1024,512]{1,0:T(8,128)(2,1)}, bf16[1024,512]{1,0:T(8,128)(2,1)}, bf16[1024,512]{1,0:T(8,128)(2,1)}, bf16[1024,512]{1,0:T(8,128)(2,1)}, f32[16,512]{1,0:T(8,128)}) custom-call(s32[3]{0:T(128)} %pad_add_fusion.place, bf16[1024,512]{1,0:T(8,128)(2,1)} %select_bitcast_fusion.3.x_ref, bf16[4,112,512]{2,1,0:T(8,128)(2,1)} %pad_maximum_fusion.2.w0, ...), custom_call_target="tpu_custom_call" | custom-call | flops 1610612736 | bytes 8000000 | tf_op jit(solution)/shard_map/pallas_call | solution.py:125
  138.3 15.8 %shard_map.161 = (bf16[1024,512]{1,0:T(8,128)(2,1)}, f32[1024,512]{1,0:T(8,128)}) custom-call(s32[3]{0:T(128)} %pad_add_fusion.place, bf16[1024,512]{1,0:T(8,128)(2,1)} %get-tuple-element.78.q_ref, bf16[1024,512]{1,0:T(8,128)(2,1)} %get-tuple-element.79.k_ref, bf16[1024,512]{1,0:T(8,128)(2,1)} %get-tuple-element.80.v_ref), custom_call_target="tpu_custom_call" | custom-call | flops 12000000000 | bytes 6000000 | tf_op jit(solution)/shard_map/pallas_call | solution.py:164
  158.3 18.0 %shard_map.162 = (bf16[1024,512]{1,0:T(8,128)(2,1)}, bf16[1024,512]{1,0:T(8,128)(2,1)}, f32[1024,1]{1,0:T(8,128)}, bf16[1024,512]{1,0:T(8,128)(2,1)}, bf16[1024,...) custom-call(s32[3]{0:T(128)} %pad_add_fusion.place, ...), custom_call_target="tpu_custom_call" | custom-call | flops 5905580032 | bytes 24000000 | tf_op jit(solution)/shard_map/pallas_call | solution.py:224
  177.1 7.3 %shard_map.163 = (bf16[1024,512]{1,0:T(8,128)(2,1)}, bf16[1024,512]{1,0:T(8,128)(2,1)}, bf16[1024,512]{1,0:T(8,128)(2,1)}, bf16[1024,512]{1,0:T(8,128)(2,1)}, f32[16,512]{1,0:T(8,128)}) custom-call(s32[3]{0:T(128)} %pad_add_fusion.place, bf16[1024,512]{1,0:T(8,128)(2,1)} %get-tuple-element.83.x_ref, bf16[4,112,512]{2,1,0:T(8,128)(2,1)} %copy-done.10, ...), custom_call_target="tpu_custom_call" | custom-call | flops 1610612736 | bytes 8000000 | tf_op jit(solution)/shard_map/pallas_call | solution.py:125
  184.5 15.9 %shard_map.164 = (bf16[1024,512]{1,0:T(8,128)(2,1)}, f32[1024,512]{1,0:T(8,128)}) custom-call(s32[3]{0:T(128)} %pad_add_fusion.place, bf16[1024,512]{1,0:T(8,128)(2,1)} %get-tuple-element.85.q_ref, bf16[1024,512]{1,0:T(8,128)(2,1)} %get-tuple-element.86.k_ref, bf16[1024,512]{1,0:T(8,128)(2,1)} %get-tuple-element.87.v_ref), custom_call_target="tpu_custom_call" | custom-call | flops 12000000000 | bytes 6000000 | tf_op jit(solution)/shard_map/pallas_call | solution.py:164
  201.9 18.2 %shard_map.165 = (bf16[1024,512]{1,0:T(8,128)(2,1)}, bf16[1024,512]{1,0:T(8,128)(2,1)}, f32[1024,1]{1,0:T(8,128)}, bf16[1024,512]{1,0:T(8,128)(2,1)}, bf16[1024,...) custom-call(s32[3]{0:T(128)} %pad_add_fusion.place, ...), custom_call_target="tpu_custom_call" | custom-call | flops 5905580032 | bytes 24000000 | tf_op jit(solution)/shard_map/pallas_call | solution.py:224
  220.1 16.6 %shard_map.166 = (f32[1024,512]{1,0:T(8,128)}, bf16[1024,512]{1,0:T(8,128)(2,1)}, bf16[1024,512]{1,0:T(8,128)(2,1)}, bf16[1024,2048]{1,0:T(8,128)(2,1)}, bf16[10...) custom-call(s32[3]{0:T(128)} %pad_add_fusion.place, ...), custom_call_target="tpu_custom_call" | custom-call | flops 5368709120 | bytes 24000000 | tf_op jit(solution)/shard_map/pallas_call | solution.py:296
  236.7 20.8 %shard_map.167 = (bf16[1024,512]{1,0:T(8,128)(2,1)}, bf16[1024,512]{1,0:T(8,128)(2,1)}, bf16[1024,512]{1,0:T(8,128)(2,1)}) custom-call(s32[3]{0:T(128)} %pad_add_fusion.place, bf16[1024,512]{1,0:T(8,128)(2,1)} %get-tuple-element.85.q_ref, bf16[1024,512]{1,0:T(8,128)(2,1)} %get-tuple-element.86.k_ref, bf16[1024,512]{1,0:T(8,128)(2,1)} %get-tuple-element.87.v_ref, ...), custom_call_target="tpu_custom_call" | custom-call | flops 20000000000 | bytes 10000000 | tf_op jit(solution)/shard_map/pallas_call | solution.py:367
  257.6 9.3 %shard_map.168 = (f32[1024,512]{1,0:T(8,128)}, bf16[1024,512]{1,0:T(8,128)(2,1)}, f32[8,512]{1,0:T(8,128)}) custom-call(s32[3]{0:T(128)} %pad_add_fusion.place, bf16[1024,512]{1,0:T(8,128)(2,1)} %get-tuple-element.83.x_ref, f32[1024,512]{1,0:T(8,128)} %get-tuple-element.98.dm_ref, bf16[1024,512]{1,0:T(8,128)(2,1)} %get-tuple-element.101.dq_ref, ...), custom_call_target="tpu_custom_call" | custom-call | flops 2147483648 | bytes 12000000 | tf_op jit(solution)/shard_map/pallas_call | solution.py:416
  270.3 16.9 %shard_map.169 = (f32[1024,512]{1,0:T(8,128)}, bf16[1024,512]{1,0:T(8,128)(2,1)}, bf16[1024,512]{1,0:T(8,128)(2,1)}, bf16[1024,2048]{1,0:T(8,128)(2,1)}, bf16[10...) custom-call(s32[3]{0:T(128)} %pad_add_fusion.place, ...), custom_call_target="tpu_custom_call" | custom-call | flops 5368709120 | bytes 24000000 | tf_op jit(solution)/shard_map/pallas_call | solution.py:296
  287.2 13.1 %shard_map.174 = (bf16[2,4,352,512]{3,2,1,0:T(8,128)(2,1)}, bf16[2,4,352,512]{3,2,1,0:T(8,128)(2,1)}) custom-call(s32[3]{0:T(128)} %pad_add_fusion.place, bf16[1024,512]{1,0:T(8,128)(2,1)} %get-tuple-element.81.o_ref, bf16[1024,512]{1,0:T(8,128)(2,1)} %get-tuple-element.77.n1_ref, bf16[1024,512]{1,0:T(8,128)(2,1)} %get-tuple-element.106.refs_2_.n2_ref, ...), custom_call_target="tpu_custom_call" | custom-call | flops 5905580032 | bytes 26000000 | tf_op jit(solution)/shard_map/pallas_call | solution.py:453
  300.5 20.7 %shard_map.170 = (bf16[1024,512]{1,0:T(8,128)(2,1)}, bf16[1024,512]{1,0:T(8,128)(2,1)}, bf16[1024,512]{1,0:T(8,128)(2,1)}) custom-call(s32[3]{0:T(128)} %pad_add_fusion.place, bf16[1024,512]{1,0:T(8,128)(2,1)} %get-tuple-element.78.q_ref, bf16[1024,512]{1,0:T(8,128)(2,1)} %get-tuple-element.79.k_ref, bf16[1024,512]{1,0:T(8,128)(2,1)} %get-tuple-element.80.v_ref, ...), custom_call_target="tpu_custom_call" | custom-call | flops 20000000000 | bytes 10000000 | tf_op jit(solution)/shard_map/pallas_call | solution.py:367
  321.2 9.3 %shard_map.171 = (f32[1024,512]{1,0:T(8,128)}, bf16[1024,512]{1,0:T(8,128)(2,1)}, f32[8,512]{1,0:T(8,128)}) custom-call(s32[3]{0:T(128)} %pad_add_fusion.place, bf16[1024,512]{1,0:T(8,128)(2,1)} %select_bitcast_fusion.3.x_ref, f32[1024,512]{1,0:T(8,128)} %get-tuple-element.113.dm_ref, bf16[1024,512]{1,0:T(8,128)(2,1)} %get-tuple-element.116.dq_ref, ...), custom_call_target="tpu_custom_call" | custom-call | flops 2147483648 | bytes 12000000 | tf_op jit(solution)/shard_map/pallas_call | solution.py:416
  345.4 13.5 %shard_map.175 = (bf16[2,4,352,512]{3,2,1,0:T(8,128)(2,1)}, bf16[2,4,352,512]{3,2,1,0:T(8,128)(2,1)}) custom-call(s32[3]{0:T(128)} %pad_add_fusion.place, bf16[1024,512]{1,0:T(8,128)(2,1)} %get-tuple-element.88.o_ref, bf16[1024,512]{1,0:T(8,128)(2,1)} %get-tuple-element.84.n1_ref, bf16[1024,512]{1,0:T(8,128)(2,1)} %get-tuple-element.91.refs_1_.n2_ref, ...), custom_call_target="tpu_custom_call" | custom-call | flops 5905580032 | bytes 26000000 | tf_op jit(solution)/shard_map/pallas_call | solution.py:453
  363.3 8.8 %collective-permute-done.28 = bf16[1024,512]{1,0:T(8,128)(2,1)S(1)} collective-permute-done((bf16[1024,512]{1,0:T(8,128)(2,1)}, bf16[1024,512]{1,0:T(8,128)(2,1)S(1)}, u32[]{:S(2)}, u32[]{:S(2)}) %collective-permute-start.28) | collective-permute-done | bytes 1048608 | tf_op jit(solution)/shard_map/ppermute | solution.py:498
  377.5 16.5 %collective-permute-done.26 = bf16[1024,512]{1,0:T(8,128)(2,1)S(1)} collective-permute-done((bf16[1024,512]{1,0:T(8,128)(2,1)S(1)}, bf16[1024,512]{1,0:T(8,128)(2,1)S(1)}, u32[]{:S(2)}, u32[]{:S(2)}) %collective-permute-start.26) | collective-permute-done | bytes 1048608 | tf_op jit(solution)/shard_map/ppermute | solution.py:498
  395.4 8.3 %collective-permute-start.32 = (bf16[112,512]{1,0:T(8,128)(2,1)S(1)}, bf16[112,512]{1,0:T(8,128)(2,1)S(1)}, u32[]{:S(2)}, u32[]{:S(2)}) collective-permute-start(bf16[112,512]{1,0:T(8,128)(2,1)S(1)} %get-tuple-element.181), channel_id=1, source_target_pairs={{0,4},{1,5},{2,6},{3,7},{4,8},{5,9},{6,10},{7,11},{8,12},{9,13},{1... | collective-permute-start | bytes 344072 | tf_op jit(solution)/shard_map/ppermute | solution.py:490
  433.1 23.4 %collective-permute-done.43 = bf16[4,352,512]{2,1,0:T(8,128)(2,1)S(1)} collective-permute-done((bf16[4,352,512]{2,1,0:T(8,128)(2,1)S(1)}, bf16[4,352,512]{2,1,0:T(8,128)(2,1)S(1)}, u32[]{:S(2)}, u32[]{:S(2)}) %collective-permute-start.43) | collective-permute-done | bytes 1441824 | tf_op jit(solution)/shard_map/ppermute | solution.py:494
  461.1 18.7 %collective-permute-done.49 = bf16[4,352,512]{2,1,0:T(8,128)(2,1)S(1)} collective-permute-done((bf16[4,352,512]{2,1,0:T(8,128)(2,1)S(1)}, bf16[4,352,512]{2,1,0:T(8,128)(2,1)S(1)}, u32[]{:S(2)}, u32[]{:S(2)}) %collective-permute-start.49) | collective-permute-done | bytes 1441824 | tf_op jit(solution)/shard_map/ppermute | solution.py:494
  496.5 12.6 %collective-permute-done.51 = bf16[352,512]{1,0:T(8,128)(2,1)S(1)} collective-permute-done((bf16[352,512]{1,0:T(8,128)(2,1)S(1)}, bf16[352,512]{1,0:T(8,128)(2,1)S(1)}, u32[]{:S(2)}, u32[]{:S(2)}) %collective-permute-start.51) | collective-permute-done | bytes 360480 | tf_op jit(solution)/shard_map/ppermute | solution.py:490
  (210 shorter events, 176.2 us)
Async XLA Ops:
  18.5 31.5 %collective-permute-start.9 = (bf16[352,512]{1,0:T(8,128)(2,1)S(1)}, bf16[352,512]{1,0:T(8,128)(2,1)S(1)}, u32[]{:S(2)}, u32[]{:S(2)}) collective-permute-start(bf16[352,512]{1,0:T(8,128)(2,1)S(1)} %get-tuple-element.180), channel_id=1, source_target_pairs={{0,8},{1,9},{2,10},{3,11},{4,12},{5,13},{6,14},{7,15},{8,0},{9,1},... | collective-permute-start | bytes 1081352 | tf_op jit(solution)/shard_map/ppermute | solution.py:490
  30.0 31.2 %collective-permute-start.2 = (bf16[112,512]{1,0:T(8,128)(2,1)S(1)}, bf16[112,512]{1,0:T(8,128)(2,1)S(1)}, u32[]{:S(2)}, u32[]{:S(2)}) collective-permute-start(bf16[112,512]{1,0:T(8,128)(2,1)S(1)} %get-tuple-element.191), channel_id=1, source_target_pairs={{0,8},{1,9},{2,10},{3,11},{4,12},{5,13},{6,14},{7,15},{8,0},{9,1},... | collective-permute-start | bytes 344072 | tf_op jit(solution)/shard_map/ppermute | solution.py:490
  52.2 70.1 %collective-permute-start.11 = (bf16[4,352,512]{2,1,0:T(8,128)(2,1)S(1)}, bf16[4,352,512]{2,1,0:T(8,128)(2,1)}, u32[]{:S(2)}, u32[]{:S(2)}) collective-permute-start(bf16[4,352,512]{2,1,0:T(8,128)(2,1)S(1)} %pad_maximum_fusion.w0.refs_10_.r0), channel_id=1, source_target_pairs={{0,2},{1,3},{2,0},{3,1},{4,6},{5,7},{6,4},{7,5},{8,10},{9,11},{10,... | collective-permute-start | bytes 4325384 | tf_op jit(solution)/shard_map/ppermute | solution.py:494
  62.0 29.7 %collective-permute-start.4 = (bf16[4,112,512]{2,1,0:T(8,128)(2,1)}, bf16[4,112,512]{2,1,0:T(8,128)(2,1)}, u32[]{:S(2)}, u32[]{:S(2)}) collective-permute-start(bf16[4,112,512]{2,1,0:T(8,128)(2,1)} %pad_maximum_fusion.2.w0), channel_id=1, source_target_pairs={{0,2},{1,3},{2,0},{3,1},{4,6},{5,7},{6,4},{7,5},{8,10},{9,11},{10,... | collective-permute-start | bytes 1376264 | tf_op jit(solution)/shard_map/ppermute | solution.py:494
  64.6 57.2 %collective-permute-start.27 = (bf16[1024,512]{1,0:T(8,128)(2,1)}, bf16[1024,512]{1,0:T(8,128)(2,1)}, u32[]{:S(2)}, u32[]{:S(2)}) collective-permute-start(bf16[1024,512]{1,0:T(8,128)(2,1)} %select_bitcast_fusion), channel_id=1, source_target_pairs={{0,16},{16,0},{1,17},{17,1},{2,18},{18,2},{3,19},{19,3},{4,20},{20... | collective-permute-start | bytes 3145736 | tf_op jit(solution)/shard_map/ppermute | solution.py:498
  66.1 34.7 %collective-permute-start.20 = (bf16[352,512]{1,0:T(8,128)(2,1)}, bf16[352,512]{1,0:T(8,128)(2,1)}, u32[]{:S(2)}, u32[]{:S(2)}) collective-permute-start(bf16[352,512]{1,0:T(8,128)(2,1)} %get-tuple-element.179), channel_id=1, source_target_pairs={{0,4},{1,5},{2,6},{3,7},{4,8},{5,9},{6,10},{7,11},{8,12},{9,13},{1... | collective-permute-start | bytes 1081352 | tf_op jit(solution)/shard_map/ppermute | solution.py:490
  91.7 29.5 %collective-permute-start.5 = (bf16[4,112,512]{2,1,0:T(8,128)(2,1)}, bf16[4,112,512]{2,1,0:T(8,128)(2,1)}, u32[]{:S(2)}, u32[]{:S(2)}) collective-permute-start(bf16[4,112,512]{2,1,0:T(8,128)(2,1)} %pad_maximum_fusion.2.w0), channel_id=1, source_target_pairs={{0,1},{1,0},{2,3},{3,2},{4,5},{5,4},{6,7},{7,6},{8,9},{9,8},{10,11... | collective-permute-start | bytes 1376264 | tf_op jit(solution)/shard_map/ppermute | solution.py:494
  121.2 33.0 %collective-permute-start.12 = (bf16[4,352,512]{2,1,0:T(8,128)(2,1)S(1)}, bf16[4,352,512]{2,1,0:T(8,128)(2,1)S(1)}, u32[]{:S(2)}, u32[]{:S(2)}) collective-permute-start(bf16[4,352,512]{2,1,0:T(8,128)(2,1)S(1)} %pad_maximum_fusion.w0.refs_10_.r0), channel_id=1, source_target_pairs={{0,1},{1,0},{2,3},{3,2},{4,5},{5,4},{6,7},{7,6},{8,9},{9,8},{10,11... | collective-permute-start | bytes 4325384 | tf_op jit(solution)/shard_map/ppermute | solution.py:494
  121.8 36.5 %collective-permute-start.23 = (bf16[4,352,512]{2,1,0:T(8,128)(2,1)S(1)}, bf16[4,352,512]{2,1,0:T(8,128)(2,1)}, u32[]{:S(2)}, u32[]{:S(2)}) collective-permute-start(bf16[4,352,512]{2,1,0:T(8,128)(2,1)S(1)} %pad_maximum_fusion.1.w0.refs_9_.r0), channel_id=1, source_target_pairs={{0,2},{1,3},{2,0},{3,1},{4,6},{5,7},{6,4},{7,5},{8,10},{9,11},{10,... | collective-permute-start | bytes 4325384 | tf_op jit(solution)/shard_map/ppermute | solution.py:494
  122.3 36.0 %collective-permute-start.13 = (bf16[4,352,512]{2,1,0:T(8,128)(2,1)}, bf16[4,352,512]{2,1,0:T(8,128)(2,1)}, u32[]{:S(2)}, u32[]{:S(2)}) collective-permute-start(bf16[4,352,512]{2,1,0:T(8,128)(2,1)} %collective-permute-done.11.w1.refs_11_.r1), channel_id=1, source_target_pairs={{0,1},{1,0},{2,3},{3,2},{4,5},{5,4},{6,7},{7,6},{8,9},{9,8},{10,11... | collective-permute-start | bytes 4325384 | tf_op jit(solution)/shard_map/ppermute | solution.py:494
  130.2 46.1 %collective-permute-start.18 = (bf16[4,112,512]{2,1,0:T(8,128)(2,1)S(1)}, bf16[4,112,512]{2,1,0:T(8,128)(2,1)S(1)}, u32[]{:S(2)}, u32[]{:S(2)}) collective-permute-start(bf16[4,112,512]{2,1,0:T(8,128)(2,1)S(1)} %pad_maximum_fusion.3.w0), channel_id=1, source_target_pairs={{0,1},{1,0},{2,3},{3,2},{4,5},{5,4},{6,7},{7,6},{8,9},{9,8},{10,11... | collective-permute-start | bytes 1376264 | tf_op jit(solution)/shard_map/ppermute | solution.py:494
  130.2 46.1 %collective-permute-start.19 = (bf16[4,112,512]{2,1,0:T(8,128)(2,1)}, bf16[4,112,512]{2,1,0:T(8,128)(2,1)}, u32[]{:S(2)}, u32[]{:S(2)}) collective-permute-start(bf16[4,112,512]{2,1,0:T(8,128)(2,1)} %collective-permute-done.17.w1), channel_id=1, source_target_pairs={{0,1},{1,0},{2,3},{3,2},{4,5},{5,4},{6,7},{7,6},{8,9},{9,8},{10,11... | collective-permute-start | bytes 1376264 | tf_op jit(solution)/shard_map/ppermute | solution.py:494
  154.2 46.1 %collective-permute-start.24 = (bf16[4,352,512]{2,1,0:T(8,128)(2,1)S(1)}, bf16[4,352,512]{2,1,0:T(8,128)(2,1)S(1)}, u32[]{:S(2)}, u32[]{:S(2)}) collective-permute-start(bf16[4,352,512]{2,1,0:T(8,128)(2,1)S(1)} %pad_maximum_fusion.1.w0.refs_9_.r0), channel_id=1, source_target_pairs={{0,1},{1,0},{2,3},{3,2},{4,5},{5,4},{6,7},{7,6},{8,9},{9,8},{10,11... | collective-permute-start | bytes 4325384 | tf_op jit(solution)/shard_map/ppermute | solution.py:494
  158.3 42.0 %collective-permute-start.25 = (bf16[4,352,512]{2,1,0:T(8,128)(2,1)}, bf16[4,352,512]{2,1,0:T(8,128)(2,1)S(1)}, u32[]{:S(2)}, u32[]{:S(2)}) collective-permute-start(bf16[4,352,512]{2,1,0:T(8,128)(2,1)} %collective-permute-done.23.w1.refs_10_.r1), channel_id=1, source_target_pairs={{0,1},{1,0},{2,3},{3,2},{4,5},{5,4},{6,7},{7,6},{8,9},{9,8},{10,11... | collective-permute-start | bytes 4325384 | tf_op jit(solution)/shard_map/ppermute | solution.py:494
  266.9 106.8 %collective-permute-start.29 = (bf16[1024,512]{1,0:T(8,128)(2,1)}, bf16[1024,512]{1,0:T(8,128)(2,1)S(1)}, u32[]{:S(2)}, u32[]{:S(2)}) collective-permute-start(bf16[1024,512]{1,0:T(8,128)(2,1)} %get-tuple-element.105.refs_1_), channel_id=1, source_target_pairs={{0,16},{1,17},{2,18},{3,19},{4,20},{5,21},{6,22},{7,23},{8,24},{9,... | collective-permute-start | bytes 3145736 | tf_op jit(solution)/shard_map/ppermute | solution.py:498
  300.3 107.1 %collective-permute-start.42 = (bf16[2,4,352,512]{3,2,1,0:T(8,128)(2,1)}, bf16[2,4,352,512]{3,2,1,0:T(8,128)(2,1)S(1)}, u32[]{:S(2)}, u32[]{:S(2)}) collective-permute-start(bf16[2,4,352,512]{3,2,1,0:T(8,128)(2,1)} %get-tuple-element.137), channel_id=1, source_target_pairs={{0,1},{1,0},{2,3},{3,2},{4,5},{5,4},{6,7},{7,6},{8,9},{9,8},{10,11... | collective-permute-start | bytes 8650760 | tf_op jit(solution)/shard_map/ppermute | solution.py:494
  359.0 35.0 %collective-permute-start.26 = (bf16[1024,512]{1,0:T(8,128)(2,1)S(1)}, bf16[1024,512]{1,0:T(8,128)(2,1)S(1)}, u32[]{:S(2)}, u32[]{:S(2)}) collective-permute-start(bf16[1024,512]{1,0:T(8,128)(2,1)S(1)} %broadcast_select_fusion.3), channel_id=1, source_target_pairs={{0,16},{16,0},{1,17},{17,1},{2,18},{18,2},{3,19},{19,3},{4,20},{20... | collective-permute-start | bytes 3145736 | tf_op jit(solution)/shard_map/ppermute | solution.py:498
  363.1 60.5 %collective-permute-start.48 = (bf16[2,4,352,512]{3,2,1,0:T(8,128)(2,1)}, bf16[2,4,352,512]{3,2,1,0:T(8,128)(2,1)S(1)}, u32[]{:S(2)}, u32[]{:S(2)}) collective-permute-start(bf16[2,4,352,512]{3,2,1,0:T(8,128)(2,1)} %get-tuple-element.144), channel_id=1, source_target_pairs={{0,1},{1,0},{2,3},{3,2},{4,5},{5,4},{6,7},{7,6},{8,9},{9,8},{10,11... | collective-permute-start | bytes 8650760 | tf_op jit(solution)/shard_map/ppermute | solution.py:494
  373.6 33.5 %collective-permute-start.37 = (bf16[4,112,512]{2,1,0:T(8,128)(2,1)S(1)}, bf16[4,112,512]{2,1,0:T(8,128)(2,1)S(1)}, u32[]{:S(2)}, u32[]{:S(2)}) collective-permute-start(bf16[4,112,512]{2,1,0:T(8,128)(2,1)S(1)} %fusion.11), channel_id=1, source_target_pairs={{0,2},{1,3},{2,0},{3,1},{4,6},{5,7},{6,4},{7,5},{8,10},{9,11},{10,... | collective-permute-start | bytes 1376264 | tf_op jit(solution)/shard_map/ppermute | solution.py:494
  422.0 34.5 %collective-permute-start.43 = (bf16[4,352,512]{2,1,0:T(8,128)(2,1)S(1)}, bf16[4,352,512]{2,1,0:T(8,128)(2,1)S(1)}, u32[]{:S(2)}, u32[]{:S(2)}) collective-permute-start(bf16[4,352,512]{2,1,0:T(8,128)(2,1)S(1)} %fusion.2), channel_id=1, source_target_pairs={{0,2},{1,3},{2,0},{3,1},{4,6},{5,7},{6,4},{7,5},{8,10},{9,11},{10,... | collective-permute-start | bytes 4325384 | tf_op jit(solution)/shard_map/ppermute | solution.py:494
  425.3 54.5 %collective-permute-start.49 = (bf16[4,352,512]{2,1,0:T(8,128)(2,1)S(1)}, bf16[4,352,512]{2,1,0:T(8,128)(2,1)S(1)}, u32[]{:S(2)}, u32[]{:S(2)}) collective-permute-start(bf16[4,352,512]{2,1,0:T(8,128)(2,1)S(1)} %fusion.3), channel_id=1, source_target_pairs={{0,2},{1,3},{2,0},{3,1},{4,6},{5,7},{6,4},{7,5},{8,10},{9,11},{10,... | collective-permute-start | bytes 4325384 | tf_op jit(solution)/shard_map/ppermute | solution.py:494
  457.2 30.3 %collective-permute-start.44 = (bf16[352,512]{1,0:T(8,128)(2,1)S(1)}, bf16[352,512]{1,0:T(8,128)(2,1)S(1)}, u32[]{:S(2)}, u32[]{:S(2)}) collective-permute-start(bf16[352,512]{1,0:T(8,128)(2,1)S(1)} %get-tuple-element.168), channel_id=1, source_target_pairs={{0,4},{1,5},{2,6},{3,7},{4,8},{5,9},{6,10},{7,11},{8,12},{9,13},{1... | collective-permute-start | bytes 1081352 | tf_op jit(solution)/shard_map/ppermute | solution.py:490
  457.6 32.5 %collective-permute-start.45 = (bf16[352,512]{1,0:T(8,128)(2,1)S(1)}, bf16[352,512]{1,0:T(8,128)(2,1)S(1)}, u32[]{:S(2)}, u32[]{:S(2)}) collective-permute-start(bf16[352,512]{1,0:T(8,128)(2,1)S(1)} %get-tuple-element.170), channel_id=1, source_target_pairs={{0,8},{1,9},{2,10},{3,11},{4,12},{5,13},{6,14},{7,15},{8,0},{9,1},... | collective-permute-start | bytes 1081352 | tf_op jit(solution)/shard_map/ppermute | solution.py:490
  457.9 32.2 %collective-permute-start.46 = (bf16[352,512]{1,0:T(8,128)(2,1)S(1)}, bf16[352,512]{1,0:T(8,128)(2,1)S(1)}, u32[]{:S(2)}, u32[]{:S(2)}) collective-permute-start(bf16[352,512]{1,0:T(8,128)(2,1)S(1)} %get-tuple-element.169), channel_id=1, source_target_pairs={{0,12},{1,13},{2,14},{3,15},{4,0},{5,1},{6,2},{7,3},{8,4},{9,5},{1... | collective-permute-start | bytes 1081352 | tf_op jit(solution)/shard_map/ppermute | solution.py:490
  (55 other events, 950.8 us)

commit v2 on v1

v2 whole, which is shorter than its diff:
```python
import functools

import jax
import jax.numpy as jnp
from jax import lax
from jax.experimental import pallas as pl
from jax.experimental.pallas import tpu as pltpu
from jax.sharding import PartitionSpec as P

HD = 64
ROWS = 256
bf16 = jnp.bfloat16
f32 = jnp.float32
root_term = 0.7978845608
cube_term = 0.044715
VMEM = 56 * 1024 * 1024
PARTS = 16
UNIT = 32
FIRST = 3 * UNIT + 16
REST = 11 * UNIT


def dense(left, right):
    return jnp.dot(left, right, preferred_element_type=f32)


def cross(left, right):
    return lax.dot_general(left, right, (((0,), (0,)), ((), ())), preferred_element_type=f32)


def against(left, right):
    return lax.dot_general(left, right, (((1,), (1,)), ((), ())), preferred_element_type=f32)


def normalise(values):
    centred = values - jnp.mean(values, axis=-1, keepdims=True)
    spread = jnp.mean(centred * centred, axis=-1, keepdims=True)
    scale = lax.rsqrt(spread + 1e-05)
    return centred * scale, scale


def norm_back(grad, hat, scale, gain):
    spread = grad * gain
    first = jnp.mean(spread, axis=-1, keepdims=True)
    second = jnp.mean(spread * hat, axis=-1, keepdims=True)
    return scale * (spread - first - hat * second)


ANY = pl.BlockSpec(memory_space=pl.ANY)


def struct(shape, dtype):
    return jax.ShapeDtypeStruct(shape, dtype)


def rows_of(width):
    return pl.BlockSpec((ROWS, width), lambda i, place: (i, 0))


def whole(*shape):
    return pl.BlockSpec(shape, lambda i, place: (0,) * len(shape))


def call(kernel, grid, in_specs, out_specs, out_shape, scratch=(), flops=0, moved=0, waits=(), onto=()):
    extra = len(onto) + len(waits)
    count = len(in_specs)

    def run(*args):
        def body(*refs):
            kernel(*refs[: 1 + count], *refs[1 + count + extra :])

        return pl.pallas_call(
            body,
            grid_spec=pltpu.PrefetchScalarGridSpec(
                num_scalar_prefetch=1, grid=grid, in_specs=in_specs + [ANY] * extra, out_specs=out_specs, scratch_shapes=list(scratch)
            ),
            out_shape=out_shape,
            input_output_aliases={1 + count + at: at for at in range(len(onto))},
            compiler_params=pltpu.CompilerParams(dimension_semantics=("arbitrary",), vmem_limit_bytes=VMEM),
            cost_estimate=pl.CostEstimate(flops=flops, bytes_accessed=moved, transcendentals=0),
        )(*args, *onto, *waits)

    return run


def fetches(place, sources, target, sems, cuts, base=0):
    copies = []
    for number, (start, stop) in enumerate(cuts):
        group = []
        for index, source in enumerate(sources):
            for slot in range(4):
                part = ((place[0] - slot) & 3) * 4 + (place[1] ^ (index & 1)) * 2 + (place[2] ^ (index >> 1))
                group.append(
                    pltpu.make_async_copy(
                        source.at[slot, pl.ds(start, stop - start)],
                        target.at[part, pl.ds(start - base, stop - start)],
                        sems.at[number],
                    )
                )
        copies.append(group)
    return copies


def unit(ref, at):
    return ref[:, at * UNIT : (at + 1) * UNIT, :].reshape(PARTS * UNIT, ref.shape[2])


def down_part(ref, at, start=7):
    return ref[at * 4 : at * 4 + 4, start * UNIT : (start + 4) * UNIT, :].reshape(16 * UNIT, ref.shape[2])


def rest_copy(layer, source, target, sem, start, stop, base):
    cut, goal = pl.ds(start, stop - start), pl.ds(start - base, stop - start)
    return pltpu.make_async_copy(source.at[:, cut], target.at[:, goal], sem)


def at_start(copies):
    @pl.when(pl.program_id(0) == 0)
    def _():
        for copy in copies:
            copy.start()
        for copy in copies:
            copy.wait()


def qkv_kernel(many, place, x_ref, *refs):
    n_ref, q_ref, k_ref, v_ref, vec_ref, buf, sems = refs[many:]
    copies = fetches(place, refs[:many], buf, sems, ((0, FIRST),))[0]

    @pl.when(pl.program_id(0) == 0)
    def _():
        for copy in copies:
            copy.start()
        for copy in copies:
            copy.wait()
        vec_ref[...] = jnp.sum(buf[:, 3 * UNIT : 3 * UNIT + 16, :].astype(f32), axis=0)

    hat, _ = normalise(x_ref[...].astype(f32))
    n1 = (hat * vec_ref[0:1, :]).astype(bf16)
    n_ref[...] = n1
    q_ref[...] = (dense(n1, unit(buf, 0)).astype(bf16) * 0.125).astype(bf16)
    k_ref[...] = dense(n1, unit(buf, 1)).astype(bf16)
    v_ref[...] = dense(n1, unit(buf, 2)).astype(bf16)


def qkv_forward(place, x, weights, waits=()):
    length, width = x.shape
    row = rows_of(width)
    return call(
        functools.partial(qkv_kernel, len(weights)),
        (length // ROWS,),
        [row] + [ANY] * len(weights),
        [row] * 4 + [whole(16, width)],
        [struct((length, width), bf16)] * 4 + [struct((16, width), f32)],
        [pltpu.VMEM((PARTS, FIRST, width), bf16), pltpu.SemaphoreType.DMA((1,))],
        flops=2 * length * width * 3 * width,
        moved=8_000_000,
        waits=waits,
    )(place, x, *weights)


def attend_kernel(block, place, q_ref, k_ref, v_ref, o_ref, s_ref):
    length = q_ref.shape[0]
    lane = lax.broadcasted_iota(jnp.int32, (block, 128), 1)
    row = lax.broadcasted_iota(jnp.int32, (block, block), 0)
    col = lax.broadcasted_iota(jnp.int32, (block, block), 1)
    for index in range(length // block):
        start, stop = index * block, (index + 1) * block
        q = q_ref[start:stop, :]
        outs, logs = [], []
        for head in range(2):
            mine = (lane >= head * HD) & (lane < (head + 1) * HD)
            own = jnp.where(mine, q, jnp.zeros_like(q))
            scores = against(own, k_ref[:stop, :])
            last = jnp.where(row >= col, scores[:, start:], -1e30)
            scores = jnp.concatenate([scores[:, :start], last], axis=1) if start else last
            highest = jnp.max(scores, axis=1, keepdims=True)
            weights = jnp.exp(scores - highest)
            total = jnp.sum(weights, axis=1, keepdims=True)
            outs.append(dense(weights.astype(bf16), v_ref[:stop, :]) * (1.0 / total))
            logs.append(highest + jnp.log(total))
        o_ref[start:stop, :] = jnp.where(lane < HD, outs[0], outs[1]).astype(bf16)
        s_ref[start:stop, :] = jnp.where(lane < HD, logs[0], logs[1])


def attend_forward(place, q, k, v, start, onto=(), waits=(), block=256):
    length, width = q.shape
    pair = pl.BlockSpec((length, 128), lambda i, place: (0, i + start))
    return call(
        functools.partial(attend_kernel, block),
        (width // 256,),
        [pair] * 3,
        [pair, pair],
        [struct((length, width), bf16), struct((length, width), f32)],
        flops=6_000_000_000,
        moved=3_000_000,
        onto=onto,
        waits=waits,
    )(place, q, k, v)


def gate_kernel(layer, place, x_ref, n1_ref, o_ref, vec_ref, rest_ref,
                middle_ref, n2_ref, scale_ref, ga_ref, ta_ref, buf, sems):
    at_start([rest_copy(layer, rest_ref, buf, sems.at[0], 0, 2 * UNIT, 0)])

    branch = dense(o_ref[...], unit(buf, 0))
    opening = jax.nn.sigmoid(dense(n1_ref[...], unit(buf, 1)) + vec_ref[2:3, :])
    gated = opening * branch
    middle = x_ref[...].astype(f32) + gated
    middle_ref[...] = middle
    ga_ref[...] = opening.astype(bf16)
    ta_ref[...] = (gated * (1.0 - opening)).astype(bf16)
    hat, scale = normalise(middle)
    n2_ref[...] = (hat * vec_ref[1:2, :]).astype(bf16)
    scale_ref[...] = scale


def gate_forward(place, layer, x, n1, o, vec, rest, waits=()):
    length, width = x.shape
    row, half = rows_of(width), struct((length, width), bf16)
    return call(
        functools.partial(gate_kernel, layer),
        (length // ROWS,),
        [row, row, row, whole(16, width), ANY],
        [row, row, rows_of(1), row, row],
        [struct((length, width), f32), half, struct((length, 1), f32), half, half],
        [pltpu.VMEM((PARTS, 2 * UNIT, width), bf16), pltpu.SemaphoreType.DMA((1,))],
        flops=2 * length * width * 2 * width,
        moved=9_000_000,
        waits=waits,
    )(place, x, n1, o, vec, rest)


def feed_kernel(layer, place, middle_ref, n2_ref, vec_ref, rest_ref, y_ref, h_ref, slope_ref, gf_ref, tf_ref, buf, sems):
    at_start([rest_copy(layer, rest_ref, buf, sems.at[0], 2 * UNIT, REST, 2 * UNIT)])

    n2 = n2_ref[...]
    feed = None
    for at in range(4):
        cut = slice(at * 512, at * 512 + 512)
        u = dense(n2, unit(buf, 1 + at))
        square = u * u
        inner = jnp.tanh(u * (root_term + (root_term * cube_term) * square))
        half = 0.5 + 0.5 * inner
        active = (u * half).astype(bf16)
        h_ref[:, cut] = active
        slope = half + u * (0.5 - 0.5 * inner * inner) * (root_term + (3.0 * root_term * cube_term) * square)
        slope_ref[:, cut] = slope.astype(bf16)
        part = dense(active, down_part(buf, at, 5))
        feed = part if feed is None else feed + part
    closing = jax.nn.sigmoid(dense(n2, unit(buf, 0)) + vec_ref[3:4, :])
    gated = closing * feed
    gf_ref[...] = closing.astype(bf16)
    tf_ref[...] = (gated * (1.0 - closing)).astype(bf16)
    y_ref[...] = (middle_ref[...] + gated).astype(bf16)


def feed_forward(place, layer, middle, n2, vec, rest, waits=()):
    length, width = middle.shape
    wide = 4 * width
    row, half = rows_of(width), struct((length, width), bf16)
    big, bigs = rows_of(wide), struct((length, wide), bf16)
    return call(
        functools.partial(feed_kernel, layer),
        (length // ROWS,),
        [row, row, whole(16, width), ANY],
        [row, big, big, row, row],
        [half, bigs, bigs, half, half],
        [pltpu.VMEM((PARTS, REST - 2 * UNIT, width), bf16), pltpu.SemaphoreType.DMA((1,))],
        flops=2 * length * width * (width + 2 * wide),
        moved=20_000_000,
        waits=waits,
    )(place, middle, n2, vec, rest)


def feed_back_kernel(layer, extra, place, *refs):
    at = 1 + extra
    e_refs = refs[:at]
    n2_ref, scale_ref, ga_ref, ta_ref, slope_ref, gf_ref, tf_ref, vec_ref, rest_ref = refs[at : at + 9]
    dm_ref, df_ref, dzf_ref, du_ref, da_ref, dza_ref, do_ref, small_ref, buf, sems = refs[at + 9 :]
    at_start([rest_copy(layer, rest_ref, buf, sems.at[0], 0, REST, 0)])
    at_first = pl.program_id(0) == 0

    e = e_refs[0][...].astype(f32)
    for ref in e_refs[1:]:
        e = e + ref[...].astype(f32)
    df = (e * gf_ref[...].astype(f32)).astype(bf16)
    dzf = (e * tf_ref[...].astype(f32)).astype(bf16)
    df_ref[...] = df
    dzf_ref[...] = dzf
    dn2 = against(dzf, unit(buf, 2))
    for at in range(4):
        cut = slice(at * 512, at * 512 + 512)
        dh = against(df, down_part(buf, at))
        du = (dh * slope_ref[:, cut].astype(f32)).astype(bf16)
        du_ref[:, cut] = du
        dn2 = dn2 + against(du, unit(buf, 3 + at))
    gain = vec_ref[1:2, :]
    hat = n2_ref[...].astype(f32) * (1.0 / gain)
    dm = e + norm_back(dn2, hat, scale_ref[...], gain)
    dm_ref[...] = dm
    da = (dm * ga_ref[...].astype(f32)).astype(bf16)
    dza = (dm * ta_ref[...].astype(f32)).astype(bf16)
    da_ref[...] = da
    dza_ref[...] = dza
    do_ref[...] = against(da, unit(buf, 0)).astype(bf16)
    sums = jnp.concatenate(
        [jnp.sum(part.astype(f32), axis=0, keepdims=True) for part in (dza, dzf)] + [jnp.zeros((14, e.shape[1]), f32)],
        axis=0,
    )

    @pl.when(at_first)
    def _():
        small_ref[...] = sums

    @pl.when(pl.program_id(0) > 0)
    def _():
        small_ref[...] += sums


def feed_back(place, layer, es, n2, scale, ga, ta, slope, gf, tf, vec, rest, waits=()):
    length, width = n2.shape
    wide = 4 * width
    row, half = rows_of(width), struct((length, width), bf16)
    big, bigs = rows_of(wide), struct((length, wide), bf16)
    return call(
        functools.partial(feed_back_kernel, layer, len(es) - 1),
        (length // ROWS,),
        [row] * len(es) + [row, rows_of(1), row, row, big, row, row, whole(16, width), ANY],
        [row, row, row, big, row, row, row, whole(16, width)],
        [struct((length, width), f32), half, half, bigs, half, half, half, struct((16, width), f32)],
        [pltpu.VMEM((PARTS, REST, width), bf16), pltpu.SemaphoreType.DMA((1,))],
        flops=2 * length * width * (2 * width + 2 * wide),
        moved=24_000_000,
        waits=waits,
    )(place, *es, n2, scale, ga, ta, slope, gf, tf, vec, rest)


def split3(value):
    first = value.astype(bf16)
    rest = value - first.astype(f32)
    second = rest.astype(bf16)
    third = (rest - second.astype(f32)).astype(bf16)
    return first, second, third


def attend_back_kernel(block, place, q_ref, k_ref, v_ref, o_ref, s_ref, do_ref, dq_ref, dk_ref, dv_ref,
                       q_s, k_s, v_s, do_s, acc):
    length = q_ref.shape[0]
    lane = lax.broadcasted_iota(jnp.int32, (length, 128), 1)
    row = lax.broadcasted_iota(jnp.int32, (block, block), 0)
    col = lax.broadcasted_iota(jnp.int32, (block, block), 1)
    q, k, v, do = q_ref[...], k_ref[...], v_ref[...], do_ref[...]
    zero = jnp.zeros_like(q)
    product = do.astype(f32) * o_ref[...].astype(f32)
    for head in range(2):
        low = head * HD
        other = (1 - head) * HD
        mine = (lane >= low) & (lane < low + HD)
        logs = -s_ref[:, low : low + 1]
        delta = -jnp.sum(jnp.where(mine, product, 0.0), axis=1, keepdims=True)
        one = jnp.where((lane >= other) & (lane < other + 3), jnp.ones_like(q), zero)
        q_aug, do_aug = jnp.where(mine, q, zero), jnp.where(mine, do, zero)
        for at, (part, piece) in enumerate(zip(split3(logs), split3(delta))):
            here = lane == other + at
            q_aug = jnp.where(here, part, q_aug)
            do_aug = jnp.where(here, piece, do_aug)
        q_s[head] = q_aug
        do_s[head] = do_aug
        k_s[head] = jnp.where(mine, k, one)
        v_s[head] = jnp.where(mine, v, one)
    for index in range(length // block):
        start, stop = index * block, (index + 1) * block
        kgrads, vgrads = [], []
        for head in range(2):
            kb, vb = k_s[head, start:stop, :], v_s[head, start:stop, :]
            scores = against(kb, q_s[head, start:, :])
            first = jnp.where(row <= col, scores[:, :block], -1e30)
            scores = jnp.concatenate([first, scores[:, block:]], axis=1) if stop < length else first
            probs = jnp.exp(scores)
            grads = (probs * against(vb, do_s[head, start:, :])).astype(bf16)
            vgrads.append(dense(probs.astype(bf16), do_ref[start:, :]))
            kgrads.append(dense(grads, q_ref[start:, :]))
            part = cross(grads, kb)
            if index == 0:
                acc[head] = part
            else:
                acc[head, start:, :] += part
        half = lane[:block] < HD
        dk_ref[start:stop, :] = jnp.where(half, kgrads[0], kgrads[1]).astype(bf16)
        dv_ref[start:stop, :] = jnp.where(half, vgrads[0], vgrads[1]).astype(bf16)
    dq_ref[...] = (jnp.where(lane < HD, acc[0], acc[1]) * 0.125).astype(bf16)


def attend_back(place, q, k, v, o, s, do, start, onto=(), waits=(), block=256):
    length, width = q.shape
    pair = pl.BlockSpec((length, 128), lambda i, place: (0, i + start))
    return call(
        functools.partial(attend_back_kernel, block),
        (width // 256,),
        [pair] * 6,
        [pair] * 3,
        [struct((length, width), bf16)] * 3,
        [pltpu.VMEM((2, length, 128), bf16)] * 4 + [pltpu.VMEM((2, length, 128), f32)],
        flops=10_000_000_000,
        moved=5_000_000,
        onto=onto,
        waits=waits,
    )(place, q, k, v, o, s, do)


def qkv_back_kernel(layer, many, place, x_ref, dm_ref, dq_ref, dk_ref, dv_ref, dza_ref, vec_ref, rest_ref, *refs):
    dx_ref, low_ref, buf, gate, sems = refs[many:]
    copies = fetches(place, refs[:many], buf, sems, ((0, 3 * UNIT),))[0]
    at_start(copies + [rest_copy(layer, rest_ref, gate, sems.at[1], UNIT, 2 * UNIT, UNIT)])
    dn = against(dza_ref[...], gate[...].reshape(PARTS * UNIT, gate.shape[2]))
    for at, ref in enumerate((dq_ref, dk_ref, dv_ref)):
        dn = dn + against(ref[...], unit(buf, at))
    hat, scale = normalise(x_ref[...].astype(f32))
    dx = dm_ref[...] + norm_back(dn, hat, scale, vec_ref[0:1, :])
    dx_ref[...] = dx
    low_ref[...] = dx.astype(bf16)


def qkv_back(place, layer, x, dm, dq, dk, dv, dza, vec, weights, rest, waits=()):
    length, width = x.shape
    row = rows_of(width)
    return call(
        functools.partial(qkv_back_kernel, layer, len(weights)),
        (length // ROWS,),
        [row] * 6 + [whole(16, width), ANY] + [ANY] * len(weights),
        [row, row],
        [struct((length, width), f32), struct((length, width), bf16)],
        [pltpu.VMEM((PARTS, 3 * UNIT, width), bf16), pltpu.VMEM((PARTS, UNIT, width), bf16), pltpu.SemaphoreType.DMA((2,))],
        flops=2 * length * width * 4 * width,
        moved=12_000_000,
        waits=waits,
    )(place, x, dm, dq, dk, dv, dza, vec, rest, *weights)


def put(place, outs, values, rows, first):
    keep, send = outs
    for y in range(2):
        low, high = (values[(y * 2 + c) * rows : (y * 2 + c + 1) * rows] for c in range(2))
        at = place[1] ^ y
        swap = place[2] == 1
        keep[at, 0, first : first + rows, :] = jnp.where(swap, high, low)
        send[at, 0, first : first + rows, :] = jnp.where(swap, low, high)


def put_plain(out, values, rows, first):
    for part in range(4):
        out[part, first : first + rows, :] = values[part * rows : (part + 1) * rows]


def grad_outs(rows, width):
    out = pl.BlockSpec((2, 1, rows, width), lambda i, place: (0, (i - place[0]) & 3, 0, 0))
    return [out, out], [struct((2, 4, rows, width), bf16)] * 2


def rest_grad_kernel(place, o_ref, n1_ref, n2_ref, h_ref, da_ref, dza_ref, dzf_ref, du_ref, df_ref, small_ref, out):
    put_plain(out, cross(o_ref[...], da_ref[...]).astype(bf16), UNIT, 0)
    put_plain(out, cross(n1_ref[...], dza_ref[...]).astype(bf16), UNIT, UNIT)
    put_plain(out, cross(n2_ref[...], dzf_ref[...]).astype(bf16), UNIT, 2 * UNIT)
    up = cross(n2_ref[...], du_ref[...]).astype(bf16)
    for at in range(4):
        put_plain(out, up[:, at * 512 : at * 512 + 512], UNIT, (3 + at) * UNIT)
    put_plain(out, cross(h_ref[...], df_ref[...]).astype(bf16), 4 * UNIT, 7 * UNIT)
    for part in range(4):
        out[part, REST:, :] = small_ref[...].astype(bf16)


def rest_grad(place, o, n1, n2, h, da, dza, dzf, du, df, small, waits=()):
    length, width = o.shape
    wide = h.shape[1]
    cols = pl.BlockSpec((length, width // 4), lambda i, place: (0, i))
    wides = pl.BlockSpec((length, wide // 4), lambda i, place: (0, i))
    full = whole(length, width)
    return call(
        rest_grad_kernel,
        (4,),
        [cols] * 3 + [wides] + [full] * 3 + [whole(length, wide), full, whole(16, width)],
        pl.BlockSpec((4, REST + 16, width), lambda i, place: (i, 0, 0)),
        struct((PARTS, REST + 16, width), bf16),
        flops=2 * length * width * (3 * width + 2 * wide),
        moved=26_000_000,
        waits=waits,
    )(place, o, n1, n2, h, da, dza, dzf, du, df, small)


def first_grad_kernel(place, *refs):
    outs = refs[-2:]
    for layer in range(len(refs) // 4):
        n1_ref = refs[4 * layer]
        for at, ref in enumerate(refs[4 * layer + 1 : 4 * layer + 4]):
            put(place, outs, cross(n1_ref[...], ref[...]).astype(bf16), UNIT, (3 * layer + at) * UNIT)


def first_grad(place, *layers, waits=()):
    length, width = layers[0][0].shape
    cols = pl.BlockSpec((length, width // 4), lambda i, place: (0, i))
    specs, shapes = grad_outs(3 * UNIT * len(layers), width)
    return call(
        first_grad_kernel,
        (4,),
        ([cols] + [whole(length, width)] * 3) * len(layers),
        specs,
        shapes,
        flops=2 * length * width * 3 * width * len(layers),
        moved=9_000_000 * len(layers),
        waits=waits,
    )(place, *(value for layer in layers for value in layer))


def moved_z(value, steps):
    count = lax.axis_size("dp")
    return lax.ppermute(value, "dp", [(d, (d + 4 * steps) % count) for d in range(count)])


def swapped(value, bit):
    return lax.ppermute(value, "dp", [(d, d ^ bit) for d in range(lax.axis_size("dp"))])


def crossed(value, sources=(0, 1)):
    return lax.ppermute(value, "section", [(s, 1 - s) for s in sources])


def along_z(block):
    return [block] + [moved_z(block, k) for k in (1, 2, 3)]


def across(own):
    beside = swapped(own, 2)
    return own, beside, swapped(own, 1), swapped(beside, 1)


def spread_whole(blocks):
    blocks = blocks.reshape(4, 2, 2, *blocks.shape[1:])
    blocks = jnp.stack([blocks[0], blocks[3], blocks[2], blocks[1]])
    return tuple(blocks[:, index & 1, index >> 1] for index in range(4))


def gather_whole(values, axis):
    values = lax.all_gather(values.astype(bf16), "dp", axis=axis, tiled=True)
    return lax.all_gather(values, "section", axis=0, tiled=True)


def split_rows(matrix, cols):
    rows, width = matrix.shape[0] // PARTS, matrix.shape[1] // cols
    return matrix.reshape(PARTS, rows, cols, width).transpose(0, 2, 1, 3).reshape(PARTS, cols * rows, width)


def merge_rows(blocks, cols):
    rows, width = blocks.shape[1] // cols, blocks.shape[2]
    return blocks.reshape(PARTS, cols, rows, width).transpose(0, 2, 1, 3).reshape(PARTS * rows, cols * width)


def weights_whole(w_qkv, w_out, w_gates, w_up, w_down, gains, biases):
    w_qkv, w_out, w_up, w_down = (gather_whole(w, 1) for w in (w_qkv, w_out, w_up, w_down))
    w_gates, gains, biases = (gather_whole(w, 2) for w in (w_gates, gains, biases))
    heads, tails = [], []
    for layer in range(2):
        lines = jnp.concatenate([gains[layer], biases[layer], jnp.zeros((12, gains.shape[2]), bf16)], axis=0)
        lines = jnp.concatenate([lines[None], jnp.zeros((PARTS - 1, *lines.shape), bf16)], axis=0)
        heads.append(spread_whole(jnp.concatenate([split_rows(w_qkv[layer], 3), lines], axis=1)))
        parts = [w_out[layer], w_gates[layer, 0], w_gates[layer, 1]]
        parts = [split_rows(part, 1) for part in parts] + [split_rows(w_up[layer], 4), split_rows(w_down[layer], 1)]
        tails.append(jnp.concatenate(parts, axis=1))
    return heads, tails


def joined(pieces):
    return jnp.stack(pieces).transpose(2, 1, 0, 3, 4).reshape(PARTS, *pieces[0].shape[2:])


def collect_whole(early, rest):
    early = joined(early)
    parts = [merge_rows(early, 3), merge_rows(rest[:, :UNIT], 1)]
    parts += [jnp.stack([merge_rows(rest[:, at * UNIT : (at + 1) * UNIT], 1) for at in (1, 2)])]
    parts += [merge_rows(rest[:, 3 * UNIT : 7 * UNIT], 4), merge_rows(rest[:, 7 * UNIT : REST], 1), rest[0, REST : REST + 2]]
    axes = (0, 0, 1, 0, 0, 1)
    parts = [lax.psum_scatter(part.astype(f32), "dp", scatter_dimension=axis, tiled=True) for part, axis in zip(parts, axes)]
    return [lax.psum(part, "section") for part in parts]


def fold_core(keep, got):
    away = (keep[1].astype(f32) + got[1].astype(f32)).astype(bf16)
    return away, keep[0].astype(f32) + got[0].astype(f32)


def fold_y(near, got):
    near = near + got.astype(f32)
    return near[0], [near[k].astype(bf16) for k in (1, 2, 3)]


def fold_z(total, gots):
    for got in gots:
        total = total + got.astype(f32)
    return total


def pack_kernel(place, qkv_ref, out_ref, gates_ref, up_ref, down_ref, lines_ref, head_ref, tail_ref):
    width = out_ref.shape[2]
    for at in range(3):
        head_ref[at * UNIT : (at + 1) * UNIT, :] = qkv_ref[0, :, at * width : (at + 1) * width].astype(bf16)
    head_ref[3 * UNIT :, :] = lines_ref[...].astype(bf16)
    tail_ref[:UNIT, :] = out_ref[0].astype(bf16)
    for at in range(2):
        tail_ref[(1 + at) * UNIT : (2 + at) * UNIT, :] = gates_ref[0, at].astype(bf16)
    for at in range(4):
        tail_ref[(3 + at) * UNIT : (4 + at) * UNIT, :] = up_ref[0, :, at * width : (at + 1) * width].astype(bf16)
    tail_ref[7 * UNIT :, :] = down_ref[0].astype(bf16)


def pack(place, index, w_qkv, w_out, w_gates, w_up, w_down, gains, biases):
    width = w_out.shape[2]
    lines = jnp.concatenate([gains[0], biases[0]], axis=0)
    mine = jnp.arange(width)[None, :] // UNIT == index
    lines = jnp.concatenate([jnp.where(mine, jnp.tile(lines, (1, PARTS)), 0.0), jnp.zeros((12, width), f32)], axis=0)
    arrays = (w_qkv, w_out, w_gates, w_up, w_down, lines)
    return call(
        pack_kernel,
        (1,),
        [whole(*array.shape) for array in arrays],
        [whole(FIRST, width), whole(REST, width)],
        [struct((FIRST, width), bf16), struct((REST, width), bf16)],
        moved=3_000_000,
    )(place, *arrays)


def after(value, *others):
    return lax.optimization_barrier((value, *others))[0]


def gain_grads(grads, w_qkv, w_gates, w_up, gains):
    d_qkv, _, d_gates, d_up = grads[:4]
    w_qkv, w_gates, w_up, gains = (w[0].astype(bf16).astype(f32) for w in (w_qkv, w_gates, w_up, gains))
    first = jnp.sum(w_qkv * d_qkv, axis=1) + jnp.sum(w_gates[0] * d_gates[0], axis=1)
    second = jnp.sum(w_up * d_up, axis=1) + jnp.sum(w_gates[1] * d_gates[1], axis=1)
    return jnp.stack([first, second]) / gains


def layer_forward(place, layer, x, head, rest):
    n1, q, k, v, vec = qkv_forward(place, x, head)
    o, s = attend_forward(place, q, k, v, 2, onto=attend_forward(place, q, k, v, 0))
    middle, n2, scale, ga, ta = gate_forward(place, layer, x, n1, o, vec, rest)
    y, h, slope, gf, tf = feed_forward(place, layer, middle, n2, vec, rest)
    return y, (x, n1, q, k, v, vec, o, s, n2, scale, ga, ta, h, slope, gf, tf)


def layer_backward(place, layer, grads, kept, head, rest):
    x, n1, q, k, v, vec, o, s, n2, scale, ga, ta, h, slope, gf, tf = kept
    dm, df, dzf, du, da, dza, do, small = feed_back(place, layer, grads, n2, scale, ga, ta, slope, gf, tf, vec, rest)
    later = rest_grad(place, o, n1, n2, h, da, dza, dzf, du, df, small)
    dqkv = attend_back(place, q, k, v, o, s, do, 2, onto=attend_back(place, q, k, v, o, s, do, 0))
    early = first_grad(place, (n1, *dqkv))
    dx, low = qkv_back(place, layer, x, dm, *dqkv, dza, vec, head, rest)
    return dx, low, collect_whole(early, later)


def per_device(tokens, cotangent, w_qkv, w_out, w_gates, w_up, w_down, norm_gains, gate_biases):
    section = lax.axis_index("section")
    index = lax.axis_index("dp")
    fast = lax.axis_size("dp") == PARTS
    first = section == 0
    masters = (w_qkv, w_out, w_gates, w_up, w_down, norm_gains, gate_biases)

    def pick(own, other):
        return jnp.where(first, own, other), jnp.where(first, other, own)

    x = jnp.where(first, tokens[0, 0], tokens[1, 0])
    seeds = [cotangent[0, m, 0] for m in range(2)]
    own_seed, other_seed = jnp.where(first, seeds[0], seeds[1]), jnp.where(first, seeds[1], seeds[0])
    if fast:
        y0, y1, theirs, dxs, lows, grads = run(x, own_seed, other_seed, masters, index, first, pick)
    else:
        place = jnp.zeros((3,), jnp.int32)
        heads, rest = weights_whole(*masters)
        y0, kept0 = layer_forward(place, 0, x, heads[0], rest[0])
        y1, kept1 = layer_forward(place, 1, y0, heads[1], rest[1])
        seeds = pick(own_seed, crossed(other_seed))
        dx1, low1, grads1 = layer_backward(place, 1, [seeds[1]], kept1, heads[1], rest[1])
        dx0, low0, grads0 = layer_backward(place, 0, [seeds[0], low1], kept0, heads[0], rest[0])
        dxs, lows = (dx0, dx1), (crossed(low0, (1,)), crossed(low1, (0,)))
        theirs = crossed(jnp.where(first, y1, y0))
        grads = [jnp.where(first, *pair) for pair in zip(grads0, grads1)]

    mine = jnp.where(first, y0, y1)
    block = jnp.stack([jnp.where(first, mine, theirs), jnp.where(first, theirs, mine)])[None, :, None]
    dx = jnp.where(first, *dxs)
    other = jnp.where(first, *lows).astype(f32)
    in_grads = jnp.stack([jnp.where(first, dx, other), jnp.where(first, other, dx)])[None, :, None]
    grads.insert(5, gain_grads(grads, w_qkv, w_gates, w_up, norm_gains))
    return (block, in_grads, *(grad[None] for grad in grads))


def run(x, own_seed, other_seed, masters, index, first, pick):
    width = x.shape[1]
    place = jnp.stack([index // 4, (index // 2) & 1, index & 1]).astype(jnp.int32)
    head, tail = pack(place, index, *masters)
    heads = pick(head, crossed(head))
    tails = pick(tail, crossed(after(tail, heads[0])))
    tail0 = lax.all_gather(tails[0], "dp", axis=0)

    def cores(z, y):
        return z, y, swapped(z, 1), swapped(y, 1)

    zh0 = jnp.stack(along_z(heads[0]))
    yh0 = swapped(zh0, 2)
    zh1 = along_z(after(heads[1], yh0))
    head0 = cores(zh0, yh0)
    n1, q, k, v, vec = qkv_forward(place, x, head0)
    zh1 = jnp.stack([after(part, n1) for part in zh1])
    yh1 = swapped(zh1, 2)
    o, s = attend_forward(place, q, k, v, 0, waits=(zh1,))
    o, s = attend_forward(place, q, k, v, 2, onto=(o, s))
    tail0 = after(tail0, o)
    tail1 = lax.all_gather(after(tails[1], tail0), "dp", axis=0)
    middle, n2, scale, ga, ta = gate_forward(place, 0, x, n1, o, vec, tail0)
    head1 = cores(after(zh1, n2), after(yh1, n2))
    y0, h, slope, gf, tf = feed_forward(place, 0, middle, n2, vec, tail0)
    other_seed = crossed(after(other_seed, n2))
    kept0 = (x, n1, q, k, v, vec, o, s, n2, scale, ga, ta, h, slope, gf, tf)

    n1, q, k, v, vec = qkv_forward(place, y0, head1)
    o, s = attend_forward(place, q, k, v, 0)
    o, s = attend_forward(place, q, k, v, 2, onto=(o, s))
    middle, n2, scale, ga, ta = gate_forward(place, 1, y0, n1, o, vec, tail1)
    y1, h, slope, gf, tf = feed_forward(place, 1, middle, n2, vec, tail1)
    theirs = crossed(jnp.where(first, y1, y0))

    seeds = pick(own_seed, after(other_seed, y1))
    dm1, df, dzf, du, da, dza1, do, small = feed_back(place, 1, [seeds[1]], n2, scale, ga, ta, slope, gf, tf, vec, tail1)
    rest1 = lax.psum_scatter(rest_grad(place, o, n1, n2, h, da, dza1, dzf, du, df, small), "dp", scatter_dimension=0)
    dqkv = attend_back(place, q, k, v, o, s, do, 0)
    dqkv = attend_back(place, q, k, v, o, s, do, 2, onto=dqkv)
    dx1, low1 = qkv_back(place, 1, y0, dm1, *dqkv, dza1, vec, head1, tail1, waits=(theirs,))
    early1 = (n1, *dqkv)
    other1 = crossed(low1, (0,))

    x, n1, q, k, v, vec, o, s, n2, scale, ga, ta, h, slope, gf, tf = kept0
    dm, df, dzf, du, da, dza, do, small = feed_back(
        place, 0, [seeds[0], low1], n2, scale, ga, ta, slope, gf, tf, vec, tail0
    )
    grad0 = rest_grad(place, o, n1, n2, h, da, dza, dzf, du, df, small, waits=(other1,))
    rest0 = lax.psum_scatter(grad0, "dp", scatter_dimension=0)
    dqkv = attend_back(place, q, k, v, o, s, do, 0)
    rest1 = after(rest1, dqkv[0])
    last1 = crossed(rest1, (0,))
    dqkv = attend_back(place, q, k, v, o, s, do, 2, onto=dqkv)
    keep, send = first_grad(place, (n1, *dqkv), early1, waits=(last1,))
    got = swapped(send, 1)
    dx0, low0 = qkv_back(place, 0, x, dm, *dqkv, dza, vec, head0, tail0, waits=(keep,))
    rest1 = rest1.astype(f32) + last1.astype(f32)
    away, near = fold_core(keep, after(got, low0))
    got = swapped(away, 2)
    other0 = crossed(after(low0, away), (1,))
    own, sends = fold_y(near, got)
    own = fold_z(own, [moved_z(part, at + 1) for at, part in enumerate(sends)])
    half = 3 * UNIT
    mine, theirs_early = jnp.where(first, own[:half], own[half:]), jnp.where(first, own[half:], own[:half])
    early = mine + crossed(theirs_early.astype(bf16)).astype(f32)
    rest0 = after(rest0, own)
    rest0 = rest0.astype(f32) + crossed(rest0, (1,)).astype(f32)
    later = jnp.where(first, rest0, rest1)
    grads = [
        jnp.concatenate([early[at * UNIT : (at + 1) * UNIT] for at in range(3)], axis=1),
        later[:UNIT],
        later[UNIT : 3 * UNIT].reshape(2, UNIT, width),
        jnp.concatenate([later[(3 + at) * UNIT : (4 + at) * UNIT] for at in range(4)], axis=1),
        later[7 * UNIT : REST],
        lax.dynamic_slice(later, (REST, index * UNIT), (2, UNIT)),
    ]
    return y0, y1, theirs, (dx0, dx1), (other0, other1), grads


def solution(mesh):
    placed = (
        P(None, "dp", None, None),
        P("section", None, "dp", None, None),
        P("section", "dp", None),
        P("section", "dp", None),
        P("section", None, "dp", None),
        P("section", "dp", None),
        P("section", "dp", None),
        P("section", None, "dp"),
        P("section", None, "dp"),
    )
    return jax.shard_map(
        per_device,
        mesh=mesh,
        in_specs=placed,
        out_specs=(P("section", None, "dp", None, None), P("section", None, "dp", None, None)) + placed[2:],
        check_vma=False,
    )
```

time: 533 us -> 440 us (0.83)
  starting transfers between devices: 107 us -> 40 us
  waiting for transfers between devices: 161 us -> 105 us
  Pallas kernels: 216 us -> 239 us
  between operations: 1.61 us -> 14.8 us
  other arithmetic: 29.5 us -> 23.4 us
    ppermute x24 -> x9, starting transfers between devices: 73.5 us -> 16.2 us  [moved_z(): lax.ppermute(value, 'dp', [(d, (d + 4 * steps) % count) for d in range(co...]
    ppermute x24 -> x9, waiting for transfers between devices: 68 us -> 25.2 us  [moved_z(): lax.ppermute(value, 'dp', [(d, (d + 4 * steps) % count) for d in range(co...]
    pallas_call x16 -> x22, Pallas kernels: 216 us -> 239 us  [run(): pl.pallas_call(body, grid_spec=pltpu.PrefetchScalarGridSpec(num_scalar_pr...]
    ppermute x10 -> x9, waiting for transfers between devices: 41.7 us -> 22 us  [crossed(): return lax.ppermute(value, 'section', [(s, 1 - s) for s in sources])]
    ppermute x20 -> x8, waiting for transfers between devices: 50.9 us -> 40 us  [swapped(): lax.ppermute(value, 'dp', [(d, d ^ bit) for d in range(lax.axis_size('dp'...]
    reduce_scatter x0 -> x2, waiting for transfers between devices: none -> 9.84 us  [the longest x1 9.82 us: run(): rest0 = lax.psum_scatter(grad0, 'dp', scatter_dimension=0)]
    ppermute x20 -> x8, starting transfers between devices: 11.7 us -> 3.03 us  [swapped(): lax.ppermute(value, 'dp', [(d, d ^ bit) for d in range(lax.axis_size('dp'...]
    all_gather x0 -> x2, waiting for transfers between devices: none -> 8.38 us  [the longest x1 5.83 us: run(): tail1 = lax.all_gather(after(tails[1], tail0), 'dp', axis=0)]
  transfers between devices with their start and end apart: 54 -> 30, of which waited for: 21 -> 15; matrix products, arithmetic and copies ran while one was open for 5% -> 3% of each run, Pallas kernels for 29% -> 48%
where the time goes in v2:
time: 440 us; the launch traced here: 432 us
  Pallas kernels  239 us (54%)
  waiting for transfers between devices  105 us (24%)
  starting transfers between devices  40 us (9%)
  other arithmetic  23.4 us (5%)
  between operations  14.8 us (3%)
  local copies, waits for them, and re-layouts  9.51 us (2%)
    pallas_call x22, Pallas kernels, run(): pl.pallas_call(body, grid_spec=pltpu.PrefetchScalarGridSpec(num_scalar_pr...  239 us
    ppermute x8, waiting for transfers between devices, swapped(): lax.ppermute(value, 'dp', [(d, d ^ bit) for d in range(lax.axis_size('dp'...  40 us
    ppermute x9, waiting for transfers between devices, moved_z(): lax.ppermute(value, 'dp', [(d, (d + 4 * steps) % count) for d in range(co...  25.2 us
    ppermute x9, waiting for transfers between devices, crossed(): return lax.ppermute(value, 'section', [(s, 1 - s) for s in sources])  22 us
    ppermute x9, starting transfers between devices, crossed(): return lax.ppermute(value, 'section', [(s, 1 - s) for s in sources])  20.5 us
    ppermute x9, starting transfers between devices, moved_z(): lax.ppermute(value, 'dp', [(d, (d + 4 * steps) % count) for d in range(co...  16.2 us
    reduce_scatter x1, waiting for transfers between devices, run(): rest0 = lax.psum_scatter(grad0, 'dp', scatter_dimension=0)  9.82 us
  transfers between devices with their start and end apart: 30, of which 15 were waited for; matrix products, arithmetic and copies ran while one was open for 3% of the time, Pallas kernels for 48%

profile of v2, /device:TPU:0, one launch (start us, length us, event | category | flops | bytes accessed | tf_op | source)
XLA Modules:
  0.0 431.9 jit_solution(4643094307898107384)
XLA Ops:
  21.0 8.1 %collective-permute-done.10 = bf16[352,512]{1,0:T(8,128)(2,1)S(1)} collective-permute-done((bf16[352,512]{1,0:T(8,128)(2,1)}, bf16[352,512]{1,0:T(8,128)(2,1)S(1)}, u32[]{:S(2)}, u32[]{:S(2)}) %collective-permute-start.10) | collective-permute-done | bytes 360480 | tf_op jit(solution)/shard_map/ppermute | solution.py:525
  43.4 13.3 %collective-permute-done.4.refs_3_.refs_10_ = bf16[4,112,512]{2,1,0:T(8,128)(2,1)S(1)} collective-permute-done((bf16[4,112,512]{2,1,0:T(8,128)(2,1)S(1)}, bf16[4,112,512]{2,1,0:T(8,128)(2,1)S(1)}, u32[]{:S(2)}, u32[]{:S(2)}) %collective-permute-start.4) | collective-permute-done | bytes 458784 | tf_op jit(solution)/shard_map/ppermute | solution.py:521
  76.4 9.2 %shard_map.162 = (bf16[1024,512]{1,0:T(8,128)(2,1)}, f32[1024,512]{1,0:T(8,128)}) custom-call(s32[3]{0:T(128)} %pad_add_fusion.refs_0_, bf16[1024,512]{1,0:T(8,128)(2,1)} %get-tuple-element.101.refs_1_, bf16[1024,512]{1,0:T(8,128)(2,1)} %get-tuple-element.102.refs_2_, bf16[1024,512]{1,0:T(8,128)(2,1)} %get-tuple-element.103.refs_3_, ...), custom_call_target="tpu_custom_call" | custom-call | flops 6000000000 | bytes 3000000 | tf_op jit(solution)/shard_map/pallas_call | solution.py:72
  85.6 9.4 %shard_map.163 = (bf16[1024,512]{1,0:T(8,128)(2,1)}, f32[1024,512]{1,0:T(8,128)}) custom-call(s32[3]{0:T(128)} %pad_add_fusion.refs_0_, bf16[1024,512]{1,0:T(8,128)(2,1)} %get-tuple-element.101.refs_1_, bf16[1024,512]{1,0:T(8,128)(2,1)} %get-tuple-element.102.refs_2_, ...), custom_call_target="tpu_custom_call", output_to_operand_aliasing={{0}: (4, {}), {1}: (5, {})} | custom-call | flops 6000000000 | bytes 3000000 | tf_op jit(solution)/shard_map/pallas_call | solution.py:72
  98.0 8.4 %shard_map.164 = (f32[1024,512]{1,0:T(8,128)}, bf16[1024,512]{1,0:T(8,128)(2,1)}, f32[1024,1]{1,0:T(8,128)}, bf16[1024,512]{1,0:T(8,128)(2,1)}, bf16[1024,512]{1,0:T(8,128)(2,1)}) custom-call(s32[3]{0:T(128)} %pad_add_fusion.refs_0_, bf16[1024,512]{1,0:T(8,128)(2,1)} %select_bitcast_fusion.3.refs_1_, bf16[1024,512]{1,0:T(8,128)(2,1)} %get-tuple-element.100.refs_2_.refs_1_, ...), custom_call_target="tpu_custom_call" | custom-call | flops 1073741824 | bytes 9000000 | tf_op jit(solution)/shard_map/pallas_call | solution.py:72
  113.3 15.1 %shard_map.165 = (bf16[1024,512]{1,0:T(8,128)(2,1)}, bf16[1024,2048]{1,0:T(8,128)(2,1)}, bf16[1024,2048]{1,0:T(8,128)(2,1)}, bf16[1024,512]{1,0:T(8,128)(2,1)}, bf16[1024,512]{1,0:T(8,128)(2,1)}) custom-call(s32[3]{0:T(128)} %pad_add_fusion.refs_0_, f32[1024,512]{1,0:T(8,128)} %get-tuple-element.116.refs_1_, ...), custom_call_target="tpu_custom_call" | custom-call | flops 4831838208 | bytes 20000000 | tf_op jit(solution)/shard_map/pallas_call | solution.py:72
  136.9 9.3 %shard_map.167 = (bf16[1024,512]{1,0:T(8,128)(2,1)}, f32[1024,512]{1,0:T(8,128)}) custom-call(s32[3]{0:T(128)} %pad_add_fusion.refs_0_, bf16[1024,512]{1,0:T(8,128)(2,1)} %get-tuple-element.122.refs_1_, bf16[1024,512]{1,0:T(8,128)(2,1)} %get-tuple-element.123.refs_2_, bf16[1024,512]{1,0:T(8,128)(2,1)} %get-tuple-element.124.refs_3_), custom_call_target="tpu_custom_call" | custom-call | flops 6000000000 | bytes 3000000 | tf_op jit(solution)/shard_map/pallas_call | solution.py:72
  146.2 9.3 %shard_map.168 = (bf16[1024,512]{1,0:T(8,128)(2,1)}, f32[1024,512]{1,0:T(8,128)}) custom-call(s32[3]{0:T(128)} %pad_add_fusion.refs_0_, bf16[1024,512]{1,0:T(8,128)(2,1)} %get-tuple-element.122.refs_1_, bf16[1024,512]{1,0:T(8,128)(2,1)} %get-tuple-element.123.refs_2_, ...), custom_call_target="tpu_custom_call", output_to_operand_aliasing={{0}: (4, {}), {1}: (5, {})} | custom-call | flops 6000000000 | bytes 3000000 | tf_op jit(solution)/shard_map/pallas_call | solution.py:72
  161.4 7.8 %shard_map.169 = (f32[1024,512]{1,0:T(8,128)}, bf16[1024,512]{1,0:T(8,128)(2,1)}, f32[1024,1]{1,0:T(8,128)}, bf16[1024,512]{1,0:T(8,128)(2,1)}, bf16[1024,512]{1,0:T(8,128)(2,1)}) custom-call(s32[3]{0:T(128)} %pad_add_fusion.refs_0_, bf16[1024,512]{1,0:T(8,128)(2,1)} %get-tuple-element.118.refs_1_, bf16[1024,512]{1,0:T(8,128)(2,1)} %get-tuple-element.121.refs_2_.refs_5_, ...), custom_call_target="tpu_custom_call" | custom-call | flops 1073741824 | bytes 9000000 | tf_op jit(solution)/shard_map/pallas_call | solution.py:72
  169.2 15.2 %shard_map.170 = (bf16[1024,512]{1,0:T(8,128)(2,1)}, bf16[1024,2048]{1,0:T(8,128)(2,1)}, bf16[1024,2048]{1,0:T(8,128)(2,1)}, bf16[1024,512]{1,0:T(8,128)(2,1)}, bf16[1024,512]{1,0:T(8,128)(2,1)}) custom-call(s32[3]{0:T(128)} %pad_add_fusion.refs_0_, f32[1024,512]{1,0:T(8,128)} %get-tuple-element.130.refs_1_, ...), custom_call_target="tpu_custom_call" | custom-call | flops 4831838208 | bytes 20000000 | tf_op jit(solution)/shard_map/pallas_call | solution.py:72
  187.2 16.5 %shard_map.171 = (f32[1024,512]{1,0:T(8,128)}, bf16[1024,512]{1,0:T(8,128)(2,1)}, bf16[1024,512]{1,0:T(8,128)(2,1)}, bf16[1024,2048]{1,0:T(8,128)(2,1)}, bf16[10...) custom-call(s32[3]{0:T(128)} %pad_add_fusion.refs_0_, ...), custom_call_target="tpu_custom_call" | custom-call | flops 5368709120 | bytes 24000000 | tf_op jit(solution)/shard_map/pallas_call | solution.py:72
  203.7 13.1 %shard_map.178 = bf16[16,368,512]{2,1,0:T(8,128)(2,1)} custom-call(s32[3]{0:T(128)} %pad_add_fusion.refs_0_, bf16[1024,512]{1,0:T(8,128)(2,1)} %get-tuple-element.127.refs_3_.refs_4_.refs_1_, bf16[1024,512]{1,0:T(8,128)(2,1)} %get-tuple-element.121.refs_2_.refs_5_, bf16[1024,512]{1,0:T(8,128)(2,1)} %get-tuple-element.131.refs_2_.refs_3_, ...), custom_call_target="tpu_custom_call" | custom-call | flops 5905580032 | bytes 26000000 | tf_op jit(solution)/shard_map/pallas_call | solution.py:72
  220.0 11.9 %shard_map.172 = (bf16[1024,512]{1,0:T(8,128)(2,1)}, bf16[1024,512]{1,0:T(8,128)(2,1)}, bf16[1024,512]{1,0:T(8,128)(2,1)}) custom-call(s32[3]{0:T(128)} %pad_add_fusion.refs_0_, bf16[1024,512]{1,0:T(8,128)(2,1)} %get-tuple-element.122.refs_1_, bf16[1024,512]{1,0:T(8,128)(2,1)} %get-tuple-element.123.refs_2_, bf16[1024,512]{1,0:T(8,128)(2,1)} %get-tuple-element.124.refs_3_, ...), custom_call_target="tpu_custom_call" | custom-call | flops 10000000000 | bytes 5000000 | tf_op jit(solution)/shard_map/pallas_call | solution.py:72
  231.9 12.0 %shard_map.173 = (bf16[1024,512]{1,0:T(8,128)(2,1)}, bf16[1024,512]{1,0:T(8,128)(2,1)}, bf16[1024,512]{1,0:T(8,128)(2,1)}) custom-call(s32[3]{0:T(128)} %pad_add_fusion.refs_0_, bf16[1024,512]{1,0:T(8,128)(2,1)} %get-tuple-element.122.refs_1_, ...), custom_call_target="tpu_custom_call", output_to_operand_aliasing={{0}: (7, {}), {1}: (8, {}), {2}: (9, {})} | custom-call | flops 10000000000 | bytes 5000000 | tf_op jit(solution)/shard_map/pallas_call | solution.py:72
  244.9 9.9 %shard_map.174 = (f32[1024,512]{1,0:T(8,128)}, bf16[1024,512]{1,0:T(8,128)(2,1)}) custom-call(s32[3]{0:T(128)} %pad_add_fusion.refs_0_, bf16[1024,512]{1,0:T(8,128)(2,1)} %get-tuple-element.118.refs_1_, f32[1024,512]{1,0:T(8,128)} %get-tuple-element.141.refs_2_, bf16[1024,512]{1,0:T(8,128)(2,1)} %get-tuple-element.147.refs_3_.refs_6_, ...), custom_call_target="tpu_custom_call" | custom-call | flops 2147483648 | bytes 12000000 | tf_op jit(solution)/shard_map/pallas_call | solution.py:72
  257.8 16.9 %shard_map.175 = (f32[1024,512]{1,0:T(8,128)}, bf16[1024,512]{1,0:T(8,128)(2,1)}, bf16[1024,512]{1,0:T(8,128)(2,1)}, bf16[1024,2048]{1,0:T(8,128)(2,1)}, bf16[10...) custom-call(s32[3]{0:T(128)} %pad_add_fusion.refs_0_, ...), custom_call_target="tpu_custom_call" | custom-call | flops 5368709120 | bytes 24000000 | tf_op jit(solution)/shard_map/pallas_call | solution.py:72
  280.9 13.4 %shard_map.181 = bf16[16,368,512]{2,1,0:T(8,128)(2,1)} custom-call(s32[3]{0:T(128)} %pad_add_fusion.refs_0_, bf16[1024,512]{1,0:T(8,128)(2,1)} %get-tuple-element.111.refs_3_.refs_4_.refs_1_, bf16[1024,512]{1,0:T(8,128)(2,1)} %get-tuple-element.100.refs_2_.refs_1_, bf16[1024,512]{1,0:T(8,128)(2,1)} %get-tuple-element.117.refs_2_.refs_3_, ...), custom_call_target="tpu_custom_call" | custom-call | flops 5905580032 | bytes 26000000 | tf_op jit(solution)/shard_map/pallas_call | solution.py:72
  294.4 12.0 %shard_map.176 = (bf16[1024,512]{1,0:T(8,128)(2,1)}, bf16[1024,512]{1,0:T(8,128)(2,1)}, bf16[1024,512]{1,0:T(8,128)(2,1)}) custom-call(s32[3]{0:T(128)} %pad_add_fusion.refs_0_, bf16[1024,512]{1,0:T(8,128)(2,1)} %get-tuple-element.101.refs_1_, bf16[1024,512]{1,0:T(8,128)(2,1)} %get-tuple-element.102.refs_2_, bf16[1024,512]{1,0:T(8,128)(2,1)} %get-tuple-element.103.refs_3_, ...), custom_call_target="tpu_custom_call" | custom-call | flops 10000000000 | bytes 5000000 | tf_op jit(solution)/shard_map/pallas_call | solution.py:72
  310.7 12.3 %shard_map.177 = (bf16[1024,512]{1,0:T(8,128)(2,1)}, bf16[1024,512]{1,0:T(8,128)(2,1)}, bf16[1024,512]{1,0:T(8,128)(2,1)}) custom-call(s32[3]{0:T(128)} %pad_add_fusion.refs_0_, bf16[1024,512]{1,0:T(8,128)(2,1)} %get-tuple-element.101.refs_1_, ...), custom_call_target="tpu_custom_call", output_to_operand_aliasing={{0}: (7, {}), {1}: (8, {}), {2}: (9, {})} | custom-call | flops 10000000000 | bytes 5000000 | tf_op jit(solution)/shard_map/pallas_call | solution.py:72
  323.8 9.3 %shard_map.179 = (bf16[2,4,192,512]{3,2,1,0:T(8,128)(2,1)}, bf16[2,4,192,512]{3,2,1,0:T(8,128)(2,1)}) custom-call(s32[3]{0:T(128)} %pad_add_fusion.refs_0_, bf16[1024,512]{1,0:T(8,128)(2,1)} %get-tuple-element.100.refs_2_.refs_1_, bf16[1024,512]{1,0:T(8,128)(2,1)} %get-tuple-element.164.refs_2_.refs_3_, ...), custom_call_target="tpu_custom_call" | custom-call | flops 3221225472 | bytes 18000000 | tf_op jit(solution)/shard_map/pallas_call | solution.py:72
  333.0 10.3 %shard_map.180 = (f32[1024,512]{1,0:T(8,128)}, bf16[1024,512]{1,0:T(8,128)(2,1)}) custom-call(s32[3]{0:T(128)} %pad_add_fusion.refs_0_, bf16[1024,512]{1,0:T(8,128)(2,1)} %select_bitcast_fusion.3.refs_1_, f32[1024,512]{1,0:T(8,128)} %get-tuple-element.158.refs_2_, bf16[1024,512]{1,0:T(8,128)(2,1)} %get-tuple-element.164.refs_2_.refs_3_, ...), custom_call_target="tpu_custom_call" | custom-call | flops 2147483648 | bytes 12000000 | tf_op jit(solution)/shard_map/pallas_call | solution.py:72
  347.3 22.7 %collective-permute-done.20 = bf16[4,192,512]{2,1,0:T(8,128)(2,1)} collective-permute-done((bf16[4,192,512]{2,1,0:T(8,128)(2,1)}, bf16[4,192,512]{2,1,0:T(8,128)(2,1)}, u32[]{:S(2)}, u32[]{:S(2)}) %collective-permute-start.20) | collective-permute-done | bytes 786464 | tf_op jit(solution)/shard_map/ppermute | solution.py:521
  381.3 13.8 %collective-permute-done.22 = bf16[192,512]{1,0:T(8,128)(2,1)S(1)} collective-permute-done((bf16[192,512]{1,0:T(8,128)(2,1)S(1)}, bf16[192,512]{1,0:T(8,128)(2,1)S(1)}, u32[]{:S(2)}, u32[]{:S(2)}) %collective-permute-start.22) | collective-permute-done | bytes 196640 | tf_op jit(solution)/shard_map/ppermute | solution.py:517
  395.2 9.8 %reduce-scatter.5.cloned.1.call-done = bf16[1,368,512]{2,1,0:T(8,128)(2,1)} async-done(((bf16[16,368,512]{2,1,0:T(8,128)(2,1)}), bf16[1,368,512]{2,1,0:T(8,128)(2,1)}) %reduce-scatter.5.cloned.1.call-update) | async-done | bytes 376848 | tf_op jit(solution)/shard_map/reduce_scatter | solution.py:746
  (156 shorter events, 128.1 us)
Async XLA Ops:
  7.2 90.4 %all-gather.5.cloned.1.call-start = ((), (), s32[]{:S(2)}) async-start(), calls=%async_computation.4 | async-start | bytes 6127616 | tf_op jit(solution)/shard_map/all_gather | solution.py:703
  19.1 9.9 %collective-permute-start.10 = (bf16[352,512]{1,0:T(8,128)(2,1)}, bf16[352,512]{1,0:T(8,128)(2,1)S(1)}, u32[]{:S(2)}, u32[]{:S(2)}) collective-permute-start(bf16[352,512]{1,0:T(8,128)(2,1)} %get-tuple-element.114), channel_id=1, source_target_pairs={{0,16},{16,0},{1,17},{17,1},{2,18},{18,2},{3,19},{19,3},{4,20},{20... | collective-permute-start | bytes 1081352 | tf_op jit(solution)/shard_map/ppermute | solution.py:525
  30.9 130.4 %all-gather.7.cloned.1.call-start = ((), (), s32[]{:S(2)}) async-start(), calls=%async_computation.5 | async-start | bytes 6127616 | tf_op jit(solution)/shard_map/all_gather | solution.py:718
  41.8 14.8 %collective-permute-start.4 = (bf16[4,112,512]{2,1,0:T(8,128)(2,1)S(1)}, bf16[4,112,512]{2,1,0:T(8,128)(2,1)S(1)}, u32[]{:S(2)}, u32[]{:S(2)}) collective-permute-start(bf16[4,112,512]{2,1,0:T(8,128)(2,1)S(1)} %pad_maximum_fusion.refs_2_.refs_9_), channel_id=1, source_target_pairs={{0,2},{1,3},{2,0},{3,1},{4,6},{5,7},{6,4},{7,5},{8,10},{9,11},{10,... | collective-permute-start | bytes 1376264 | tf_op jit(solution)/shard_map/ppermute | solution.py:521
  43.4 19.8 %collective-permute-start.5 = (bf16[4,112,512]{2,1,0:T(8,128)(2,1)S(1)}, bf16[4,112,512]{2,1,0:T(8,128)(2,1)S(1)}, u32[]{:S(2)}, u32[]{:S(2)}) collective-permute-start(bf16[4,112,512]{2,1,0:T(8,128)(2,1)S(1)} %pad_maximum_fusion.refs_2_.refs_9_), channel_id=1, source_target_pairs={{0,1},{1,0},{2,3},{3,2},{4,5},{5,4},{6,7},{7,6},{8,9},{9,8},{10,11... | collective-permute-start | bytes 1376264 | tf_op jit(solution)/shard_map/ppermute | solution.py:521
  57.8 14.3 %collective-permute-start.7 = (bf16[112,512]{1,0:T(8,128)(2,1)S(1)}, bf16[112,512]{1,0:T(8,128)(2,1)S(1)}, u32[]{:S(2)}, u32[]{:S(2)}) collective-permute-start(bf16[112,512]{1,0:T(8,128)(2,1)S(1)} %get-tuple-element.105), channel_id=1, source_target_pairs={{0,4},{1,5},{2,6},{3,7},{4,8},{5,9},{6,10},{7,11},{8,12},{9,13},{1... | collective-permute-start | bytes 344072 | tf_op jit(solution)/shard_map/ppermute | solution.py:517
  59.3 16.3 %collective-permute-start.8 = (bf16[112,512]{1,0:T(8,128)(2,1)S(1)}, bf16[112,512]{1,0:T(8,128)(2,1)S(1)}, u32[]{:S(2)}, u32[]{:S(2)}) collective-permute-start(bf16[112,512]{1,0:T(8,128)(2,1)S(1)} %get-tuple-element.105), channel_id=1, source_target_pairs={{0,8},{1,9},{2,10},{3,11},{4,12},{5,13},{6,14},{7,15},{8,0},{9,1},... | collective-permute-start | bytes 344072 | tf_op jit(solution)/shard_map/ppermute | solution.py:517
  60.2 15.3 %collective-permute-start.9 = (bf16[112,512]{1,0:T(8,128)(2,1)S(1)}, bf16[112,512]{1,0:T(8,128)(2,1)S(1)}, u32[]{:S(2)}, u32[]{:S(2)}) collective-permute-start(bf16[112,512]{1,0:T(8,128)(2,1)S(1)} %get-tuple-element.105), channel_id=1, source_target_pairs={{0,12},{1,13},{2,14},{3,15},{4,0},{5,1},{6,2},{7,3},{8,4},{9,5},{1... | collective-permute-start | bytes 344072 | tf_op jit(solution)/shard_map/ppermute | solution.py:517
  97.6 208.8 %reduce-scatter.3.cloned.1.call-start = ((), (), s32[]{:S(2)}) async-start(), calls=%async_computation.2 | async-start | bytes 6406144 | tf_op jit(solution)/shard_map/reduce_scatter | solution.py:734
  97.6 12.7 %collective-permute-start.11 = (bf16[4,112,512]{2,1,0:T(8,128)(2,1)S(1)}, bf16[4,112,512]{2,1,0:T(8,128)(2,1)S(1)}, u32[]{:S(2)}, u32[]{:S(2)}) collective-permute-start(bf16[4,112,512]{2,1,0:T(8,128)(2,1)S(1)} %copy-done.13), channel_id=1, source_target_pairs={{0,2},{1,3},{2,0},{3,1},{4,6},{5,7},{6,4},{7,5},{8,10},{9,11},{10,... | collective-permute-start | bytes 1376264 | tf_op jit(solution)/shard_map/ppermute | solution.py:521
  110.4 18.1 %collective-permute-start.13 = (bf16[4,112,512]{2,1,0:T(8,128)(2,1)S(1)}, bf16[4,112,512]{2,1,0:T(8,128)(2,1)S(1)}, u32[]{:S(2)}, u32[]{:S(2)}) collective-permute-start(bf16[4,112,512]{2,1,0:T(8,128)(2,1)S(1)} %collective-permute-done.11.refs_3_.refs_10_), channel_id=1, source_target_pairs={{0,1},{1,0},{2,3},{3,2},{4,5},{5,4},{6,7},{7,6},{8,9},{9,8},{10,11... | collective-permute-start | bytes 1376264 | tf_op jit(solution)/shard_map/ppermute | solution.py:521
  110.4 18.1 %collective-permute-start.12 = (bf16[4,112,512]{2,1,0:T(8,128)(2,1)S(1)}, bf16[4,112,512]{2,1,0:T(8,128)(2,1)S(1)}, u32[]{:S(2)}, u32[]{:S(2)}) collective-permute-start(bf16[4,112,512]{2,1,0:T(8,128)(2,1)S(1)} %copy-done.13), channel_id=1, source_target_pairs={{0,1},{1,0},{2,3},{3,2},{4,5},{5,4},{6,7},{7,6},{8,9},{9,8},{10,11... | collective-permute-start | bytes 1376264 | tf_op jit(solution)/shard_map/ppermute | solution.py:521
  112.0 72.4 %collective-permute-start.15 = (bf16[1024,512]{1,0:T(8,128)(2,1)}, bf16[1024,512]{1,0:T(8,128)(2,1)}, u32[]{:S(2)}, u32[]{:S(2)}) collective-permute-start(bf16[1024,512]{1,0:T(8,128)(2,1)} %select_bitcast_fusion), channel_id=1, source_target_pairs={{0,16},{16,0},{1,17},{17,1},{2,18},{18,2},{3,19},{19,3},{4,20},{20... | collective-permute-start | bytes 3145736 | tf_op jit(solution)/shard_map/ppermute | solution.py:525
  216.8 188.2 %reduce-scatter.5.cloned.1.call-start = ((), (), s32[]{:S(2)}) async-start(), calls=%async_computation.3 | async-start | bytes 6406144 | tf_op jit(solution)/shard_map/reduce_scatter | solution.py:746
  218.5 25.4 %collective-permute-start.14 = (bf16[1024,512]{1,0:T(8,128)(2,1)S(1)}, bf16[1024,512]{1,0:T(8,128)(2,1)S(1)}, u32[]{:S(2)}, u32[]{:S(2)}) collective-permute-start(bf16[1024,512]{1,0:T(8,128)(2,1)S(1)} %broadcast_select_fusion.3), channel_id=1, source_target_pairs={{0,16},{16,0},{1,17},{17,1},{2,18},{18,2},{3,19},{19,3},{4,20},{20... | collective-permute-start | bytes 3145736 | tf_op jit(solution)/shard_map/ppermute | solution.py:525
  254.8 25.2 %collective-permute-start.19 = (bf16[1024,512]{1,0:T(8,128)(2,1)}, bf16[1024,512]{1,0:T(8,128)(2,1)S(1)}, u32[]{:S(2)}, u32[]{:S(2)}) collective-permute-start(bf16[1024,512]{1,0:T(8,128)(2,1)} %get-tuple-element.151.refs_2_), channel_id=1, source_target_pairs={{0,16},{1,17},{2,18},{3,19},{4,20},{5,21},{6,22},{7,23},{8,24},{9,... | collective-permute-start | bytes 3145736 | tf_op jit(solution)/shard_map/ppermute | solution.py:525
  306.4 16.6 %collective-permute-start.16 = (bf16[368,512]{1,0:T(8,128)(2,1)}, bf16[368,512]{1,0:T(8,128)(2,1)S(1)}, u32[]{:S(2)}, u32[]{:S(2)}) collective-permute-start(bf16[368,512]{1,0:T(8,128)(2,1)} %bitcast.98), channel_id=1, source_target_pairs={{0,16},{1,17},{2,18},{3,19},{4,20},{5,21},{6,22},{7,23},{8,24},{9,... | collective-permute-start | bytes 1130504 | tf_op jit(solution)/shard_map/ppermute | solution.py:525
  333.0 10.3 %collective-permute-start.17 = (bf16[2,4,192,512]{3,2,1,0:T(8,128)(2,1)}, bf16[2,4,192,512]{3,2,1,0:T(8,128)(2,1)S(1)}, u32[]{:S(2)}, u32[]{:S(2)}) collective-permute-start(bf16[2,4,192,512]{3,2,1,0:T(8,128)(2,1)} %get-tuple-element.179), channel_id=1, source_target_pairs={{0,1},{1,0},{2,3},{3,2},{4,5},{5,4},{6,7},{7,6},{8,9},{9,8},{10,11... | collective-permute-start | bytes 4718600 | tf_op jit(solution)/shard_map/ppermute | solution.py:521
  344.4 25.6 %collective-permute-start.20 = (bf16[4,192,512]{2,1,0:T(8,128)(2,1)}, bf16[4,192,512]{2,1,0:T(8,128)(2,1)}, u32[]{:S(2)}, u32[]{:S(2)}) collective-permute-start(bf16[4,192,512]{2,1,0:T(8,128)(2,1)} %fusion.2), channel_id=1, source_target_pairs={{0,2},{1,3},{2,0},{3,1},{4,6},{5,7},{6,4},{7,5},{8,10},{9,11},{10,... | collective-permute-start | bytes 2359304 | tf_op jit(solution)/shard_map/ppermute | solution.py:521
  345.7 63.4 %collective-permute-start.18 = (bf16[1024,512]{1,0:T(8,128)(2,1)}, bf16[1024,512]{1,0:T(8,128)(2,1)}, u32[]{:S(2)}, u32[]{:S(2)}) collective-permute-start(bf16[1024,512]{1,0:T(8,128)(2,1)} %get-tuple-element.181), channel_id=1, source_target_pairs={{16,0},{17,1},{18,2},{19,3},{20,4},{21,5},{22,6},{23,7},{24,8},{25... | collective-permute-start | bytes 3145736 | tf_op jit(solution)/shard_map/ppermute | solution.py:525
  373.1 22.0 %collective-permute-start.22 = (bf16[192,512]{1,0:T(8,128)(2,1)S(1)}, bf16[192,512]{1,0:T(8,128)(2,1)S(1)}, u32[]{:S(2)}, u32[]{:S(2)}) collective-permute-start(bf16[192,512]{1,0:T(8,128)(2,1)S(1)} %get-tuple-element.210), channel_id=1, source_target_pairs={{0,8},{1,9},{2,10},{3,11},{4,12},{5,13},{6,14},{7,15},{8,0},{9,1},... | collective-permute-start | bytes 589832 | tf_op jit(solution)/shard_map/ppermute | solution.py:517
  375.5 19.6 %collective-permute-start.23 = (bf16[192,512]{1,0:T(8,128)(2,1)S(1)}, bf16[192,512]{1,0:T(8,128)(2,1)S(1)}, u32[]{:S(2)}, u32[]{:S(2)}) collective-permute-start(bf16[192,512]{1,0:T(8,128)(2,1)S(1)} %get-tuple-element.209), channel_id=1, source_target_pairs={{0,12},{1,13},{2,14},{3,15},{4,0},{5,1},{6,2},{7,3},{8,4},{9,5},{1... | collective-permute-start | bytes 589832 | tf_op jit(solution)/shard_map/ppermute | solution.py:517
  405.1 15.4 %collective-permute-start.25 = (bf16[368,512]{1,0:T(8,128)(2,1)}, bf16[368,512]{1,0:T(8,128)(2,1)S(1)}, u32[]{:S(2)}, u32[]{:S(2)}) collective-permute-start(bf16[368,512]{1,0:T(8,128)(2,1)} %bitcast.100), channel_id=1, source_target_pairs={{16,0},{17,1},{18,2},{19,3},{20,4},{21,5},{22,6},{23,7},{24,8},{25... | collective-permute-start | bytes 1130504 | tf_op jit(solution)/shard_map/ppermute | solution.py:525
  406.4 13.1 %collective-permute-start.24 = (bf16[96,512]{1,0:T(8,128)(2,1)S(1)}, bf16[96,512]{1,0:T(8,128)(2,1)S(1)}, u32[]{:S(2)}, u32[]{:S(2)}) collective-permute-start(bf16[96,512]{1,0:T(8,128)(2,1)S(1)} %select_convert_fusion), channel_id=1, source_target_pairs={{0,16},{16,0},{1,17},{17,1},{2,18},{18,2},{3,19},{19,3},{4,20},{20... | collective-permute-start | bytes 294920 | tf_op jit(solution)/shard_map/ppermute | solution.py:525
  (35 other events, 387.6 us)
Sparse Core Ops, SparseCore 0:
  31.1 66.4 all-gather.4
  99.8 61.4 all-gather.6
  217.0 84.3 reduce-scatter.2
  305.7 99.3 reduce-scatter.4

commit v3 on v2

--- a/solution.py
+++ b/solution.py
@@ -109,7 +109,7 @@
     return ref[at * 4 : at * 4 + 4, start * UNIT : (start + 4) * UNIT, :].reshape(16 * UNIT, ref.shape[2])
 
 
-def rest_copy(layer, source, target, sem, start, stop, base):
+def rest_copy(source, target, sem, start, stop, base):
     cut, goal = pl.ds(start, stop - start), pl.ds(start - base, stop - start)
     return pltpu.make_async_copy(source.at[:, cut], target.at[:, goal], sem)
 
@@ -199,141 +199,245 @@
     )(place, q, k, v)
 
 
-def gate_kernel(layer, place, x_ref, n1_ref, o_ref, vec_ref, rest_ref,
-                middle_ref, n2_ref, scale_ref, ga_ref, ta_ref, buf, sems):
-    at_start([rest_copy(layer, rest_ref, buf, sems.at[0], 0, 2 * UNIT, 0)])
-
-    branch = dense(o_ref[...], unit(buf, 0))
-    opening = jax.nn.sigmoid(dense(n1_ref[...], unit(buf, 1)) + vec_ref[2:3, :])
+def gelu(u):
+    square = u * u
+    inner = jnp.tanh(u * (root_term + (root_term * cube_term) * square))
+    half = 0.5 + 0.5 * inner
+    slope = half + (0.5 * root_term) * u * (1.0 - inner * inner) * (1.0 + (3.0 * cube_term) * square)
+    return u * half, slope
+
+
+def gated_rows(x, n1, o, vec, buf):
+    branch = dense(o, unit(buf, 0))
+    opening = jax.nn.sigmoid(dense(n1, unit(buf, 1)) + vec[2:3, :])
     gated = opening * branch
-    middle = x_ref[...].astype(f32) + gated
-    middle_ref[...] = middle
-    ga_ref[...] = opening.astype(bf16)
-    ta_ref[...] = (gated * (1.0 - opening)).astype(bf16)
+    middle = x.astype(f32) + gated
     hat, scale = normalise(middle)
-    n2_ref[...] = (hat * vec_ref[1:2, :]).astype(bf16)
-    scale_ref[...] = scale
-
-
-def gate_forward(place, layer, x, n1, o, vec, rest, waits=()):
-    length, width = x.shape
-    row, half = rows_of(width), struct((length, width), bf16)
-    return call(
-        functools.partial(gate_kernel, layer),
-        (length // ROWS,),
-        [row, row, row, whole(16, width), ANY],
-        [row, row, rows_of(1), row, row],
-        [struct((length, width), f32), half, struct((length, 1), f32), half, half],
-        [pltpu.VMEM((PARTS, 2 * UNIT, width), bf16), pltpu.SemaphoreType.DMA((1,))],
-        flops=2 * length * width * 2 * width,
-        moved=9_000_000,
-        waits=waits,
-    )(place, x, n1, o, vec, rest)
-
-
-def feed_kernel(layer, place, middle_ref, n2_ref, vec_ref, rest_ref, y_ref, h_ref, slope_ref, gf_ref, tf_ref, buf, sems):
-    at_start([rest_copy(layer, rest_ref, buf, sems.at[0], 2 * UNIT, REST, 2 * UNIT)])
-
-    n2 = n2_ref[...]
+    n2 = (hat * vec[1:2, :]).astype(bf16)
+    return middle, n2, hat, scale, opening, gated * (1.0 - opening)
+
+
+def feed_rows(middle, n2, vec, buf, h_ref, slope_ref, at_rows):
     feed = None
     for at in range(4):
         cut = slice(at * 512, at * 512 + 512)
-        u = dense(n2, unit(buf, 1 + at))
-        square = u * u
-        inner = jnp.tanh(u * (root_term + (root_term * cube_term) * square))
-        half = 0.5 + 0.5 * inner
-        active = (u * half).astype(bf16)
-        h_ref[:, cut] = active
-        slope = half + u * (0.5 - 0.5 * inner * inner) * (root_term + (3.0 * root_term * cube_term) * square)
+        active, slope = gelu(dense(n2, unit(buf, 3 + at)))
+        active = active.astype(bf16)
+        h_ref[at_rows, cut] = active
         slope_ref[:, cut] = slope.astype(bf16)
-        part = dense(active, down_part(buf, at, 5))
+        part = dense(active, down_part(buf, at))
         feed = part if feed is None else feed + part
-    closing = jax.nn.sigmoid(dense(n2, unit(buf, 0)) + vec_ref[3:4, :])
+    closing = jax.nn.sigmoid(dense(n2, unit(buf, 2)) + vec[3:4, :])
     gated = closing * feed
-    gf_ref[...] = closing.astype(bf16)
-    tf_ref[...] = (gated * (1.0 - closing)).astype(bf16)
-    y_ref[...] = (middle_ref[...] + gated).astype(bf16)
-
-
-def feed_forward(place, layer, middle, n2, vec, rest, waits=()):
-    length, width = middle.shape
+    return middle + gated, closing, gated * (1.0 - closing)
+
+
+def feed_kernel(place, x_ref, n1_ref, o_ref, vec_ref, rest_ref,
+                y_ref, n2_ref, scale_ref, ga_ref, ta_ref, h_ref, slope_ref, gf_ref, tf_ref, buf, sems):
+    at_start([rest_copy(rest_ref, buf, sems.at[0], 0, REST, 0)])
+    vec = vec_ref[...]
+    middle, n2, _, scale, ga, ta = gated_rows(x_ref[...], n1_ref[...], o_ref[...], vec, buf)
+    ga_ref[...] = ga.astype(bf16)
+    ta_ref[...] = ta.astype(bf16)
+    n2_ref[...] = n2
+    scale_ref[...] = jnp.broadcast_to(scale, scale_ref.shape)
+    y, gf, tf = feed_rows(middle, n2, vec, buf, h_ref, slope_ref, slice(None))
+    gf_ref[...] = gf.astype(bf16)
+    tf_ref[...] = tf.astype(bf16)
+    y_ref[...] = y.astype(bf16)
+
+
+def feed_forward(place, x, n1, o, vec, rest, waits=()):
+    length, width = x.shape
     wide = 4 * width
     row, half = rows_of(width), struct((length, width), bf16)
     big, bigs = rows_of(wide), struct((length, wide), bf16)
     return call(
-        functools.partial(feed_kernel, layer),
+        feed_kernel,
         (length // ROWS,),
-        [row, row, whole(16, width), ANY],
-        [row, big, big, row, row],
-        [half, bigs, bigs, half, half],
-        [pltpu.VMEM((PARTS, REST - 2 * UNIT, width), bf16), pltpu.SemaphoreType.DMA((1,))],
-        flops=2 * length * width * (width + 2 * wide),
-        moved=20_000_000,
+        [row, row, row, whole(16, width), ANY],
+        [row, row, rows_of(128), row, row, big, big, row, row],
+        [half, half, struct((length, 128), f32), half, half, bigs, bigs, half, half],
+        [pltpu.VMEM((PARTS, REST, width), bf16), pltpu.SemaphoreType.DMA((1,))],
+        flops=2 * length * width * (3 * width + 2 * wide),
+        moved=24_000_000,
         waits=waits,
-    )(place, middle, n2, vec, rest)
-
-
-def feed_back_kernel(layer, extra, place, *refs):
-    at = 1 + extra
-    e_refs = refs[:at]
-    n2_ref, scale_ref, ga_ref, ta_ref, slope_ref, gf_ref, tf_ref, vec_ref, rest_ref = refs[at : at + 9]
-    dm_ref, df_ref, dzf_ref, du_ref, da_ref, dza_ref, do_ref, small_ref, buf, sems = refs[at + 9 :]
-    at_start([rest_copy(layer, rest_ref, buf, sems.at[0], 0, REST, 0)])
-    at_first = pl.program_id(0) == 0
-
-    e = e_refs[0][...].astype(f32)
-    for ref in e_refs[1:]:
-        e = e + ref[...].astype(f32)
-    df = (e * gf_ref[...].astype(f32)).astype(bf16)
-    dzf = (e * tf_ref[...].astype(f32)).astype(bf16)
-    df_ref[...] = df
-    dzf_ref[...] = dzf
+    )(place, x, n1, o, vec, rest)
+
+
+def back_rows(e, hat, scale, ga, ta, slope_ref, gf, tf, gain, buf, du_ref, at_rows):
+    df = (e * gf).astype(bf16)
+    dzf = (e * tf).astype(bf16)
     dn2 = against(dzf, unit(buf, 2))
     for at in range(4):
         cut = slice(at * 512, at * 512 + 512)
-        dh = against(df, down_part(buf, at))
-        du = (dh * slope_ref[:, cut].astype(f32)).astype(bf16)
-        du_ref[:, cut] = du
+        du = (against(df, down_part(buf, at)) * slope_ref[:, cut].astype(f32)).astype(bf16)
+        du_ref[at_rows, cut] = du
         dn2 = dn2 + against(du, unit(buf, 3 + at))
-    gain = vec_ref[1:2, :]
-    hat = n2_ref[...].astype(f32) * (1.0 / gain)
-    dm = e + norm_back(dn2, hat, scale_ref[...], gain)
-    dm_ref[...] = dm
-    da = (dm * ga_ref[...].astype(f32)).astype(bf16)
-    dza = (dm * ta_ref[...].astype(f32)).astype(bf16)
-    da_ref[...] = da
-    dza_ref[...] = dza
-    do_ref[...] = against(da, unit(buf, 0)).astype(bf16)
-    sums = jnp.concatenate(
-        [jnp.sum(part.astype(f32), axis=0, keepdims=True) for part in (dza, dzf)] + [jnp.zeros((14, e.shape[1]), f32)],
-        axis=0,
-    )
-
-    @pl.when(at_first)
+    dm = e + norm_back(dn2, hat, scale, gain)
+    da = (dm * ga).astype(bf16)
+    dza = (dm * ta).astype(bf16)
+    return dm, df, dzf, da, dza, against(da, unit(buf, 0)).astype(bf16)
+
+
+def put_lanes(swap, keep, send, values, rows, first):
+    for y in range(2):
+        low, high = (values[(y * 2 + c) * rows : (y * 2 + c + 1) * rows] for c in range(2))
+        keep[y, first : first + rows, :] = jnp.where(swap, high, low)
+        send[y, first : first + rows, :] = jnp.where(swap, low, high)
+
+
+def rest_grads(place, keep, send, o, n1, n2, h, da, dza, dzf, du_ref, df, sums):
+    put = functools.partial(put_lanes, place[2] == 1, keep, send)
+    put(cross(o, da).astype(bf16), UNIT, 0)
+    put(cross(n1, dza).astype(bf16), UNIT, UNIT)
+    put(cross(n2, dzf).astype(bf16), UNIT, 2 * UNIT)
+    for at in range(4):
+        put(cross(n2, du_ref[:, at * 512 : at * 512 + 512]).astype(bf16), UNIT, (3 + at) * UNIT)
+    put(cross(h, df).astype(bf16), 4 * UNIT, 7 * UNIT)
+    small = jnp.concatenate([sums, jnp.zeros((8, sums.shape[1]), f32)], axis=0).astype(bf16)
+    for ref in (keep, send):
+        for y in range(2):
+            ref[y, REST:, :] = small
+
+
+def keep_rows(at_rows, refs, values):
+    for ref, value in zip(refs, values):
+        ref[at_rows, :] = value
+
+
+def add_sums(sums, dza, dzf):
+    rows = [jnp.sum(part.astype(f32), axis=0, keepdims=True) for part in (dza, dzf)]
+    new = jnp.concatenate(rows + [jnp.zeros((6, dza.shape[1]), f32)], axis=0)
+    sums[...] = jnp.where(pl.program_id(0) == 0, new, sums[...] + new)
+
+
+def turn_kernel(count, place, x_ref, n1_ref, o_ref, e_ref, vec_ref, o_cols, n1_cols, rest_ref,
+                y_ref, dm_ref, dza_ref, do_ref, keep, send, buf, h, du, slope, n2, df, dzf, da, dza, sums, sems):
+    step = pl.program_id(0)
+    at_start([rest_copy(rest_ref, buf, sems.at[0], 0, REST, 0)])
+
+    @pl.when(step < count)
     def _():
-        small_ref[...] = sums
-
-    @pl.when(pl.program_id(0) > 0)
+        at_rows = pl.ds(pl.multiple_of(step * ROWS, ROWS), ROWS)
+        vec = vec_ref[...]
+        middle, low, hat, scale, ga, ta = gated_rows(x_ref[...], n1_ref[...], o_ref[...], vec, buf)
+        y, gf, tf = feed_rows(middle, low, vec, buf, h, slope, at_rows)
+        y_ref[...] = y.astype(bf16)
+        e = e_ref[...].astype(f32)
+        dm, *parts, grad_o = back_rows(e, hat, scale, ga, ta, slope, gf, tf, vec[1:2, :], buf, du, at_rows)
+        dm_ref[...] = dm
+        do_ref[...] = grad_o
+        keep_rows(at_rows, (n2, df, dzf, da, dza), (low, *parts))
+        dza_ref[...] = parts[3]
+        add_sums(sums, parts[3], parts[1])
+
+    @pl.when(step >= count)
     def _():
-        small_ref[...] += sums
-
-
-def feed_back(place, layer, es, n2, scale, ga, ta, slope, gf, tf, vec, rest, waits=()):
-    length, width = n2.shape
-    wide = 4 * width
-    row, half = rows_of(width), struct((length, width), bf16)
-    big, bigs = rows_of(wide), struct((length, wide), bf16)
+        at = step - count
+        narrow, wide = pl.ds(pl.multiple_of(at * 128, 128), 128), pl.ds(pl.multiple_of(at * 512, 512), 512)
+        lefts = (o_cols[...], n1_cols[...], n2[:, narrow], h[:, wide])
+        rest_grads(place, keep, send, *lefts, da[...], dza[...], dzf[...], du, df[...], sums[...])
+
+
+def late_specs(length, width, count):
+    row = pl.BlockSpec((ROWS, width), lambda i, place: (jnp.minimum(i, count - 1), 0))
+    cols = pl.BlockSpec((length, width // 4), lambda i, place: (0, jnp.maximum(i - count, 0)))
+    grad = pl.BlockSpec((2, REST + 16, width), lambda i, place: (jnp.maximum(i - count, 0), 0, 0))
+    return row, cols, grad
+
+
+def turn(place, x, n1, o, e, vec, rest, waits=()):
+    length, width = x.shape
+    wide, count = 4 * width, length // ROWS
+    row, cols, grad = late_specs(length, width, count)
+    half, tall = struct((length, width), bf16), pltpu.VMEM((length, width), bf16)
     return call(
-        functools.partial(feed_back_kernel, layer, len(es) - 1),
-        (length // ROWS,),
-        [row] * len(es) + [row, rows_of(1), row, row, big, row, row, whole(16, width), ANY],
-        [row, row, row, big, row, row, row, whole(16, width)],
-        [struct((length, width), f32), half, half, bigs, half, half, half, struct((16, width), f32)],
-        [pltpu.VMEM((PARTS, REST, width), bf16), pltpu.SemaphoreType.DMA((1,))],
-        flops=2 * length * width * (2 * width + 2 * wide),
+        functools.partial(turn_kernel, count),
+        (count + 4,),
+        [row] * 4 + [whole(16, width), cols, cols, ANY],
+        [row] * 4 + [grad] * 2,
+        [half, struct((length, width), f32), half, half] + [struct((PARTS // 2, REST + 16, width), bf16)] * 2,
+        [pltpu.VMEM((PARTS, REST, width), bf16)]
+        + [pltpu.VMEM((length, wide), bf16)] * 2
+        + [pltpu.VMEM((ROWS, wide), bf16)]
+        + [tall] * 5
+        + [pltpu.VMEM((8, width), f32), pltpu.SemaphoreType.DMA((1,))],
+        flops=6 * length * width * (3 * width + 2 * wide),
         moved=24_000_000,
         waits=waits,
-    )(place, *es, n2, scale, ga, ta, slope, gf, tf, vec, rest)
+    )(place, x, n1, o, e, vec, o, n1, rest)
+
+
+def dx_rows(x, dm, dqkv, dza, gain, buf, gate):
+    width = x.shape[1]
+    dn = against(dza, gate[...].reshape(PARTS * UNIT, width))
+    for at, part in enumerate(dqkv):
+        dn = dn + against(part, unit(buf, at))
+    hat, scale = normalise(x.astype(f32))
+    return dm + norm_back(dn, hat, scale, gain)
+
+
+def joint_kernel(count, many, place, x_ref, dm1_ref, dq_ref, dk_ref, dv_ref, dza1_ref, e_ref,
+                 n2_ref, scale_ref, ga_ref, ta_ref, slope_ref, gf_ref, tf_ref, vec1_ref, vec_ref,
+                 o_cols, n1_cols, n2_cols, h_cols, rest1_ref, rest_ref, *refs):
+    dx_ref, low_ref, dm_ref, dza_ref, do_ref, keep, send, head, gate, buf, du, df, dzf, da, dza, sums, sems = refs[many:]
+    step = pl.program_id(0)
+    copies = fetches(place, refs[:many], head, sems, ((0, 3 * UNIT),))[0]
+    copies.append(rest_copy(rest1_ref, gate, sems.at[1], UNIT, 2 * UNIT, UNIT))
+    copies.append(rest_copy(rest_ref, buf, sems.at[2], 0, REST, 0))
+    at_start(copies)
+
+    @pl.when(step < count)
+    def _():
+        at_rows = pl.ds(pl.multiple_of(step * ROWS, ROWS), ROWS)
+        dqkv = (dq_ref[...], dk_ref[...], dv_ref[...])
+        dx = dx_rows(x_ref[...], dm1_ref[...], dqkv, dza1_ref[...], vec1_ref[0:1, :], head, gate)
+        dx_ref[...] = dx
+        low = dx.astype(bf16)
+        low_ref[...] = low
+        e = e_ref[...].astype(f32) + low.astype(f32)
+        gain = vec_ref[1:2, :]
+        hat = n2_ref[...].astype(f32) * (1.0 / gain)
+        ga, ta, gf, tf = (ref[...].astype(f32) for ref in (ga_ref, ta_ref, gf_ref, tf_ref))
+        dm, *parts, grad_o = back_rows(e, hat, scale_ref[:, 0:1], ga, ta, slope_ref, gf, tf, gain, buf, du, at_rows)
+        dm_ref[...] = dm
+        do_ref[...] = grad_o
+        keep_rows(at_rows, (df, dzf, da, dza), parts)
+        dza_ref[...] = parts[3]
+        add_sums(sums, parts[3], parts[1])
+
+    @pl.when(step >= count)
+    def _():
+        lefts = (o_cols[...], n1_cols[...], n2_cols[...], h_cols[...])
+        rest_grads(place, keep, send, *lefts, da[...], dza[...], dzf[...], du, df[...], sums[...])
+
+
+def joint_back(place, x, dm1, dqkv, dza1, vec1, head, rest1, e, kept, rest, waits=()):
+    n1, o, vec, n2, scale, ga, ta, h, slope, gf, tf = kept
+    length, width = x.shape
+    wide, count = 4 * width, length // ROWS
+    row, cols, grad = late_specs(length, width, count)
+    lanes = pl.BlockSpec((ROWS, 128), lambda i, place: (jnp.minimum(i, count - 1), 0))
+    big = pl.BlockSpec((ROWS, wide), lambda i, place: (jnp.minimum(i, count - 1), 0))
+    wides = pl.BlockSpec((length, wide // 4), lambda i, place: (0, jnp.maximum(i - count, 0)))
+    half, tall = struct((length, width), bf16), pltpu.VMEM((length, width), bf16)
+    floats = struct((length, width), f32)
+    return call(
+        functools.partial(joint_kernel, count, len(head)),
+        (count + 4,),
+        [row] * 8 + [lanes, row, row, big, row, row, whole(16, width), whole(16, width), cols, cols, cols, wides, ANY, ANY]
+        + [ANY] * len(head),
+        [row] * 5 + [grad] * 2,
+        [floats, half, floats, half, half] + [struct((PARTS // 2, REST + 16, width), bf16)] * 2,
+        [pltpu.VMEM((PARTS, 3 * UNIT, width), bf16), pltpu.VMEM((PARTS, UNIT, width), bf16), pltpu.VMEM((PARTS, REST, width), bf16)]
+        + [pltpu.VMEM((length, wide), bf16)]
+        + [tall] * 4
+        + [pltpu.VMEM((8, width), f32), pltpu.SemaphoreType.DMA((3,))],
+        flops=4 * length * width * (5 * width + 2 * wide),
+        moved=40_000_000,
+        waits=waits,
+    )(place, x, dm1, *dqkv, dza1, e, n2, scale, ga, ta, slope, gf, tf, vec1, vec, o, n1, n2, h, rest1, rest, *head)
 
 
 def split3(value):
@@ -392,41 +496,38 @@
     dq_ref[...] = (jnp.where(lane < HD, acc[0], acc[1]) * 0.125).astype(bf16)
 
 
-def attend_back(place, q, k, v, o, s, do, start, onto=(), waits=(), block=256):
+def attend_back(place, q, k, v, o, s, do, start, count=2, onto=(), waits=(), block=256):
     length, width = q.shape
     pair = pl.BlockSpec((length, 128), lambda i, place: (0, i + start))
     return call(
         functools.partial(attend_back_kernel, block),
-        (width // 256,),
+        (count,),
         [pair] * 6,
         [pair] * 3,
         [struct((length, width), bf16)] * 3,
         [pltpu.VMEM((2, length, 128), bf16)] * 4 + [pltpu.VMEM((2, length, 128), f32)],
-        flops=10_000_000_000,
+        flops=5_000_000_000 * count,
         moved=5_000_000,
         onto=onto,
         waits=waits,
     )(place, q, k, v, o, s, do)
 
 
-def qkv_back_kernel(layer, many, place, x_ref, dm_ref, dq_ref, dk_ref, dv_ref, dza_ref, vec_ref, rest_ref, *refs):
+def qkv_back_kernel(many, place, x_ref, dm_ref, dq_ref, dk_ref, dv_ref, dza_ref, vec_ref, rest_ref, *refs):
     dx_ref, low_ref, buf, gate, sems = refs[many:]
     copies = fetches(place, refs[:many], buf, sems, ((0, 3 * UNIT),))[0]
-    at_start(copies + [rest_copy(layer, rest_ref, gate, sems.at[1], UNIT, 2 * UNIT, UNIT)])
-    dn = against(dza_ref[...], gate[...].reshape(PARTS * UNIT, gate.shape[2]))
-    for at, ref in enumerate((dq_ref, dk_ref, dv_ref)):
-        dn = dn + against(ref[...], unit(buf, at))
-    hat, scale = normalise(x_ref[...].astype(f32))
-    dx = dm_ref[...] + norm_back(dn, hat, scale, vec_ref[0:1, :])
+    at_start(copies + [rest_copy(rest_ref, gate, sems.at[1], UNIT, 2 * UNIT, UNIT)])
+    dqkv = (dq_ref[...], dk_ref[...], dv_ref[...])
+    dx = dx_rows(x_ref[...], dm_ref[...], dqkv, dza_ref[...], vec_ref[0:1, :], buf, gate)
     dx_ref[...] = dx
     low_ref[...] = dx.astype(bf16)
 
 
-def qkv_back(place, layer, x, dm, dq, dk, dv, dza, vec, weights, rest, waits=()):
+def qkv_back(place, x, dm, dq, dk, dv, dza, vec, weights, rest, waits=()):
     length, width = x.shape
     row = rows_of(width)
     return call(
-        functools.partial(qkv_back_kernel, layer, len(weights)),
+        functools.partial(qkv_back_kernel, len(weights)),
         (length // ROWS,),
         [row] * 6 + [whole(16, width), ANY] + [ANY] * len(weights),
         [row, row],
@@ -448,44 +549,9 @@
         send[at, 0, first : first + rows, :] = jnp.where(swap, low, high)
 
 
-def put_plain(out, values, rows, first):
-    for part in range(4):
-        out[part, first : first + rows, :] = values[part * rows : (part + 1) * rows]
-
-
 def grad_outs(rows, width):
     out = pl.BlockSpec((2, 1, rows, width), lambda i, place: (0, (i - place[0]) & 3, 0, 0))
     return [out, out], [struct((2, 4, rows, width), bf16)] * 2
-
-
-def rest_grad_kernel(place, o_ref, n1_ref, n2_ref, h_ref, da_ref, dza_ref, dzf_ref, du_ref, df_ref, small_ref, out):
-    put_plain(out, cross(o_ref[...], da_ref[...]).astype(bf16), UNIT, 0)
-    put_plain(out, cross(n1_ref[...], dza_ref[...]).astype(bf16), UNIT, UNIT)
-    put_plain(out, cross(n2_ref[...], dzf_ref[...]).astype(bf16), UNIT, 2 * UNIT)
-    up = cross(n2_ref[...], du_ref[...]).astype(bf16)
-    for at in range(4):
-        put_plain(out, up[:, at * 512 : at * 512 + 512], UNIT, (3 + at) * UNIT)
-    put_plain(out, cross(h_ref[...], df_ref[...]).astype(bf16), 4 * UNIT, 7 * UNIT)
-    for part in range(4):
-        out[part, REST:, :] = small_ref[...].astype(bf16)
-
-
-def rest_grad(place, o, n1, n2, h, da, dza, dzf, du, df, small, waits=()):
-    length, width = o.shape
-    wide = h.shape[1]
-    cols = pl.BlockSpec((length, width // 4), lambda i, place: (0, i))
-    wides = pl.BlockSpec((length, wide // 4), lambda i, place: (0, i))
-    full = whole(length, width)
-    return call(
-        rest_grad_kernel,
-        (4,),
-        [cols] * 3 + [wides] + [full] * 3 + [whole(length, wide), full, whole(16, width)],
-        pl.BlockSpec((4, REST + 16, width), lambda i, place: (i, 0, 0)),
-        struct((PARTS, REST + 16, width), bf16),
-        flops=2 * length * width * (3 * width + 2 * wide),
-        moved=26_000_000,
-        waits=waits,
-    )(place, o, n1, n2, h, da, dza, dzf, du, df, small)
 
 
 def first_grad_kernel(place, *refs):
@@ -574,7 +640,7 @@
 
 
 def collect_whole(early, rest):
-    early = joined(early)
+    early, rest = joined(early), jnp.stack(rest, axis=1).reshape(PARTS, *rest[0].shape[1:])
     parts = [merge_rows(early, 3), merge_rows(rest[:, :UNIT], 1)]
     parts += [jnp.stack([merge_rows(rest[:, at * UNIT : (at + 1) * UNIT], 1) for at in (1, 2)])]
     parts += [merge_rows(rest[:, 3 * UNIT : 7 * UNIT], 4), merge_rows(rest[:, 7 * UNIT : REST], 1), rest[0, REST : REST + 2]]
@@ -586,6 +652,12 @@
 def fold_core(keep, got):
     away = (keep[1].astype(f32) + got[1].astype(f32)).astype(bf16)
     return away, keep[0].astype(f32) + got[0].astype(f32)
+
+
+def scattered(keep, got):
+    lanes = [[d for d in range(PARTS) if d % 2 == c] for c in range(2)]
+    both = (keep.astype(f32) + got.astype(f32)).astype(bf16)
+    return lax.psum_scatter(both, "dp", scatter_dimension=0, axis_index_groups=lanes)
 
 
 def fold_y(near, got):
@@ -640,24 +712,6 @@
     return jnp.stack([first, second]) / gains
 
 
-def layer_forward(place, layer, x, head, rest):
-    n1, q, k, v, vec = qkv_forward(place, x, head)
-    o, s = attend_forward(place, q, k, v, 2, onto=attend_forward(place, q, k, v, 0))
-    middle, n2, scale, ga, ta = gate_forward(place, layer, x, n1, o, vec, rest)
-    y, h, slope, gf, tf = feed_forward(place, layer, middle, n2, vec, rest)
-    return y, (x, n1, q, k, v, vec, o, s, n2, scale, ga, ta, h, slope, gf, tf)
-
-
-def layer_backward(place, layer, grads, kept, head, rest):
-    x, n1, q, k, v, vec, o, s, n2, scale, ga, ta, h, slope, gf, tf = kept
-    dm, df, dzf, du, da, dza, do, small = feed_back(place, layer, grads, n2, scale, ga, ta, slope, gf, tf, vec, rest)
-    later = rest_grad(place, o, n1, n2, h, da, dza, dzf, du, df, small)
-    dqkv = attend_back(place, q, k, v, o, s, do, 2, onto=attend_back(place, q, k, v, o, s, do, 0))
-    early = first_grad(place, (n1, *dqkv))
-    dx, low = qkv_back(place, layer, x, dm, *dqkv, dza, vec, head, rest)
-    return dx, low, collect_whole(early, later)
-
-
 def per_device(tokens, cotangent, w_qkv, w_out, w_gates, w_up, w_down, norm_gains, gate_biases):
     section = lax.axis_index("section")
     index = lax.axis_index("dp")
@@ -676,20 +730,31 @@
     else:
         place = jnp.zeros((3,), jnp.int32)
         heads, rest = weights_whole(*masters)
-        y0, kept0 = layer_forward(place, 0, x, heads[0], rest[0])
-        y1, kept1 = layer_forward(place, 1, y0, heads[1], rest[1])
+        n0, q0, k0, v0, vec0 = qkv_forward(place, x, heads[0])
+        o0, s0 = attend_forward(place, q0, k0, v0, 2, onto=attend_forward(place, q0, k0, v0, 0))
+        y0, *kept = feed_forward(place, x, n0, o0, vec0, rest[0])
+        n1, q1, k1, v1, vec1 = qkv_forward(place, y0, heads[1])
+        o1, s1 = attend_forward(place, q1, k1, v1, 2, onto=attend_forward(place, q1, k1, v1, 0))
         seeds = pick(own_seed, crossed(other_seed))
-        dx1, low1, grads1 = layer_backward(place, 1, [seeds[1]], kept1, heads[1], rest[1])
-        dx0, low0, grads0 = layer_backward(place, 0, [seeds[0], low1], kept0, heads[0], rest[0])
+        y1, dm, dza, do, *later1 = turn(place, y0, n1, o1, seeds[1], vec1, rest[1])
+        dqkv = attend_back(place, q1, k1, v1, o1, s1, do, 2, onto=attend_back(place, q1, k1, v1, o1, s1, do, 0))
+        early1 = first_grad(place, (n1, *dqkv))
+        dx1, low1, dm, dza, do, *later0 = joint_back(
+            place, y0, dm, dqkv, dza, vec1, heads[1], rest[1], seeds[0], (n0, o0, vec0, *kept), rest[0]
+        )
+        dqkv = attend_back(place, q0, k0, v0, o0, s0, do, 2, onto=attend_back(place, q0, k0, v0, o0, s0, do, 0))
+        early0 = first_grad(place, (n0, *dqkv))
+        dx0, low0 = qkv_back(place, x, dm, *dqkv, dza, vec0, heads[0], rest[0])
+        grads0, grads1 = collect_whole(early0, later0), collect_whole(early1, later1)
         dxs, lows = (dx0, dx1), (crossed(low0, (1,)), crossed(low1, (0,)))
         theirs = crossed(jnp.where(first, y1, y0))
         grads = [jnp.where(first, *pair) for pair in zip(grads0, grads1)]
 
     mine = jnp.where(first, y0, y1)
     block = jnp.stack([jnp.where(first, mine, theirs), jnp.where(first, theirs, mine)])[None, :, None]
-    dx = jnp.where(first, *dxs)
-    other = jnp.where(first, *lows).astype(f32)
-    in_grads = jnp.stack([jnp.where(first, dx, other), jnp.where(first, other, dx)])[None, :, None]
+    in_grads = jnp.stack([jnp.where(first, dxs[0], lows[1].astype(f32)), dxs[1]])
+    last = jnp.where(first, lows[0].astype(f32), dxs[1])
+    in_grads = lax.dynamic_update_slice(in_grads, last[None], (1, 0, 0))[None, :, None]
     grads.insert(5, gain_grads(grads, w_qkv, w_gates, w_up, norm_gains))
     return (block, in_grads, *(grad[None] for grad in grads))
 
@@ -699,7 +764,7 @@
     place = jnp.stack([index // 4, (index // 2) & 1, index & 1]).astype(jnp.int32)
     head, tail = pack(place, index, *masters)
     heads = pick(head, crossed(head))
-    tails = pick(tail, crossed(after(tail, heads[0])))
+    tails = pick(tail, crossed(tail))
     tail0 = lax.all_gather(tails[0], "dp", axis=0)
 
     def cores(z, y):
@@ -710,57 +775,62 @@
     zh1 = along_z(after(heads[1], yh0))
     head0 = cores(zh0, yh0)
     n1, q, k, v, vec = qkv_forward(place, x, head0)
-    zh1 = jnp.stack([after(part, n1) for part in zh1])
+    o, s = attend_forward(place, q, k, v, 0)
+    zh1 = jnp.stack([after(part, o) for part in zh1])
     yh1 = swapped(zh1, 2)
-    o, s = attend_forward(place, q, k, v, 0, waits=(zh1,))
-    o, s = attend_forward(place, q, k, v, 2, onto=(o, s))
+    o, s = attend_forward(place, q, k, v, 2, onto=(o, s), waits=(zh1,))
     tail0 = after(tail0, o)
     tail1 = lax.all_gather(after(tails[1], tail0), "dp", axis=0)
-    middle, n2, scale, ga, ta = gate_forward(place, 0, x, n1, o, vec, tail0)
-    head1 = cores(after(zh1, n2), after(yh1, n2))
-    y0, h, slope, gf, tf = feed_forward(place, 0, middle, n2, vec, tail0)
-    other_seed = crossed(after(other_seed, n2))
-    kept0 = (x, n1, q, k, v, vec, o, s, n2, scale, ga, ta, h, slope, gf, tf)
+    other_seed = crossed(after(other_seed, o))
+    y0, *held = feed_forward(place, x, n1, o, vec, tail0)
+    head1 = cores(after(zh1, y0), after(yh1, y0))
+    kept0 = (n1, o, vec, *held)
+    layer0 = (q, k, v, o, s)
 
     n1, q, k, v, vec = qkv_forward(place, y0, head1)
     o, s = attend_forward(place, q, k, v, 0)
     o, s = attend_forward(place, q, k, v, 2, onto=(o, s))
-    middle, n2, scale, ga, ta = gate_forward(place, 1, y0, n1, o, vec, tail1)
-    y1, h, slope, gf, tf = feed_forward(place, 1, middle, n2, vec, tail1)
+    seeds = pick(own_seed, after(other_seed, o))
+    y1, dm, dza, do, keep, send = turn(place, y0, n1, o, seeds[1], vec, tail1)
+    got = swapped(send, 1)
     theirs = crossed(jnp.where(first, y1, y0))
-
-    seeds = pick(own_seed, after(other_seed, y1))
-    dm1, df, dzf, du, da, dza1, do, small = feed_back(place, 1, [seeds[1]], n2, scale, ga, ta, slope, gf, tf, vec, tail1)
-    rest1 = lax.psum_scatter(rest_grad(place, o, n1, n2, h, da, dza1, dzf, du, df, small), "dp", scatter_dimension=0)
     dqkv = attend_back(place, q, k, v, o, s, do, 0)
+    rest1 = scattered(keep, after(got, dqkv[0]))
     dqkv = attend_back(place, q, k, v, o, s, do, 2, onto=dqkv)
-    dx1, low1 = qkv_back(place, 1, y0, dm1, *dqkv, dza1, vec, head1, tail1, waits=(theirs,))
-    early1 = (n1, *dqkv)
+    keep_b, send_b = first_grad(place, (n1, *dqkv))
+    got_b = swapped(send_b, 1)
+    dx1, low1, dm, dza, do, keep, send = joint_back(
+        place, y0, dm, dqkv, dza, vec, head1, tail1, seeds[0], kept0, tail0, waits=(keep_b,)
+    )
+    n1, o, vec = kept0[:3]
+    q, k, v, o, s = layer0
+    got = swapped(send, 1)
+    away, near = fold_core(keep_b, after(got_b, low1))
+    got_b = swapped(away, 2)
     other1 = crossed(low1, (0,))
-
-    x, n1, q, k, v, vec, o, s, n2, scale, ga, ta, h, slope, gf, tf = kept0
-    dm, df, dzf, du, da, dza, do, small = feed_back(
-        place, 0, [seeds[0], low1], n2, scale, ga, ta, slope, gf, tf, vec, tail0
-    )
-    grad0 = rest_grad(place, o, n1, n2, h, da, dza, dzf, du, df, small, waits=(other1,))
-    rest0 = lax.psum_scatter(grad0, "dp", scatter_dimension=0)
-    dqkv = attend_back(place, q, k, v, o, s, do, 0)
+    dqkv = attend_back(place, q, k, v, o, s, do, 0, 1, waits=(away,))
     rest1 = after(rest1, dqkv[0])
-    last1 = crossed(rest1, (0,))
-    dqkv = attend_back(place, q, k, v, o, s, do, 2, onto=dqkv)
-    keep, send = first_grad(place, (n1, *dqkv), early1, waits=(last1,))
+    rest0 = scattered(keep, after(got, dqkv[0]))
+    own, sends = fold_y(near, after(got_b, dqkv[0]))
+    gots = [moved_z(part, at + 1) for at, part in enumerate(sends)]
+    dqkv = attend_back(place, q, k, v, o, s, do, 1, 3, onto=dqkv, waits=(theirs, *sends))
+    early1 = fold_z(own, [after(got, dqkv[0]) for got in gots])
+    low = jnp.concatenate([rest1, early1.astype(bf16)])
+    last1 = crossed(low, (0,))
+    keep, send = first_grad(place, (n1, *dqkv), waits=(other1, low))
     got = swapped(send, 1)
-    dx0, low0 = qkv_back(place, 0, x, dm, *dqkv, dza, vec, head0, tail0, waits=(keep,))
-    rest1 = rest1.astype(f32) + last1.astype(f32)
-    away, near = fold_core(keep, after(got, low0))
+    away, near = fold_core(keep, got)
     got = swapped(away, 2)
-    other0 = crossed(after(low0, away), (1,))
-    own, sends = fold_y(near, got)
-    own = fold_z(own, [moved_z(part, at + 1) for at, part in enumerate(sends)])
-    half = 3 * UNIT
-    mine, theirs_early = jnp.where(first, own[:half], own[half:]), jnp.where(first, own[half:], own[:half])
-    early = mine + crossed(theirs_early.astype(bf16)).astype(f32)
-    rest0 = after(rest0, own)
+    dx0, low0 = qkv_back(place, x, dm, *dqkv, dza, vec, head0, tail0, waits=(away,))
+    last1 = after(last1, low0).astype(f32)
+    rest1, early1 = rest1.astype(f32) + last1[: REST + 16], early1 + last1[REST + 16 :]
+    other0 = crossed(low0, (1,))
+    own, sends = fold_y(near, after(got, low0))
+    gots = [moved_z(part, at + 1) for at, part in enumerate(sends)]
+    early0 = fold_z(own, gots)
+    early0 = early0 + crossed(early0.astype(bf16), (1,)).astype(f32)
+    early = jnp.where(first, early0, early1)
+    rest0 = after(rest0, gots[0])
     rest0 = rest0.astype(f32) + crossed(rest0, (1,)).astype(f32)
     later = jnp.where(first, rest0, rest1)
     grads = [

time: 440 us -> 394 us (0.90)
  Pallas kernels: 239 us -> 207 us
  waiting for transfers between devices: 105 us -> 76 us
  other arithmetic: 23.4 us -> 34.8 us
  starting transfers between devices: 40 us -> 45.9 us
    pallas_call x22 -> x17, Pallas kernels: 239 us -> 207 us  [run(): pl.pallas_call(body, grid_spec=pltpu.PrefetchScalarGridSpec(num_scalar_pr...]
    ppermute x8 -> x12, waiting for transfers between devices: 40 us -> 13 us  [swapped(): lax.ppermute(value, 'dp', [(d, d ^ bit) for d in range(lax.axis_size('dp'...]
    reduce_scatter x2, waiting for transfers between devices: 9.84 us -> 0.01 us  [scattered(): lax.psum_scatter(both, 'dp', scatter_dimension=0, axis_index_groups=lanes)]
    ppermute x9, waiting for transfers between devices: 22 us -> 29.3 us  [crossed(): return lax.ppermute(value, 'section', [(s, 1 - s) for s in sources])]
    convert_element_type x1 -> x5, other arithmetic: 0.02 us -> 7.06 us  [the longest x2 6.86 us: scattered(): both = (keep.astype(f32) + got.astype(f32)).astype(bf16)]
    ppermute x9 -> x12, starting transfers between devices: 16.2 us -> 18.6 us  [moved_z(): lax.ppermute(value, 'dp', [(d, (d + 4 * steps) % count) for d in range(co...]
    ppermute x9 -> x12, waiting for transfers between devices: 25.2 us -> 24.7 us  [moved_z(): lax.ppermute(value, 'dp', [(d, (d + 4 * steps) % count) for d in range(co...]
  transfers between devices with their start and end apart: 30 -> 37, of which waited for: 15 -> 17; matrix products, arithmetic and copies ran while one was open for 3% -> 7% of each run, Pallas kernels for 48% -> 44%
where the time goes in v3:
time: 394 us; the launch traced here: 386 us
  Pallas kernels  207 us (53%)
  waiting for transfers between devices  76 us (19%)
  starting transfers between devices  45.9 us (12%)
  other arithmetic  34.8 us (9%)
  between operations  14.8 us (4%)
  local copies, waits for them, and re-layouts  8.12 us (2%)
    pallas_call x17, Pallas kernels, run(): pl.pallas_call(body, grid_spec=pltpu.PrefetchScalarGridSpec(num_scalar_pr...  207 us
    ppermute x9, waiting for transfers between devices, crossed(): return lax.ppermute(value, 'section', [(s, 1 - s) for s in sources])  29.3 us
    ppermute x12, waiting for transfers between devices, moved_z(): lax.ppermute(value, 'dp', [(d, (d + 4 * steps) % count) for d in range(co...  24.7 us
    ppermute x9, starting transfers between devices, crossed(): return lax.ppermute(value, 'section', [(s, 1 - s) for s in sources])  20.7 us
    ppermute x12, starting transfers between devices, moved_z(): lax.ppermute(value, 'dp', [(d, (d + 4 * steps) % count) for d in range(co...  18.6 us
    ppermute x12, waiting for transfers between devices, swapped(): lax.ppermute(value, 'dp', [(d, d ^ bit) for d in range(lax.axis_size('dp'...  13 us
    all_gather x1, waiting for transfers between devices, run(): tail1 = lax.all_gather(after(tails[1], tail0), 'dp', axis=0)  7.89 us
  transfers between devices with their start and end apart: 37, of which 17 were waited for; matrix products, arithmetic and copies ran while one was open for 7% of the time, Pallas kernels for 44%

profile of v3, /device:TPU:0, one launch (start us, length us, event | category | flops | bytes accessed | tf_op | source)
XLA Modules:
  0.0 386.5 jit_solution(9227257613300579750)
XLA Ops:
  15.0 8.6 %collective-permute-done.10 = bf16[352,512]{1,0:T(8,128)(2,1)S(1)} collective-permute-done((bf16[352,512]{1,0:T(8,128)(2,1)}, bf16[352,512]{1,0:T(8,128)(2,1)S(1)}, u32[]{:S(2)}, u32[]{:S(2)}) %collective-permute-start.10) | collective-permute-done | bytes 360480 | tf_op jit(solution)/shard_map/ppermute | solution.py:591
  40.8 10.7 %collective-permute-done.2 = bf16[112,512]{1,0:T(8,128)(2,1)S(1)} collective-permute-done((bf16[112,512]{1,0:T(8,128)(2,1)S(1)}, bf16[112,512]{1,0:T(8,128)(2,1)S(1)}, u32[]{:S(2)}, u32[]{:S(2)}) %collective-permute-start.2) | collective-permute-done | bytes 114720 | tf_op jit(solution)/shard_map/ppermute | solution.py:583
  53.1 7.1 %collective-permute-done.4.refs_3_.refs_10_ = bf16[4,112,512]{2,1,0:T(8,128)(2,1)S(1)} collective-permute-done((bf16[4,112,512]{2,1,0:T(8,128)(2,1)S(1)}, bf16[4,112,512]{2,1,0:T(8,128)(2,1)S(1)}, u32[]{:S(2)}, u32[]{:S(2)}) %collective-permute-start.4) | collective-permute-done | bytes 458784 | tf_op jit(solution)/shard_map/ppermute | solution.py:587
  68.8 7.4 %shard_map.161 = (bf16[1024,512]{1,0:T(8,128)(2,1)}, bf16[1024,512]{1,0:T(8,128)(2,1)}, bf16[1024,512]{1,0:T(8,128)(2,1)}, bf16[1024,512]{1,0:T(8,128)(2,1)}, f32[16,512]{1,0:T(8,128)}) custom-call(s32[3]{0:T(128)} %pad_add_fusion.refs_0_, bf16[1024,512]{1,0:T(8,128)(2,1)} %select_bitcast_fusion.4.refs_1_, bf16[4,112,512]{2,1,0:T(8,128)(2,1)} %copy-done.8, ...), custom_call_target="tpu_custom_call" | custom-call | flops 1610612736 | bytes 8000000 | tf_op jit(solution)/shard_map/pallas_call | solution.py:72
  76.2 9.2 %shard_map.162 = (bf16[1024,512]{1,0:T(8,128)(2,1)}, f32[1024,512]{1,0:T(8,128)}) custom-call(s32[3]{0:T(128)} %pad_add_fusion.refs_0_, bf16[1024,512]{1,0:T(8,128)(2,1)} %get-tuple-element.93.refs_1_, bf16[1024,512]{1,0:T(8,128)(2,1)} %get-tuple-element.94.refs_2_, bf16[1024,512]{1,0:T(8,128)(2,1)} %get-tuple-element.95.refs_3_), custom_call_target="tpu_custom_call" | custom-call | flops 6000000000 | bytes 3000000 | tf_op jit(solution)/shard_map/pallas_call | solution.py:72
  89.2 9.4 %shard_map.163 = (bf16[1024,512]{1,0:T(8,128)(2,1)}, f32[1024,512]{1,0:T(8,128)}) custom-call(s32[3]{0:T(128)} %pad_add_fusion.refs_0_, bf16[1024,512]{1,0:T(8,128)(2,1)} %get-tuple-element.93.refs_1_, bf16[1024,512]{1,0:T(8,128)(2,1)} %get-tuple-element.94.refs_2_, ...), custom_call_target="tpu_custom_call", output_to_operand_aliasing={{0}: (4, {}), {1}: (5, {})} | custom-call | flops 6000000000 | bytes 3000000 | tf_op jit(solution)/shard_map/pallas_call | solution.py:72
  102.0 18.2 %shard_map.164 = (bf16[1024,512]{1,0:T(8,128)(2,1)}, bf16[1024,512]{1,0:T(8,128)(2,1)}, f32[1024,128]{1,0:T(8,128)}, bf16[1024,512]{1,0:T(8,128)(2,1)}, bf16[102...) custom-call(s32[3]{0:T(128)} %pad_add_fusion.refs_0_, ...), custom_call_target="tpu_custom_call" | custom-call | flops 5905580032 | bytes 24000000 | tf_op jit(solution)/shard_map/pallas_call | solution.py:72
  124.2 7.5 %shard_map.165 = (bf16[1024,512]{1,0:T(8,128)(2,1)}, bf16[1024,512]{1,0:T(8,128)(2,1)}, bf16[1024,512]{1,0:T(8,128)(2,1)}, bf16[1024,512]{1,0:T(8,128)(2,1)}, f32[16,512]{1,0:T(8,128)}) custom-call(s32[3]{0:T(128)} %pad_add_fusion.refs_0_, bf16[1024,512]{1,0:T(8,128)(2,1)} %get-tuple-element.107.refs_1_, ...), custom_call_target="tpu_custom_call" | custom-call | flops 1610612736 | bytes 8000000 | tf_op jit(solution)/shard_map/pallas_call | solution.py:72
  131.7 9.3 %shard_map.166 = (bf16[1024,512]{1,0:T(8,128)(2,1)}, f32[1024,512]{1,0:T(8,128)}) custom-call(s32[3]{0:T(128)} %pad_add_fusion.refs_0_, bf16[1024,512]{1,0:T(8,128)(2,1)} %get-tuple-element.111.refs_1_, bf16[1024,512]{1,0:T(8,128)(2,1)} %get-tuple-element.112.refs_2_, bf16[1024,512]{1,0:T(8,128)(2,1)} %get-tuple-element.113.refs_3_), custom_call_target="tpu_custom_call" | custom-call | flops 6000000000 | bytes 3000000 | tf_op jit(solution)/shard_map/pallas_call | solution.py:72
  141.0 9.3 %shard_map.167 = (bf16[1024,512]{1,0:T(8,128)(2,1)}, f32[1024,512]{1,0:T(8,128)}) custom-call(s32[3]{0:T(128)} %pad_add_fusion.refs_0_, bf16[1024,512]{1,0:T(8,128)(2,1)} %get-tuple-element.111.refs_1_, bf16[1024,512]{1,0:T(8,128)(2,1)} %get-tuple-element.112.refs_2_, ...), custom_call_target="tpu_custom_call", output_to_operand_aliasing={{0}: (4, {}), {1}: (5, {})} | custom-call | flops 6000000000 | bytes 3000000 | tf_op jit(solution)/shard_map/pallas_call | solution.py:72
  151.9 7.9 %all-gather.7.cloned.1.call-done = bf16[5632,512]{1,0:T(8,128)(2,1)} async-done(((bf16[352,512]{1,0:T(8,128)(2,1)}), bf16[5632,512]{1,0:T(8,128)(2,1)}) %all-gather.7.cloned.1.call-update) | async-done | bytes 5767184 | tf_op jit(solution)/shard_map/all_gather | solution.py:783
  159.8 32.7 %shard_map.168 = (bf16[1024,512]{1,0:T(8,128)(2,1)}, f32[1024,512]{1,0:T(8,128)}, bf16[1024,512]{1,0:T(8,128)(2,1)}, bf16[1024,512]{1,0:T(8,128)(2,1)}, bf16[8,3...) custom-call(s32[3]{0:T(128)} %pad_add_fusion.refs_0_, bf16[1024,512]{1,0:T(8,128)(2,1)} %get-tuple-element.107.refs_1_, ...), custom_call_target="tpu_custom_call" | custom-call | flops 17716740096 | bytes 24000000 | tf_op jit(solution)/shard_map/pallas_call | solution.py:72
  192.8 12.1 %shard_map.169 = (bf16[1024,512]{1,0:T(8,128)(2,1)}, bf16[1024,512]{1,0:T(8,128)(2,1)}, bf16[1024,512]{1,0:T(8,128)(2,1)}) custom-call(s32[3]{0:T(128)} %pad_add_fusion.refs_0_, bf16[1024,512]{1,0:T(8,128)(2,1)} %get-tuple-element.111.refs_1_, bf16[1024,512]{1,0:T(8,128)(2,1)} %get-tuple-element.112.refs_2_, bf16[1024,512]{1,0:T(8,128)(2,1)} %get-tuple-element.113.refs_3_, ...), custom_call_target="tpu_custom_call" | custom-call | flops 10000000000 | bytes 5000000 | tf_op jit(solution)/shard_map/pallas_call | solution.py:72
  207.4 12.1 %shard_map.170 = (bf16[1024,512]{1,0:T(8,128)(2,1)}, bf16[1024,512]{1,0:T(8,128)(2,1)}, bf16[1024,512]{1,0:T(8,128)(2,1)}) custom-call(s32[3]{0:T(128)} %pad_add_fusion.refs_0_, bf16[1024,512]{1,0:T(8,128)(2,1)} %get-tuple-element.111.refs_1_, ...), custom_call_target="tpu_custom_call", output_to_operand_aliasing={{0}: (7, {}), {1}: (8, {}), {2}: (9, {})} | custom-call | flops 10000000000 | bytes 5000000 | tf_op jit(solution)/shard_map/pallas_call | solution.py:72
  219.5 6.5 %shard_map.171 = (bf16[2,4,96,512]{3,2,1,0:T(8,128)(2,1)}, bf16[2,4,96,512]{3,2,1,0:T(8,128)(2,1)}) custom-call(s32[3]{0:T(128)} %pad_add_fusion.refs_0_, bf16[1024,512]{1,0:T(8,128)(2,1)} %get-tuple-element.110.refs_2_.refs_7_.refs_1_, bf16[1024,512]{1,0:T(8,128)(2,1)} %get-tuple-element.128.refs_2_.refs_3_, ...), custom_call_target="tpu_custom_call" | custom-call | flops 1610612736 | bytes 9000000 | tf_op jit(solution)/shard_map/pallas_call | solution.py:72
  226.0 30.2 %shard_map.172 = (f32[1024,512]{1,0:T(8,128)}, bf16[1024,512]{1,0:T(8,128)(2,1)}, f32[1024,512]{1,0:T(8,128)}, bf16[1024,512]{1,0:T(8,128)(2,1)}, bf16[1024,512]...) custom-call(s32[3]{0:T(128)} %pad_add_fusion.refs_0_, ...), custom_call_target="tpu_custom_call" | custom-call | flops 13958643712 | bytes 40000000 | tf_op jit(solution)/shard_map/pallas_call | solution.py:72
  263.7 7.6 %shard_map.173 = (bf16[1024,512]{1,0:T(8,128)(2,1)}, bf16[1024,512]{1,0:T(8,128)(2,1)}, bf16[1024,512]{1,0:T(8,128)(2,1)}) custom-call(s32[3]{0:T(128)} %pad_add_fusion.refs_0_, bf16[1024,512]{1,0:T(8,128)(2,1)} %get-tuple-element.93.refs_1_, bf16[1024,512]{1,0:T(8,128)(2,1)} %get-tuple-element.94.refs_2_, bf16[1024,512]{1,0:T(8,128)(2,1)} %get-tuple-element.95.refs_3_, ...), custom_call_target="tpu_custom_call" | custom-call | flops 5000000000 | bytes 5000000 | tf_op jit(solution)/shard_map/pallas_call | solution.py:72
  285.9 16.7 %shard_map.174 = (bf16[1024,512]{1,0:T(8,128)(2,1)}, bf16[1024,512]{1,0:T(8,128)(2,1)}, bf16[1024,512]{1,0:T(8,128)(2,1)}) custom-call(s32[3]{0:T(128)} %pad_add_fusion.refs_0_, bf16[1024,512]{1,0:T(8,128)(2,1)} %get-tuple-element.93.refs_1_, ...), custom_call_target="tpu_custom_call", output_to_operand_aliasing={{0}: (7, {}), {1}: (8, {}), {2}: (9, {})} | custom-call | flops 15000000512 | bytes 5000000 | tf_op jit(solution)/shard_map/pallas_call | solution.py:72
  304.9 6.5 %shard_map.175 = (bf16[2,4,96,512]{3,2,1,0:T(8,128)(2,1)}, bf16[2,4,96,512]{3,2,1,0:T(8,128)(2,1)}) custom-call(s32[3]{0:T(128)} %pad_add_fusion.refs_0_, bf16[1024,512]{1,0:T(8,128)(2,1)} %get-tuple-element.92.refs_2_.refs_18_.refs_1_, bf16[1024,512]{1,0:T(8,128)(2,1)} %get-tuple-element.151.refs_2_.refs_3_, ...), custom_call_target="tpu_custom_call" | custom-call | flops 1610612736 | bytes 9000000 | tf_op jit(solution)/shard_map/pallas_call | solution.py:72
  318.6 4.4 %collective-permute-start.30 = (bf16[464,512]{1,0:T(8,128)(2,1)S(1)}, bf16[464,512]{1,0:T(8,128)(2,1)S(1)}, u32[]{:S(2)}, u32[]{:S(2)}) collective-permute-start(bf16[464,512]{1,0:T(8,128)(2,1)S(1)} %copy-done.17), channel_id=1, source_target_pairs={{0,16},{1,17},{2,18},{3,19},{4,20},{5,21},{6,22},{7,23},{8,24},{9,... | collective-permute-start | bytes 1425416 | tf_op jit(solution)/shard_map/ppermute | solution.py:591
  323.0 9.5 %shard_map.176 = (f32[1024,512]{1,0:T(8,128)}, bf16[1024,512]{1,0:T(8,128)(2,1)}) custom-call(s32[3]{0:T(128)} %pad_add_fusion.refs_0_, bf16[1024,512]{1,0:T(8,128)(2,1)} %select_bitcast_fusion.4.refs_1_, f32[1024,512]{1,0:T(8,128)} %get-tuple-element.141.refs_2_, bf16[1024,512]{1,0:T(8,128)(2,1)} %get-tuple-element.151.refs_2_.refs_3_, ...), custom_call_target="tpu_custom_call" | custom-call | flops 2147483648 | bytes 12000000 | tf_op jit(solution)/shard_map/pallas_call | solution.py:72
  341.9 4.7 %collective-permute-done.27 = bf16[96,512]{1,0:T(8,128)(2,1)S(1)} collective-permute-done((bf16[96,512]{1,0:T(8,128)(2,1)S(1)}, bf16[96,512]{1,0:T(8,128)(2,1)S(1)}, u32[]{:S(2)}, u32[]{:S(2)}) %collective-permute-start.27) | collective-permute-done | bytes 98336 | tf_op jit(solution)/shard_map/ppermute | solution.py:583
  350.6 11.0 %collective-permute-done.29 = bf16[96,512]{1,0:T(8,128)(2,1)S(1)} collective-permute-done((bf16[96,512]{1,0:T(8,128)(2,1)S(1)}, bf16[96,512]{1,0:T(8,128)(2,1)S(1)}, u32[]{:S(2)}, u32[]{:S(2)}) %collective-permute-start.29) | collective-permute-done | bytes 98336 | tf_op jit(solution)/shard_map/ppermute | solution.py:591
  369.5 5.6 %collective-permute-done.32 = bf16[368,512]{1,0:T(8,128)(2,1)S(1)} collective-permute-done((bf16[368,512]{1,0:T(8,128)(2,1)}, bf16[368,512]{1,0:T(8,128)(2,1)S(1)}, u32[]{:S(2)}, u32[]{:S(2)}) %collective-permute-start.32) | collective-permute-done | bytes 376864 | tf_op jit(solution)/shard_map/ppermute | solution.py:591
  (185 shorter events, 107.5 us)
Async XLA Ops:
  7.2 92.4 %all-gather.5.cloned.1.call-start = ((), (), s32[]{:S(2)}) async-start(), calls=%async_computation.4 | async-start | bytes 6127616 | tf_op jit(solution)/shard_map/all_gather | solution.py:768
  25.5 134.2 %all-gather.7.cloned.1.call-start = ((), (), s32[]{:S(2)}) async-start(), calls=%async_computation.5 | async-start | bytes 6127616 | tf_op jit(solution)/shard_map/all_gather | solution.py:783
  35.5 16.1 %collective-permute-start.2 = (bf16[112,512]{1,0:T(8,128)(2,1)S(1)}, bf16[112,512]{1,0:T(8,128)(2,1)S(1)}, u32[]{:S(2)}, u32[]{:S(2)}) collective-permute-start(bf16[112,512]{1,0:T(8,128)(2,1)S(1)} %get-tuple-element.208), channel_id=1, source_target_pairs={{0,8},{1,9},{2,10},{3,11},{4,12},{5,13},{6,14},{7,15},{8,0},{9,1},... | collective-permute-start | bytes 344072 | tf_op jit(solution)/shard_map/ppermute | solution.py:583
  35.5 16.1 %collective-permute-start.1 = (bf16[112,512]{1,0:T(8,128)(2,1)S(1)}, bf16[112,512]{1,0:T(8,128)(2,1)S(1)}, u32[]{:S(2)}, u32[]{:S(2)}) collective-permute-start(bf16[112,512]{1,0:T(8,128)(2,1)S(1)} %get-tuple-element.208), channel_id=1, source_target_pairs={{0,4},{1,5},{2,6},{3,7},{4,8},{5,9},{6,10},{7,11},{8,12},{9,13},{1... | collective-permute-start | bytes 344072 | tf_op jit(solution)/shard_map/ppermute | solution.py:583
  53.1 14.2 %collective-permute-start.5 = (bf16[4,112,512]{2,1,0:T(8,128)(2,1)S(1)}, bf16[4,112,512]{2,1,0:T(8,128)(2,1)S(1)}, u32[]{:S(2)}, u32[]{:S(2)}) collective-permute-start(bf16[4,112,512]{2,1,0:T(8,128)(2,1)S(1)} %pad_maximum_fusion.1.refs_2_.refs_9_), channel_id=1, source_target_pairs={{0,1},{1,0},{2,3},{3,2},{4,5},{5,4},{6,7},{7,6},{8,9},{9,8},{10,11... | collective-permute-start | bytes 1376264 | tf_op jit(solution)/shard_map/ppermute | solution.py:587
  61.3 24.1 %collective-permute-start.9 = (bf16[112,512]{1,0:T(8,128)(2,1)S(1)}, bf16[112,512]{1,0:T(8,128)(2,1)S(1)}, u32[]{:S(2)}, u32[]{:S(2)}) collective-permute-start(bf16[112,512]{1,0:T(8,128)(2,1)S(1)} %get-tuple-element.99), channel_id=1, source_target_pairs={{0,12},{1,13},{2,14},{3,15},{4,0},{5,1},{6,2},{7,3},{8,4},{9,5},{1... | collective-permute-start | bytes 344072 | tf_op jit(solution)/shard_map/ppermute | solution.py:583
  61.3 27.0 %collective-permute-start.8 = (bf16[112,512]{1,0:T(8,128)(2,1)S(1)}, bf16[112,512]{1,0:T(8,128)(2,1)S(1)}, u32[]{:S(2)}, u32[]{:S(2)}) collective-permute-start(bf16[112,512]{1,0:T(8,128)(2,1)S(1)} %get-tuple-element.99), channel_id=1, source_target_pairs={{0,8},{1,9},{2,10},{3,11},{4,12},{5,13},{6,14},{7,15},{8,0},{9,1},... | collective-permute-start | bytes 344072 | tf_op jit(solution)/shard_map/ppermute | solution.py:583
  65.2 23.1 %collective-permute-start.7 = (bf16[112,512]{1,0:T(8,128)(2,1)S(1)}, bf16[112,512]{1,0:T(8,128)(2,1)S(1)}, u32[]{:S(2)}, u32[]{:S(2)}) collective-permute-start(bf16[112,512]{1,0:T(8,128)(2,1)S(1)} %get-tuple-element.99), channel_id=1, source_target_pairs={{0,4},{1,5},{2,6},{3,7},{4,8},{5,9},{6,10},{7,11},{8,12},{9,13},{1... | collective-permute-start | bytes 344072 | tf_op jit(solution)/shard_map/ppermute | solution.py:583
  99.6 186.2 %reduce-scatter.3.cloned.1.call-start = ((), (), s32[]{:S(2)}) async-start(), calls=%async_computation.2 | async-start | bytes 3391488 | tf_op jit(solution)/shard_map/reduce_scatter | solution.py:660
  100.2 20.1 %collective-permute-start.11 = (bf16[4,112,512]{2,1,0:T(8,128)(2,1)S(1)}, bf16[4,112,512]{2,1,0:T(8,128)(2,1)S(1)}, u32[]{:S(2)}, u32[]{:S(2)}) collective-permute-start(bf16[4,112,512]{2,1,0:T(8,128)(2,1)S(1)} %copy-done.18), channel_id=1, source_target_pairs={{0,2},{1,3},{2,0},{3,1},{4,6},{5,7},{6,4},{7,5},{8,10},{9,11},{10,... | collective-permute-start | bytes 1376264 | tf_op jit(solution)/shard_map/ppermute | solution.py:587
  120.9 29.4 %collective-permute-start.14 = (bf16[1024,512]{1,0:T(8,128)(2,1)S(1)}, bf16[1024,512]{1,0:T(8,128)(2,1)S(1)}, u32[]{:S(2)}, u32[]{:S(2)}) collective-permute-start(bf16[1024,512]{1,0:T(8,128)(2,1)S(1)} %select_bitcast_fusion.3), channel_id=1, source_target_pairs={{0,16},{16,0},{1,17},{17,1},{2,18},{18,2},{3,19},{19,3},{4,20},{20... | collective-permute-start | bytes 3145736 | tf_op jit(solution)/shard_map/ppermute | solution.py:591
  192.4 12.4 %collective-permute-start.19 = (bf16[8,368,512]{2,1,0:T(8,128)(2,1)}, bf16[8,368,512]{2,1,0:T(8,128)(2,1)S(1)}, u32[]{:S(2)}, u32[]{:S(2)}) collective-permute-start(bf16[8,368,512]{2,1,0:T(8,128)(2,1)} %get-tuple-element.156), channel_id=1, source_target_pairs={{0,1},{1,0},{2,3},{3,2},{4,5},{5,4},{6,7},{7,6},{8,9},{9,8},{10,11... | collective-permute-start | bytes 9043976 | tf_op jit(solution)/shard_map/ppermute | solution.py:587
  207.3 156.0 %reduce-scatter.5.cloned.1.call-start = ((), (), s32[]{:S(2)}) async-start(), calls=%async_computation.3 | async-start | bytes 3391488 | tf_op jit(solution)/shard_map/reduce_scatter | solution.py:660
  256.2 15.1 %collective-permute-start.31 = (bf16[8,368,512]{2,1,0:T(8,128)(2,1)}, bf16[8,368,512]{2,1,0:T(8,128)(2,1)}, u32[]{:S(2)}, u32[]{:S(2)}) collective-permute-start(bf16[8,368,512]{2,1,0:T(8,128)(2,1)} %get-tuple-element.170), channel_id=1, source_target_pairs={{0,1},{1,0},{2,3},{3,2},{4,5},{5,4},{6,7},{7,6},{8,9},{9,8},{10,11... | collective-permute-start | bytes 9043976 | tf_op jit(solution)/shard_map/ppermute | solution.py:587
  257.9 28.0 %collective-permute-start.15 = (bf16[1024,512]{1,0:T(8,128)(2,1)}, bf16[1024,512]{1,0:T(8,128)(2,1)}, u32[]{:S(2)}, u32[]{:S(2)}) collective-permute-start(bf16[1024,512]{1,0:T(8,128)(2,1)} %broadcast_select_fusion.1), channel_id=1, source_target_pairs={{0,16},{16,0},{1,17},{17,1},{2,18},{18,2},{3,19},{19,3},{4,20},{20... | collective-permute-start | bytes 3145736 | tf_op jit(solution)/shard_map/ppermute | solution.py:591
  262.8 17.2 %collective-permute-start.17 = (bf16[4,96,512]{2,1,0:T(8,128)(2,1)S(1)}, bf16[4,96,512]{2,1,0:T(8,128)(2,1)}, u32[]{:S(2)}, u32[]{:S(2)}) collective-permute-start(bf16[4,96,512]{2,1,0:T(8,128)(2,1)S(1)} %fusion.1.refs_7_), channel_id=1, source_target_pairs={{0,2},{1,3},{2,0},{3,1},{4,6},{5,7},{6,4},{7,5},{8,10},{9,11},{10,... | collective-permute-start | bytes 1179656 | tf_op jit(solution)/shard_map/ppermute | solution.py:587
  275.7 29.2 %collective-permute-start.18 = (bf16[1024,512]{1,0:T(8,128)(2,1)}, bf16[1024,512]{1,0:T(8,128)(2,1)}, u32[]{:S(2)}, u32[]{:S(2)}) collective-permute-start(bf16[1024,512]{1,0:T(8,128)(2,1)} %get-tuple-element.145), channel_id=1, source_target_pairs={{0,16},{1,17},{2,18},{3,19},{4,20},{5,21},{6,22},{7,23},{8,24},{9,... | collective-permute-start | bytes 3145736 | tf_op jit(solution)/shard_map/ppermute | solution.py:591
  282.2 20.4 %collective-permute-start.22 = (bf16[96,512]{1,0:T(8,128)(2,1)}, bf16[96,512]{1,0:T(8,128)(2,1)S(1)}, u32[]{:S(2)}, u32[]{:S(2)}) collective-permute-start(bf16[96,512]{1,0:T(8,128)(2,1)} %get-tuple-element.202.refs_13_), channel_id=1, source_target_pairs={{0,12},{1,13},{2,14},{3,15},{4,0},{5,1},{6,2},{7,3},{8,4},{9,5},{1... | collective-permute-start | bytes 294920 | tf_op jit(solution)/shard_map/ppermute | solution.py:583
  284.3 18.3 %collective-permute-start.21 = (bf16[96,512]{1,0:T(8,128)(2,1)}, bf16[96,512]{1,0:T(8,128)(2,1)S(1)}, u32[]{:S(2)}, u32[]{:S(2)}) collective-permute-start(bf16[96,512]{1,0:T(8,128)(2,1)} %get-tuple-element.203.refs_12_), channel_id=1, source_target_pairs={{0,8},{1,9},{2,10},{3,11},{4,12},{5,13},{6,14},{7,15},{8,0},{9,1},... | collective-permute-start | bytes 294920 | tf_op jit(solution)/shard_map/ppermute | solution.py:583
  284.9 17.7 %collective-permute-start.20 = (bf16[96,512]{1,0:T(8,128)(2,1)}, bf16[96,512]{1,0:T(8,128)(2,1)S(1)}, u32[]{:S(2)}, u32[]{:S(2)}) collective-permute-start(bf16[96,512]{1,0:T(8,128)(2,1)} %get-tuple-element.204.refs_11_), channel_id=1, source_target_pairs={{0,4},{1,5},{2,6},{3,7},{4,8},{5,9},{6,10},{7,11},{8,12},{9,13},{1... | collective-permute-start | bytes 294920 | tf_op jit(solution)/shard_map/ppermute | solution.py:583
  315.0 19.0 %collective-permute-start.25 = (bf16[4,96,512]{2,1,0:T(8,128)(2,1)S(1)}, bf16[4,96,512]{2,1,0:T(8,128)(2,1)S(1)}, u32[]{:S(2)}, u32[]{:S(2)}) collective-permute-start(bf16[4,96,512]{2,1,0:T(8,128)(2,1)S(1)} %fusion.2.refs_13_), channel_id=1, source_target_pairs={{0,2},{1,3},{2,0},{3,1},{4,6},{5,7},{6,4},{7,5},{8,10},{9,11},{10,... | collective-permute-start | bytes 1179656 | tf_op jit(solution)/shard_map/ppermute | solution.py:587
  318.6 31.9 %collective-permute-start.30 = (bf16[464,512]{1,0:T(8,128)(2,1)S(1)}, bf16[464,512]{1,0:T(8,128)(2,1)S(1)}, u32[]{:S(2)}, u32[]{:S(2)}) collective-permute-start(bf16[464,512]{1,0:T(8,128)(2,1)S(1)} %copy-done.17), channel_id=1, source_target_pairs={{0,16},{1,17},{2,18},{3,19},{4,20},{5,21},{6,22},{7,23},{8,24},{9,... | collective-permute-start | bytes 1425416 | tf_op jit(solution)/shard_map/ppermute | solution.py:591
  332.6 34.0 %collective-permute-start.24 = (bf16[1024,512]{1,0:T(8,128)(2,1)}, bf16[1024,512]{1,0:T(8,128)(2,1)}, u32[]{:S(2)}, u32[]{:S(2)}) collective-permute-start(bf16[1024,512]{1,0:T(8,128)(2,1)} %get-tuple-element.166), channel_id=1, source_target_pairs={{16,0},{17,1},{18,2},{19,3},{20,4},{21,5},{22,6},{23,7},{24,8},{25... | collective-permute-start | bytes 3145736 | tf_op jit(solution)/shard_map/ppermute | solution.py:591
  346.7 14.9 %collective-permute-start.29 = (bf16[96,512]{1,0:T(8,128)(2,1)S(1)}, bf16[96,512]{1,0:T(8,128)(2,1)S(1)}, u32[]{:S(2)}, u32[]{:S(2)}) collective-permute-start(bf16[96,512]{1,0:T(8,128)(2,1)S(1)} %fusion.17), channel_id=1, source_target_pairs={{16,0},{17,1},{18,2},{19,3},{20,4},{21,5},{22,6},{23,7},{24,8},{25... | collective-permute-start | bytes 294920 | tf_op jit(solution)/shard_map/ppermute | solution.py:591
  (48 other events, 482.4 us)
Sparse Core Ops, SparseCore 0:
  25.7 73.9 all-gather.4
  101.9 57.8 all-gather.6
  207.5 74.9 reduce-scatter.2
  286.3 74.6 reduce-scatter.4

commit v4 on v3

--- a/solution.py
+++ b/solution.py
@@ -8,7 +8,7 @@
 from jax.sharding import PartitionSpec as P
 
 HD = 64
-ROWS = 256
+ROWS = 512
 bf16 = jnp.bfloat16
 f32 = jnp.float32
 root_term = 0.7978845608
@@ -712,6 +712,69 @@
     return jnp.stack([first, second]) / gains
 
 
+def finish_kernel(place, own0, got0, own1, got1, own2, got2, own3, got3, w_qkv, w_gates, w_up, gains,
+                  g_qkv, g_out, g_gates, g_up, g_down, g_gains, g_biases):
+    width = own0.shape[1]
+    first = place[3] == 0
+
+    def total(start, stop):
+        early = own0[start:stop, :] + got0[start:stop, :].astype(f32), own1[start:stop, :] + got1[start:stop, :].astype(f32)
+        return jnp.where(first, *early)
+
+    def rest(start, stop):
+        return jnp.where(
+            first,
+            own2[start:stop, :].astype(f32) + got2[start:stop, :].astype(f32),
+            own3[start:stop, :].astype(f32) + got3[start:stop, :].astype(f32),
+        )
+
+    def against_weight(weight, grad):
+        return jnp.sum(weight.astype(bf16).astype(f32) * grad, axis=1, keepdims=True)
+
+    rows = lax.broadcasted_iota(jnp.int32, (UNIT, UNIT), 0)
+    diagonal = rows == lax.broadcasted_iota(jnp.int32, (UNIT, UNIT), 1)
+    lines = [None, None]
+    for at in range(2):
+        part = rest((1 + at) * UNIT, (2 + at) * UNIT)
+        g_gates[0, at] = part
+        lines[at] = against_weight(w_gates[0, at], part)
+    for at in range(3):
+        cut = slice(at * width, at * width + width)
+        part = total(at * UNIT, (at + 1) * UNIT)
+        g_qkv[0, :, cut] = part
+        lines[0] += against_weight(w_qkv[0, :, cut], part)
+    for at in range(4):
+        cut = slice(at * width, at * width + width)
+        part = rest((3 + at) * UNIT, (4 + at) * UNIT)
+        g_up[0, :, cut] = part
+        lines[1] += against_weight(w_up[0, :, cut], part)
+    g_out[0] = rest(0, UNIT)
+    g_down[0] = rest(7 * UNIT, REST)
+    sums = rest(REST, REST + 16)
+    index = (place[0] * 2 + place[1]) * 2 + place[2]
+    for at in range(2):
+        line = jnp.sum(jnp.where(diagonal, lines[at], 0.0), axis=0, keepdims=True)
+        g_gains[0, at : at + 1, :] = line / gains[0, at : at + 1, :].astype(bf16).astype(f32)
+        mine = jnp.zeros((1, UNIT), f32)
+        for part in range(PARTS):
+            mine = jnp.where(index == part, sums[at : at + 1, part * UNIT : (part + 1) * UNIT], mine)
+        g_biases[0, at : at + 1, :] = mine
+
+
+def finish(place, sums, masters):
+    w_qkv, w_out, w_gates, w_up, w_down, gains, biases = masters
+    inputs = (*sums, w_qkv, w_gates, w_up, gains)
+    shapes = [struct(master.shape, f32) for master in (w_qkv, w_out, w_gates, w_up, w_down, gains, biases)]
+    return call(
+        finish_kernel,
+        (1,),
+        [whole(*value.shape) for value in inputs],
+        [whole(*shape.shape) for shape in shapes],
+        shapes,
+        moved=6_000_000,
+    )(place, *inputs)
+
+
 def per_device(tokens, cotangent, w_qkv, w_out, w_gates, w_up, w_down, norm_gains, gate_biases):
     section = lax.axis_index("section")
     index = lax.axis_index("dp")
@@ -726,7 +789,7 @@
     seeds = [cotangent[0, m, 0] for m in range(2)]
     own_seed, other_seed = jnp.where(first, seeds[0], seeds[1]), jnp.where(first, seeds[1], seeds[0])
     if fast:
-        y0, y1, theirs, dxs, lows, grads = run(x, own_seed, other_seed, masters, index, first, pick)
+        y0, y1, theirs, dxs, lows, grads = run(x, own_seed, other_seed, masters, index, section, pick)
     else:
         place = jnp.zeros((3,), jnp.int32)
         heads, rest = weights_whole(*masters)
@@ -749,19 +812,21 @@
         dxs, lows = (dx0, dx1), (crossed(low0, (1,)), crossed(low1, (0,)))
         theirs = crossed(jnp.where(first, y1, y0))
         grads = [jnp.where(first, *pair) for pair in zip(grads0, grads1)]
+        grads.insert(5, gain_grads(grads, w_qkv, w_gates, w_up, norm_gains))
+        grads = [grad[None] for grad in grads]
 
     mine = jnp.where(first, y0, y1)
     block = jnp.stack([jnp.where(first, mine, theirs), jnp.where(first, theirs, mine)])[None, :, None]
     in_grads = jnp.stack([jnp.where(first, dxs[0], lows[1].astype(f32)), dxs[1]])
     last = jnp.where(first, lows[0].astype(f32), dxs[1])
     in_grads = lax.dynamic_update_slice(in_grads, last[None], (1, 0, 0))[None, :, None]
-    grads.insert(5, gain_grads(grads, w_qkv, w_gates, w_up, norm_gains))
-    return (block, in_grads, *(grad[None] for grad in grads))
-
-
-def run(x, own_seed, other_seed, masters, index, first, pick):
+    return (block, in_grads, *grads)
+
+
+def run(x, own_seed, other_seed, masters, index, section, pick):
+    first = section == 0
     width = x.shape[1]
-    place = jnp.stack([index // 4, (index // 2) & 1, index & 1]).astype(jnp.int32)
+    place = jnp.stack([index // 4, (index // 2) & 1, index & 1, section]).astype(jnp.int32)
     head, tail = pack(place, index, *masters)
     heads = pick(head, crossed(head))
     tails = pick(tail, crossed(tail))
@@ -794,13 +859,13 @@
     y1, dm, dza, do, keep, send = turn(place, y0, n1, o, seeds[1], vec, tail1)
     got = swapped(send, 1)
     theirs = crossed(jnp.where(first, y1, y0))
-    dqkv = attend_back(place, q, k, v, o, s, do, 0)
+    dqkv = attend_back(place, q, k, v, o, s, do, 0, 1)
     rest1 = scattered(keep, after(got, dqkv[0]))
-    dqkv = attend_back(place, q, k, v, o, s, do, 2, onto=dqkv)
+    dqkv = attend_back(place, q, k, v, o, s, do, 1, 3, onto=dqkv)
     keep_b, send_b = first_grad(place, (n1, *dqkv))
     got_b = swapped(send_b, 1)
     dx1, low1, dm, dza, do, keep, send = joint_back(
-        place, y0, dm, dqkv, dza, vec, head1, tail1, seeds[0], kept0, tail0, waits=(keep_b,)
+        place, y0, dm, dqkv, dza, vec, head1, tail1, seeds[0], kept0, tail0, waits=(keep_b, theirs)
     )
     n1, o, vec = kept0[:3]
     q, k, v, o, s = layer0
@@ -809,38 +874,27 @@
     got_b = swapped(away, 2)
     other1 = crossed(low1, (0,))
     dqkv = attend_back(place, q, k, v, o, s, do, 0, 1, waits=(away,))
-    rest1 = after(rest1, dqkv[0])
     rest0 = scattered(keep, after(got, dqkv[0]))
+    dqkv = attend_back(place, q, k, v, o, s, do, 1, 3, onto=dqkv)
     own, sends = fold_y(near, after(got_b, dqkv[0]))
     gots = [moved_z(part, at + 1) for at, part in enumerate(sends)]
-    dqkv = attend_back(place, q, k, v, o, s, do, 1, 3, onto=dqkv, waits=(theirs, *sends))
-    early1 = fold_z(own, [after(got, dqkv[0]) for got in gots])
-    low = jnp.concatenate([rest1, early1.astype(bf16)])
-    last1 = crossed(low, (0,))
-    keep, send = first_grad(place, (n1, *dqkv), waits=(other1, low))
+    keep, send = first_grad(place, (n1, *dqkv), waits=(other1, *sends))
     got = swapped(send, 1)
     away, near = fold_core(keep, got)
     got = swapped(away, 2)
     dx0, low0 = qkv_back(place, x, dm, *dqkv, dza, vec, head0, tail0, waits=(away,))
-    last1 = after(last1, low0).astype(f32)
-    rest1, early1 = rest1.astype(f32) + last1[: REST + 16], early1 + last1[REST + 16 :]
+    early1 = fold_z(own, [after(part, low0) for part in gots])
+    rest1 = after(rest1, low0)
+    last1 = crossed(jnp.concatenate([rest1, early1.astype(bf16)]), (0,))
     other0 = crossed(low0, (1,))
     own, sends = fold_y(near, after(got, low0))
     gots = [moved_z(part, at + 1) for at, part in enumerate(sends)]
     early0 = fold_z(own, gots)
-    early0 = early0 + crossed(early0.astype(bf16), (1,)).astype(f32)
-    early = jnp.where(first, early0, early1)
-    rest0 = after(rest0, gots[0])
-    rest0 = rest0.astype(f32) + crossed(rest0, (1,)).astype(f32)
-    later = jnp.where(first, rest0, rest1)
-    grads = [
-        jnp.concatenate([early[at * UNIT : (at + 1) * UNIT] for at in range(3)], axis=1),
-        later[:UNIT],
-        later[UNIT : 3 * UNIT].reshape(2, UNIT, width),
-        jnp.concatenate([later[(3 + at) * UNIT : (4 + at) * UNIT] for at in range(4)], axis=1),
-        later[7 * UNIT : REST],
-        lax.dynamic_slice(later, (REST, index * UNIT), (2, UNIT)),
-    ]
+    last0 = crossed(early0.astype(bf16), (1,))
+    rest0 = after(rest0, last0, last1, other0)
+    later0 = crossed(rest0, (1,))
+    sums = (early0, last0, early1, last1[REST + 16 :], rest0, later0, rest1, last1[: REST + 16])
+    grads = finish(place, sums, masters)
     return y0, y1, theirs, (dx0, dx1), (other0, other1), grads
 
 

time: 394 us -> 388 us (0.985)
  other arithmetic: 34.8 us -> 29.7 us
    pallas_call x17 -> x18, Pallas kernels: 207 us -> 207 us  [run(): pl.pallas_call(body, grid_spec=pltpu.PrefetchScalarGridSpec(num_scalar_pr...]
  transfers between devices with their start and end apart: 37 -> 37, of which waited for: 17 -> 16; matrix products, arithmetic and copies ran while one was open for 7% -> 8% of each run, Pallas kernels for 44% -> 45%
where the time goes in v4:
time: 388 us; the launch traced here: 381 us
  Pallas kernels  207 us (53%)
  waiting for transfers between devices  76.1 us (20%)
  starting transfers between devices  44 us (11%)
  other arithmetic  29.7 us (8%)
  between operations  14.5 us (4%)
  local copies, waits for them, and re-layouts  9.46 us (2%)
    pallas_call x18, Pallas kernels, run(): pl.pallas_call(body, grid_spec=pltpu.PrefetchScalarGridSpec(num_scalar_pr...  207 us
    ppermute x9, waiting for transfers between devices, crossed(): return lax.ppermute(value, 'section', [(s, 1 - s) for s in sources])  28.9 us
    ppermute x12, waiting for transfers between devices, moved_z(): lax.ppermute(value, 'dp', [(d, (d + 4 * steps) % count) for d in range(co...  20.9 us
    ppermute x9, starting transfers between devices, crossed(): return lax.ppermute(value, 'section', [(s, 1 - s) for s in sources])  19.1 us
    ppermute x12, starting transfers between devices, moved_z(): lax.ppermute(value, 'dp', [(d, (d + 4 * steps) % count) for d in range(co...  18.8 us
    ppermute x12, waiting for transfers between devices, swapped(): lax.ppermute(value, 'dp', [(d, d ^ bit) for d in range(lax.axis_size('dp'...  15.1 us
    all_gather x1, waiting for transfers between devices, run(): tail1 = lax.all_gather(after(tails[1], tail0), 'dp', axis=0)  9.53 us
  transfers between devices with their start and end apart: 37, of which 16 were waited for; matrix products, arithmetic and copies ran while one was open for 8% of the time, Pallas kernels for 45%

profile of v4, /device:TPU:0, one launch (start us, length us, event | category | flops | bytes accessed | tf_op | source)
XLA Modules:
  0.0 380.7 jit_solution(8647058207154016379)
XLA Ops:
  15.1 8.6 %collective-permute-done.10 = bf16[352,512]{1,0:T(8,128)(2,1)S(1)} collective-permute-done((bf16[352,512]{1,0:T(8,128)(2,1)}, bf16[352,512]{1,0:T(8,128)(2,1)S(1)}, u32[]{:S(2)}, u32[]{:S(2)}) %collective-permute-start.10) | collective-permute-done | bytes 360480 | tf_op jit(solution)/shard_map/ppermute | solution.py:591
  40.9 10.7 %collective-permute-done.2 = bf16[112,512]{1,0:T(8,128)(2,1)S(1)} collective-permute-done((bf16[112,512]{1,0:T(8,128)(2,1)S(1)}, bf16[112,512]{1,0:T(8,128)(2,1)S(1)}, u32[]{:S(2)}, u32[]{:S(2)}) %collective-permute-start.2) | collective-permute-done | bytes 114720 | tf_op jit(solution)/shard_map/ppermute | solution.py:583
  53.2 7.1 %collective-permute-done.4.refs_3_.refs_10_ = bf16[4,112,512]{2,1,0:T(8,128)(2,1)S(1)} collective-permute-done((bf16[4,112,512]{2,1,0:T(8,128)(2,1)S(1)}, bf16[4,112,512]{2,1,0:T(8,128)(2,1)S(1)}, u32[]{:S(2)}, u32[]{:S(2)}) %collective-permute-start.4) | collective-permute-done | bytes 458784 | tf_op jit(solution)/shard_map/ppermute | solution.py:587
  68.9 6.6 %shard_map.161 = (bf16[1024,512]{1,0:T(8,128)(2,1)}, bf16[1024,512]{1,0:T(8,128)(2,1)}, bf16[1024,512]{1,0:T(8,128)(2,1)}, bf16[1024,512]{1,0:T(8,128)(2,1)}, f32[16,512]{1,0:T(8,128)}) custom-call(s32[4]{0:T(128)} %pad_add_fusion.refs_0_, bf16[1024,512]{1,0:T(8,128)(2,1)} %select_bitcast_fusion.4.refs_1_, bf16[4,112,512]{2,1,0:T(8,128)(2,1)} %copy-done.9, ...), custom_call_target="tpu_custom_call" | custom-call | flops 1610612736 | bytes 8000000 | tf_op jit(solution)/shard_map/pallas_call | solution.py:72
  75.6 9.3 %shard_map.162 = (bf16[1024,512]{1,0:T(8,128)(2,1)}, f32[1024,512]{1,0:T(8,128)}) custom-call(s32[4]{0:T(128)} %pad_add_fusion.refs_0_, bf16[1024,512]{1,0:T(8,128)(2,1)} %get-tuple-element.99.refs_1_, bf16[1024,512]{1,0:T(8,128)(2,1)} %get-tuple-element.100.refs_2_, bf16[1024,512]{1,0:T(8,128)(2,1)} %get-tuple-element.101.refs_3_), custom_call_target="tpu_custom_call" | custom-call | flops 6000000000 | bytes 3000000 | tf_op jit(solution)/shard_map/pallas_call | solution.py:72
  89.3 9.4 %shard_map.163 = (bf16[1024,512]{1,0:T(8,128)(2,1)}, f32[1024,512]{1,0:T(8,128)}) custom-call(s32[4]{0:T(128)} %pad_add_fusion.refs_0_, bf16[1024,512]{1,0:T(8,128)(2,1)} %get-tuple-element.99.refs_1_, bf16[1024,512]{1,0:T(8,128)(2,1)} %get-tuple-element.100.refs_2_, ...), custom_call_target="tpu_custom_call", output_to_operand_aliasing={{0}: (4, {}), {1}: (5, {})} | custom-call | flops 6000000000 | bytes 3000000 | tf_op jit(solution)/shard_map/pallas_call | solution.py:72
  101.7 17.7 %shard_map.164 = (bf16[1024,512]{1,0:T(8,128)(2,1)}, bf16[1024,512]{1,0:T(8,128)(2,1)}, f32[1024,128]{1,0:T(8,128)}, bf16[1024,512]{1,0:T(8,128)(2,1)}, bf16[102...) custom-call(s32[4]{0:T(128)} %pad_add_fusion.refs_0_, ...), custom_call_target="tpu_custom_call" | custom-call | flops 5905580032 | bytes 24000000 | tf_op jit(solution)/shard_map/pallas_call | solution.py:72
  123.3 6.6 %shard_map.165 = (bf16[1024,512]{1,0:T(8,128)(2,1)}, bf16[1024,512]{1,0:T(8,128)(2,1)}, bf16[1024,512]{1,0:T(8,128)(2,1)}, bf16[1024,512]{1,0:T(8,128)(2,1)}, f32[16,512]{1,0:T(8,128)}) custom-call(s32[4]{0:T(128)} %pad_add_fusion.refs_0_, bf16[1024,512]{1,0:T(8,128)(2,1)} %get-tuple-element.113.refs_1_, ...), custom_call_target="tpu_custom_call" | custom-call | flops 1610612736 | bytes 8000000 | tf_op jit(solution)/shard_map/pallas_call | solution.py:72
  130.0 9.3 %shard_map.166 = (bf16[1024,512]{1,0:T(8,128)(2,1)}, f32[1024,512]{1,0:T(8,128)}) custom-call(s32[4]{0:T(128)} %pad_add_fusion.refs_0_, bf16[1024,512]{1,0:T(8,128)(2,1)} %get-tuple-element.117.refs_1_, bf16[1024,512]{1,0:T(8,128)(2,1)} %get-tuple-element.118.refs_2_, bf16[1024,512]{1,0:T(8,128)(2,1)} %get-tuple-element.119.refs_3_), custom_call_target="tpu_custom_call" | custom-call | flops 6000000000 | bytes 3000000 | tf_op jit(solution)/shard_map/pallas_call | solution.py:72
  139.3 9.7 %shard_map.167 = (bf16[1024,512]{1,0:T(8,128)(2,1)}, f32[1024,512]{1,0:T(8,128)}) custom-call(s32[4]{0:T(128)} %pad_add_fusion.refs_0_, bf16[1024,512]{1,0:T(8,128)(2,1)} %get-tuple-element.117.refs_1_, bf16[1024,512]{1,0:T(8,128)(2,1)} %get-tuple-element.118.refs_2_, ...), custom_call_target="tpu_custom_call", output_to_operand_aliasing={{0}: (4, {}), {1}: (5, {})} | custom-call | flops 6000000000 | bytes 3000000 | tf_op jit(solution)/shard_map/pallas_call | solution.py:72
  150.5 9.5 %all-gather.7.cloned.1.call-done = bf16[5632,512]{1,0:T(8,128)(2,1)} async-done(((bf16[352,512]{1,0:T(8,128)(2,1)}), bf16[5632,512]{1,0:T(8,128)(2,1)}) %all-gather.7.cloned.1.call-update) | async-done | bytes 5767184 | tf_op jit(solution)/shard_map/all_gather | solution.py:848
  160.0 30.0 %shard_map.168 = (bf16[1024,512]{1,0:T(8,128)(2,1)}, f32[1024,512]{1,0:T(8,128)}, bf16[1024,512]{1,0:T(8,128)(2,1)}, bf16[1024,512]{1,0:T(8,128)(2,1)}, bf16[8,3...) custom-call(s32[4]{0:T(128)} %pad_add_fusion.refs_0_, bf16[1024,512]{1,0:T(8,128)(2,1)} %get-tuple-element.113.refs_1_, ...), custom_call_target="tpu_custom_call" | custom-call | flops 17716740096 | bytes 24000000 | tf_op jit(solution)/shard_map/pallas_call | solution.py:72
  192.1 7.6 %shard_map.169 = (bf16[1024,512]{1,0:T(8,128)(2,1)}, bf16[1024,512]{1,0:T(8,128)(2,1)}, bf16[1024,512]{1,0:T(8,128)(2,1)}) custom-call(s32[4]{0:T(128)} %pad_add_fusion.refs_0_, bf16[1024,512]{1,0:T(8,128)(2,1)} %get-tuple-element.117.refs_1_, bf16[1024,512]{1,0:T(8,128)(2,1)} %get-tuple-element.118.refs_2_, bf16[1024,512]{1,0:T(8,128)(2,1)} %get-tuple-element.119.refs_3_, ...), custom_call_target="tpu_custom_call" | custom-call | flops 5000000000 | bytes 5000000 | tf_op jit(solution)/shard_map/pallas_call | solution.py:72
  204.0 16.5 %shard_map.170 = (bf16[1024,512]{1,0:T(8,128)(2,1)}, bf16[1024,512]{1,0:T(8,128)(2,1)}, bf16[1024,512]{1,0:T(8,128)(2,1)}) custom-call(s32[4]{0:T(128)} %pad_add_fusion.refs_0_, bf16[1024,512]{1,0:T(8,128)(2,1)} %get-tuple-element.117.refs_1_, ...), custom_call_target="tpu_custom_call", output_to_operand_aliasing={{0}: (7, {}), {1}: (8, {}), {2}: (9, {})} | custom-call | flops 15000000512 | bytes 5000000 | tf_op jit(solution)/shard_map/pallas_call | solution.py:72
  220.6 6.4 %shard_map.171 = (bf16[2,4,96,512]{3,2,1,0:T(8,128)(2,1)}, bf16[2,4,96,512]{3,2,1,0:T(8,128)(2,1)}) custom-call(s32[4]{0:T(128)} %pad_add_fusion.refs_0_, bf16[1024,512]{1,0:T(8,128)(2,1)} %get-tuple-element.116.refs_2_.refs_7_.refs_1_, bf16[1024,512]{1,0:T(8,128)(2,1)} %get-tuple-element.134.refs_2_.refs_3_, ...), custom_call_target="tpu_custom_call" | custom-call | flops 1610612736 | bytes 9000000 | tf_op jit(solution)/shard_map/pallas_call | solution.py:72
  228.0 30.6 %shard_map.172 = (f32[1024,512]{1,0:T(8,128)}, bf16[1024,512]{1,0:T(8,128)(2,1)}, f32[1024,512]{1,0:T(8,128)}, bf16[1024,512]{1,0:T(8,128)(2,1)}, bf16[1024,512]...) custom-call(s32[4]{0:T(128)} %pad_add_fusion.refs_0_, ...), custom_call_target="tpu_custom_call" | custom-call | flops 13958643712 | bytes 40000000 | tf_op jit(solution)/shard_map/pallas_call | solution.py:72
  259.2 5.8 %collective-permute-done.16 = bf16[2,4,96,512]{3,2,1,0:T(8,128)(2,1)S(1)} collective-permute-done((bf16[2,4,96,512]{3,2,1,0:T(8,128)(2,1)S(1)}, bf16[2,4,96,512]{3,2,1,0:T(8,128)(2,1)S(1)}, u32[]{:S(2)}, u32[]{:S(2)}) %collective-permute-start.16) | collective-permute-done | bytes 786464 | tf_op jit(solution)/shard_map/ppermute | solution.py:587
  265.9 7.7 %shard_map.173 = (bf16[1024,512]{1,0:T(8,128)(2,1)}, bf16[1024,512]{1,0:T(8,128)(2,1)}, bf16[1024,512]{1,0:T(8,128)(2,1)}) custom-call(s32[4]{0:T(128)} %pad_add_fusion.refs_0_, bf16[1024,512]{1,0:T(8,128)(2,1)} %get-tuple-element.99.refs_1_, bf16[1024,512]{1,0:T(8,128)(2,1)} %get-tuple-element.100.refs_2_, bf16[1024,512]{1,0:T(8,128)(2,1)} %get-tuple-element.101.refs_3_, ...), custom_call_target="tpu_custom_call" | custom-call | flops 5000000000 | bytes 5000000 | tf_op jit(solution)/shard_map/pallas_call | solution.py:72
  280.6 16.3 %shard_map.174 = (bf16[1024,512]{1,0:T(8,128)(2,1)}, bf16[1024,512]{1,0:T(8,128)(2,1)}, bf16[1024,512]{1,0:T(8,128)(2,1)}) custom-call(s32[4]{0:T(128)} %pad_add_fusion.refs_0_, bf16[1024,512]{1,0:T(8,128)(2,1)} %get-tuple-element.99.refs_1_, ...), custom_call_target="tpu_custom_call", output_to_operand_aliasing={{0}: (7, {}), {1}: (8, {}), {2}: (9, {})} | custom-call | flops 15000000512 | bytes 5000000 | tf_op jit(solution)/shard_map/pallas_call | solution.py:72
  297.8 5.4 %collective-permute-done.17.refs_5_ = bf16[1024,512]{1,0:T(8,128)(2,1)S(1)} collective-permute-done((bf16[1024,512]{1,0:T(8,128)(2,1)}, bf16[1024,512]{1,0:T(8,128)(2,1)S(1)}, u32[]{:S(2)}, u32[]{:S(2)}) %collective-permute-start.17) | collective-permute-done | bytes 1048608 | tf_op jit(solution)/shard_map/ppermute | solution.py:591
  304.2 6.5 %shard_map.175 = (bf16[2,4,96,512]{3,2,1,0:T(8,128)(2,1)}, bf16[2,4,96,512]{3,2,1,0:T(8,128)(2,1)}) custom-call(s32[4]{0:T(128)} %pad_add_fusion.refs_0_, bf16[1024,512]{1,0:T(8,128)(2,1)} %get-tuple-element.98.refs_2_.refs_18_.refs_1_, bf16[1024,512]{1,0:T(8,128)(2,1)} %get-tuple-element.156.refs_2_.refs_3_, ...), custom_call_target="tpu_custom_call" | custom-call | flops 1610612736 | bytes 9000000 | tf_op jit(solution)/shard_map/pallas_call | solution.py:72
  317.4 9.6 %shard_map.176 = (f32[1024,512]{1,0:T(8,128)}, bf16[1024,512]{1,0:T(8,128)(2,1)}) custom-call(s32[4]{0:T(128)} %pad_add_fusion.refs_0_, bf16[1024,512]{1,0:T(8,128)(2,1)} %select_bitcast_fusion.4.refs_1_, f32[1024,512]{1,0:T(8,128)} %get-tuple-element.147.refs_2_, bf16[1024,512]{1,0:T(8,128)(2,1)} %get-tuple-element.156.refs_2_.refs_3_, ...), custom_call_target="tpu_custom_call" | custom-call | flops 2147483648 | bytes 12000000 | tf_op jit(solution)/shard_map/pallas_call | solution.py:72
  349.7 6.4 %collective-permute-done.25.refs_2_ = bf16[96,512]{1,0:T(8,128)(2,1)S(1)} collective-permute-done((bf16[96,512]{1,0:T(8,128)(2,1)S(1)}, bf16[96,512]{1,0:T(8,128)(2,1)S(1)}, u32[]{:S(2)}, u32[]{:S(2)}) %collective-permute-start.25) | collective-permute-done | bytes 98336 | tf_op jit(solution)/shard_map/ppermute | solution.py:591
  363.6 5.2 %collective-permute-done.32.refs_6_ = bf16[368,512]{1,0:T(8,128)(2,1)S(1)} collective-permute-done((bf16[368,512]{1,0:T(8,128)(2,1)}, bf16[368,512]{1,0:T(8,128)(2,1)S(1)}, u32[]{:S(2)}, u32[]{:S(2)}) %collective-permute-start.32) | collective-permute-done | bytes 376864 | tf_op jit(solution)/shard_map/ppermute | solution.py:591
  (165 shorter events, 107.5 us)
Async XLA Ops:
  7.2 92.5 %all-gather.5.cloned.1.call-start = ((), (), s32[]{:S(2)}) async-start(), calls=%async_computation.4 | async-start | bytes 6127616 | tf_op jit(solution)/shard_map/all_gather | solution.py:833
  12.2 11.6 %collective-permute-start.10 = (bf16[352,512]{1,0:T(8,128)(2,1)}, bf16[352,512]{1,0:T(8,128)(2,1)S(1)}, u32[]{:S(2)}, u32[]{:S(2)}) collective-permute-start(bf16[352,512]{1,0:T(8,128)(2,1)} %get-tuple-element.111), channel_id=1, source_target_pairs={{0,16},{16,0},{1,17},{17,1},{2,18},{18,2},{3,19},{19,3},{4,20},{20... | collective-permute-start | bytes 1081352 | tf_op jit(solution)/shard_map/ppermute | solution.py:591
  25.6 134.4 %all-gather.7.cloned.1.call-start = ((), (), s32[]{:S(2)}) async-start(), calls=%async_computation.5 | async-start | bytes 6127616 | tf_op jit(solution)/shard_map/all_gather | solution.py:848
  35.6 16.1 %collective-permute-start.2 = (bf16[112,512]{1,0:T(8,128)(2,1)S(1)}, bf16[112,512]{1,0:T(8,128)(2,1)S(1)}, u32[]{:S(2)}, u32[]{:S(2)}) collective-permute-start(bf16[112,512]{1,0:T(8,128)(2,1)S(1)} %get-tuple-element.215), channel_id=1, source_target_pairs={{0,8},{1,9},{2,10},{3,11},{4,12},{5,13},{6,14},{7,15},{8,0},{9,1},... | collective-permute-start | bytes 344072 | tf_op jit(solution)/shard_map/ppermute | solution.py:583
  35.6 16.1 %collective-permute-start.1 = (bf16[112,512]{1,0:T(8,128)(2,1)S(1)}, bf16[112,512]{1,0:T(8,128)(2,1)S(1)}, u32[]{:S(2)}, u32[]{:S(2)}) collective-permute-start(bf16[112,512]{1,0:T(8,128)(2,1)S(1)} %get-tuple-element.215), channel_id=1, source_target_pairs={{0,4},{1,5},{2,6},{3,7},{4,8},{5,9},{6,10},{7,11},{8,12},{9,13},{1... | collective-permute-start | bytes 344072 | tf_op jit(solution)/shard_map/ppermute | solution.py:583
  53.2 14.2 %collective-permute-start.5 = (bf16[4,112,512]{2,1,0:T(8,128)(2,1)S(1)}, bf16[4,112,512]{2,1,0:T(8,128)(2,1)S(1)}, u32[]{:S(2)}, u32[]{:S(2)}) collective-permute-start(bf16[4,112,512]{2,1,0:T(8,128)(2,1)S(1)} %pad_maximum_fusion.1.refs_2_.refs_9_), channel_id=1, source_target_pairs={{0,1},{1,0},{2,3},{3,2},{4,5},{5,4},{6,7},{7,6},{8,9},{9,8},{10,11... | collective-permute-start | bytes 1376264 | tf_op jit(solution)/shard_map/ppermute | solution.py:587
  61.4 23.4 %collective-permute-start.9 = (bf16[112,512]{1,0:T(8,128)(2,1)S(1)}, bf16[112,512]{1,0:T(8,128)(2,1)S(1)}, u32[]{:S(2)}, u32[]{:S(2)}) collective-permute-start(bf16[112,512]{1,0:T(8,128)(2,1)S(1)} %get-tuple-element.105), channel_id=1, source_target_pairs={{0,12},{1,13},{2,14},{3,15},{4,0},{5,1},{6,2},{7,3},{8,4},{9,5},{1... | collective-permute-start | bytes 344072 | tf_op jit(solution)/shard_map/ppermute | solution.py:583
  61.4 27.0 %collective-permute-start.8 = (bf16[112,512]{1,0:T(8,128)(2,1)S(1)}, bf16[112,512]{1,0:T(8,128)(2,1)S(1)}, u32[]{:S(2)}, u32[]{:S(2)}) collective-permute-start(bf16[112,512]{1,0:T(8,128)(2,1)S(1)} %get-tuple-element.105), channel_id=1, source_target_pairs={{0,8},{1,9},{2,10},{3,11},{4,12},{5,13},{6,14},{7,15},{8,0},{9,1},... | collective-permute-start | bytes 344072 | tf_op jit(solution)/shard_map/ppermute | solution.py:583
  65.3 23.1 %collective-permute-start.7 = (bf16[112,512]{1,0:T(8,128)(2,1)S(1)}, bf16[112,512]{1,0:T(8,128)(2,1)S(1)}, u32[]{:S(2)}, u32[]{:S(2)}) collective-permute-start(bf16[112,512]{1,0:T(8,128)(2,1)S(1)} %get-tuple-element.105), channel_id=1, source_target_pairs={{0,4},{1,5},{2,6},{3,7},{4,8},{5,9},{6,10},{7,11},{8,12},{9,13},{1... | collective-permute-start | bytes 344072 | tf_op jit(solution)/shard_map/ppermute | solution.py:583
  99.7 235.4 %reduce-scatter.3.cloned.1.call-start = ((), (), s32[]{:S(2)}) async-start(), calls=%async_computation.2 | async-start | bytes 3391488 | tf_op jit(solution)/shard_map/reduce_scatter | solution.py:660
  100.0 19.5 %collective-permute-start.11 = (bf16[4,112,512]{2,1,0:T(8,128)(2,1)S(1)}, bf16[4,112,512]{2,1,0:T(8,128)(2,1)S(1)}, u32[]{:S(2)}, u32[]{:S(2)}) collective-permute-start(bf16[4,112,512]{2,1,0:T(8,128)(2,1)S(1)} %copy-done.16), channel_id=1, source_target_pairs={{0,2},{1,3},{2,0},{3,1},{4,6},{5,7},{6,4},{7,5},{8,10},{9,11},{10,... | collective-permute-start | bytes 1376264 | tf_op jit(solution)/shard_map/ppermute | solution.py:587
  120.1 28.8 %collective-permute-start.14 = (bf16[1024,512]{1,0:T(8,128)(2,1)S(1)}, bf16[1024,512]{1,0:T(8,128)(2,1)S(1)}, u32[]{:S(2)}, u32[]{:S(2)}) collective-permute-start(bf16[1024,512]{1,0:T(8,128)(2,1)S(1)} %select_bitcast_fusion.3), channel_id=1, source_target_pairs={{0,16},{16,0},{1,17},{17,1},{2,18},{18,2},{3,19},{19,3},{4,20},{20... | collective-permute-start | bytes 3145736 | tf_op jit(solution)/shard_map/ppermute | solution.py:591
  191.8 35.2 %collective-permute-start.15 = (bf16[1024,512]{1,0:T(8,128)(2,1)S(1)}, bf16[1024,512]{1,0:T(8,128)(2,1)S(1)}, u32[]{:S(2)}, u32[]{:S(2)}) collective-permute-start(bf16[1024,512]{1,0:T(8,128)(2,1)S(1)} %broadcast_select_fusion.1), channel_id=1, source_target_pairs={{0,16},{16,0},{1,17},{17,1},{2,18},{18,2},{3,19},{19,3},{4,20},{20... | collective-permute-start | bytes 3145736 | tf_op jit(solution)/shard_map/ppermute | solution.py:591
  204.0 152.7 %reduce-scatter.5.cloned.1.call-start = ((), (), s32[]{:S(2)}) async-start(), calls=%async_computation.3 | async-start | bytes 3391488 | tf_op jit(solution)/shard_map/reduce_scatter | solution.py:660
  258.7 14.9 %collective-permute-start.31 = (bf16[8,368,512]{2,1,0:T(8,128)(2,1)}, bf16[8,368,512]{2,1,0:T(8,128)(2,1)S(1)}, u32[]{:S(2)}, u32[]{:S(2)}) collective-permute-start(bf16[8,368,512]{2,1,0:T(8,128)(2,1)} %get-tuple-element.175), channel_id=1, source_target_pairs={{0,1},{1,0},{2,3},{3,2},{4,5},{5,4},{6,7},{7,6},{8,9},{9,8},{10,11... | collective-permute-start | bytes 9043976 | tf_op jit(solution)/shard_map/ppermute | solution.py:587
  276.1 27.1 %collective-permute-start.17 = (bf16[1024,512]{1,0:T(8,128)(2,1)}, bf16[1024,512]{1,0:T(8,128)(2,1)S(1)}, u32[]{:S(2)}, u32[]{:S(2)}) collective-permute-start(bf16[1024,512]{1,0:T(8,128)(2,1)} %get-tuple-element.151), channel_id=1, source_target_pairs={{0,16},{1,17},{2,18},{3,19},{4,20},{5,21},{6,22},{7,23},{8,24},{9,... | collective-permute-start | bytes 3145736 | tf_op jit(solution)/shard_map/ppermute | solution.py:591
  280.0 16.9 %collective-permute-start.18 = (bf16[4,96,512]{2,1,0:T(8,128)(2,1)S(1)}, bf16[4,96,512]{2,1,0:T(8,128)(2,1)S(1)}, u32[]{:S(2)}, u32[]{:S(2)}) collective-permute-start(bf16[4,96,512]{2,1,0:T(8,128)(2,1)S(1)} %copy-done.20), channel_id=1, source_target_pairs={{0,2},{1,3},{2,0},{3,1},{4,6},{5,7},{6,4},{7,5},{8,10},{9,11},{10,... | collective-permute-start | bytes 1179656 | tf_op jit(solution)/shard_map/ppermute | solution.py:587
  312.5 15.9 %collective-permute-start.28 = (bf16[96,512]{1,0:T(8,128)(2,1)S(1)}, bf16[96,512]{1,0:T(8,128)(2,1)S(1)}, u32[]{:S(2)}, u32[]{:S(2)}) collective-permute-start(bf16[96,512]{1,0:T(8,128)(2,1)S(1)} %copy-done.25), channel_id=1, source_target_pairs={{0,12},{1,13},{2,14},{3,15},{4,0},{5,1},{6,2},{7,3},{8,4},{9,5},{1... | collective-permute-start | bytes 294920 | tf_op jit(solution)/shard_map/ppermute | solution.py:583
  314.5 13.9 %collective-permute-start.27 = (bf16[96,512]{1,0:T(8,128)(2,1)S(1)}, bf16[96,512]{1,0:T(8,128)(2,1)S(1)}, u32[]{:S(2)}, u32[]{:S(2)}) collective-permute-start(bf16[96,512]{1,0:T(8,128)(2,1)S(1)} %copy-done.24), channel_id=1, source_target_pairs={{0,8},{1,9},{2,10},{3,11},{4,12},{5,13},{6,14},{7,15},{8,0},{9,1},... | collective-permute-start | bytes 294920 | tf_op jit(solution)/shard_map/ppermute | solution.py:583
  315.5 12.9 %collective-permute-start.26 = (bf16[96,512]{1,0:T(8,128)(2,1)S(1)}, bf16[96,512]{1,0:T(8,128)(2,1)S(1)}, u32[]{:S(2)}, u32[]{:S(2)}) collective-permute-start(bf16[96,512]{1,0:T(8,128)(2,1)S(1)} %copy-done.23), channel_id=1, source_target_pairs={{0,4},{1,5},{2,6},{3,7},{4,8},{5,9},{6,10},{7,11},{8,12},{9,13},{1... | collective-permute-start | bytes 294920 | tf_op jit(solution)/shard_map/ppermute | solution.py:583
  316.7 14.4 %collective-permute-start.21 = (bf16[4,96,512]{2,1,0:T(8,128)(2,1)S(1)}, bf16[4,96,512]{2,1,0:T(8,128)(2,1)S(1)}, u32[]{:S(2)}, u32[]{:S(2)}) collective-permute-start(bf16[4,96,512]{2,1,0:T(8,128)(2,1)S(1)} %fusion.1.refs_13_), channel_id=1, source_target_pairs={{0,2},{1,3},{2,0},{3,1},{4,6},{5,7},{6,4},{7,5},{8,10},{9,11},{10,... | collective-permute-start | bytes 1179656 | tf_op jit(solution)/shard_map/ppermute | solution.py:587
  327.1 29.0 %collective-permute-start.20 = (bf16[1024,512]{1,0:T(8,128)(2,1)}, bf16[1024,512]{1,0:T(8,128)(2,1)}, u32[]{:S(2)}, u32[]{:S(2)}) collective-permute-start(bf16[1024,512]{1,0:T(8,128)(2,1)} %get-tuple-element.165), channel_id=1, source_target_pairs={{16,0},{17,1},{18,2},{19,3},{20,4},{21,5},{22,6},{23,7},{24,8},{25... | collective-permute-start | bytes 3145736 | tf_op jit(solution)/shard_map/ppermute | solution.py:591
  336.2 19.9 %collective-permute-start.30 = (bf16[464,512]{1,0:T(8,128)(2,1)S(1)}, bf16[464,512]{1,0:T(8,128)(2,1)S(1)}, u32[]{:S(2)}, u32[]{:S(2)}) collective-permute-start(bf16[464,512]{1,0:T(8,128)(2,1)S(1)} %pad_maximum_fusion), channel_id=1, source_target_pairs={{0,16},{1,17},{2,18},{3,19},{4,20},{5,21},{6,22},{7,23},{8,24},{9,... | collective-permute-start | bytes 1425416 | tf_op jit(solution)/shard_map/ppermute | solution.py:591
  356.7 12.1 %collective-permute-start.32 = (bf16[368,512]{1,0:T(8,128)(2,1)}, bf16[368,512]{1,0:T(8,128)(2,1)S(1)}, u32[]{:S(2)}, u32[]{:S(2)}) collective-permute-start(bf16[368,512]{1,0:T(8,128)(2,1)} %bitcast.92), channel_id=1, source_target_pairs={{16,0},{17,1},{18,2},{19,3},{20,4},{21,5},{22,6},{23,7},{24,8},{25... | collective-permute-start | bytes 1130504 | tf_op jit(solution)/shard_map/ppermute | solution.py:591
  (43 other events, 409.6 us)
Sparse Core Ops, SparseCore 0:
  25.8 73.9 all-gather.4
  102.0 58.0 all-gather.6
  204.1 71.7 reduce-scatter.2
  280.3 76.3 reduce-scatter.4

commit v5 on v4

--- a/solution.py
+++ b/solution.py
@@ -837,9 +837,9 @@
 
     zh0 = jnp.stack(along_z(heads[0]))
     yh0 = swapped(zh0, 2)
-    zh1 = along_z(after(heads[1], yh0))
     head0 = cores(zh0, yh0)
     n1, q, k, v, vec = qkv_forward(place, x, head0)
+    zh1 = along_z(after(heads[1], n1))
     o, s = attend_forward(place, q, k, v, 0)
     zh1 = jnp.stack([after(part, o) for part in zh1])
     yh1 = swapped(zh1, 2)

time: 388 us -> 394 us (1.015)
  waiting for transfers between devices: 76.1 us -> 82.4 us
    ppermute x12, waiting for transfers between devices: 20.9 us -> 28.3 us  [moved_z(): lax.ppermute(value, 'dp', [(d, (d + 4 * steps) % count) for d in range(co...]
  transfers between devices with their start and end apart: 37 -> 37, of which waited for: 16 -> 16; matrix products, arithmetic and copies ran while one was open for 8% -> 7% of each run, Pallas kernels for 45% -> 44%
where the time goes in v5:
time: 394 us; the launch traced here: 386 us
  Pallas kernels  207 us (53%)
  waiting for transfers between devices  82.4 us (21%)
  starting transfers between devices  44 us (11%)
  other arithmetic  29.7 us (8%)
  between operations  14.5 us (4%)
  local copies, waits for them, and re-layouts  8.6 us (2%)
    pallas_call x18, Pallas kernels, run(): pl.pallas_call(body, grid_spec=pltpu.PrefetchScalarGridSpec(num_scalar_pr...  207 us
    ppermute x9, waiting for transfers between devices, crossed(): return lax.ppermute(value, 'section', [(s, 1 - s) for s in sources])  29.1 us
    ppermute x12, waiting for transfers between devices, moved_z(): lax.ppermute(value, 'dp', [(d, (d + 4 * steps) % count) for d in range(co...  28.3 us
    ppermute x12, starting transfers between devices, moved_z(): lax.ppermute(value, 'dp', [(d, (d + 4 * steps) % count) for d in range(co...  19.3 us
    ppermute x9, starting transfers between devices, crossed(): return lax.ppermute(value, 'section', [(s, 1 - s) for s in sources])  18.9 us
    ppermute x12, waiting for transfers between devices, swapped(): lax.ppermute(value, 'dp', [(d, d ^ bit) for d in range(lax.axis_size('dp'...  16.1 us
    all_gather x1, waiting for transfers between devices, run(): tail1 = lax.all_gather(after(tails[1], tail0), 'dp', axis=0)  8.14 us
  transfers between devices with their start and end apart: 37, of which 16 were waited for; matrix products, arithmetic and copies ran while one was open for 7% of the time, Pallas kernels for 44%

profile of v5, /device:TPU:0, one launch (start us, length us, event | category | flops | bytes accessed | tf_op | source)
XLA Modules:
  0.0 386.3 jit_solution(9931423481107169324)
XLA Ops:
  15.1 8.6 %collective-permute-done.10 = bf16[352,512]{1,0:T(8,128)(2,1)S(1)} collective-permute-done((bf16[352,512]{1,0:T(8,128)(2,1)}, bf16[352,512]{1,0:T(8,128)(2,1)S(1)}, u32[]{:S(2)}, u32[]{:S(2)}) %collective-permute-start.10) | collective-permute-done | bytes 360480 | tf_op jit(solution)/shard_map/ppermute | solution.py:591
  40.9 10.7 %collective-permute-done.2 = bf16[112,512]{1,0:T(8,128)(2,1)S(1)} collective-permute-done((bf16[112,512]{1,0:T(8,128)(2,1)S(1)}, bf16[112,512]{1,0:T(8,128)(2,1)S(1)}, u32[]{:S(2)}, u32[]{:S(2)}) %collective-permute-start.2) | collective-permute-done | bytes 114720 | tf_op jit(solution)/shard_map/ppermute | solution.py:583
  53.2 7.1 %collective-permute-done.4.refs_3_.refs_10_ = bf16[4,112,512]{2,1,0:T(8,128)(2,1)S(1)} collective-permute-done((bf16[4,112,512]{2,1,0:T(8,128)(2,1)S(1)}, bf16[4,112,512]{2,1,0:T(8,128)(2,1)S(1)}, u32[]{:S(2)}, u32[]{:S(2)}) %collective-permute-start.4) | collective-permute-done | bytes 458784 | tf_op jit(solution)/shard_map/ppermute | solution.py:587
  63.0 6.6 %shard_map.161 = (bf16[1024,512]{1,0:T(8,128)(2,1)}, bf16[1024,512]{1,0:T(8,128)(2,1)}, bf16[1024,512]{1,0:T(8,128)(2,1)}, bf16[1024,512]{1,0:T(8,128)(2,1)}, f32[16,512]{1,0:T(8,128)}) custom-call(s32[4]{0:T(128)} %pad_add_fusion.refs_0_, bf16[1024,512]{1,0:T(8,128)(2,1)} %select_bitcast_fusion.4.refs_1_, bf16[4,112,512]{2,1,0:T(8,128)(2,1)} %copy-done.9, ...), custom_call_target="tpu_custom_call" | custom-call | flops 1610612736 | bytes 8000000 | tf_op jit(solution)/shard_map/pallas_call | solution.py:72
  76.1 9.2 %shard_map.162 = (bf16[1024,512]{1,0:T(8,128)(2,1)}, f32[1024,512]{1,0:T(8,128)}) custom-call(s32[4]{0:T(128)} %pad_add_fusion.refs_0_, bf16[1024,512]{1,0:T(8,128)(2,1)} %get-tuple-element.99.refs_1_, bf16[1024,512]{1,0:T(8,128)(2,1)} %get-tuple-element.100.refs_2_, bf16[1024,512]{1,0:T(8,128)(2,1)} %get-tuple-element.101.refs_3_), custom_call_target="tpu_custom_call" | custom-call | flops 6000000000 | bytes 3000000 | tf_op jit(solution)/shard_map/pallas_call | solution.py:72
  85.4 11.3 %collective-permute-done.8 = bf16[112,512]{1,0:T(8,128)(2,1)S(1)} collective-permute-done((bf16[112,512]{1,0:T(8,128)(2,1)S(1)}, bf16[112,512]{1,0:T(8,128)(2,1)S(1)}, u32[]{:S(2)}, u32[]{:S(2)}) %collective-permute-start.8) | collective-permute-done | bytes 114720 | tf_op jit(solution)/shard_map/ppermute | solution.py:583
  97.5 9.4 %shard_map.163 = (bf16[1024,512]{1,0:T(8,128)(2,1)}, f32[1024,512]{1,0:T(8,128)}) custom-call(s32[4]{0:T(128)} %pad_add_fusion.refs_0_, bf16[1024,512]{1,0:T(8,128)(2,1)} %get-tuple-element.99.refs_1_, bf16[1024,512]{1,0:T(8,128)(2,1)} %get-tuple-element.100.refs_2_, ...), custom_call_target="tpu_custom_call", output_to_operand_aliasing={{0}: (4, {}), {1}: (5, {})} | custom-call | flops 6000000000 | bytes 3000000 | tf_op jit(solution)/shard_map/pallas_call | solution.py:72
  108.6 17.9 %shard_map.164 = (bf16[1024,512]{1,0:T(8,128)(2,1)}, bf16[1024,512]{1,0:T(8,128)(2,1)}, f32[1024,128]{1,0:T(8,128)}, bf16[1024,512]{1,0:T(8,128)(2,1)}, bf16[102...) custom-call(s32[4]{0:T(128)} %pad_add_fusion.refs_0_, ...), custom_call_target="tpu_custom_call" | custom-call | flops 5905580032 | bytes 24000000 | tf_op jit(solution)/shard_map/pallas_call | solution.py:72
  130.3 6.6 %shard_map.165 = (bf16[1024,512]{1,0:T(8,128)(2,1)}, bf16[1024,512]{1,0:T(8,128)(2,1)}, bf16[1024,512]{1,0:T(8,128)(2,1)}, bf16[1024,512]{1,0:T(8,128)(2,1)}, f32[16,512]{1,0:T(8,128)}) custom-call(s32[4]{0:T(128)} %pad_add_fusion.refs_0_, bf16[1024,512]{1,0:T(8,128)(2,1)} %get-tuple-element.113.refs_1_, ...), custom_call_target="tpu_custom_call" | custom-call | flops 1610612736 | bytes 8000000 | tf_op jit(solution)/shard_map/pallas_call | solution.py:72
  136.9 9.3 %shard_map.166 = (bf16[1024,512]{1,0:T(8,128)(2,1)}, f32[1024,512]{1,0:T(8,128)}) custom-call(s32[4]{0:T(128)} %pad_add_fusion.refs_0_, bf16[1024,512]{1,0:T(8,128)(2,1)} %get-tuple-element.117.refs_1_, bf16[1024,512]{1,0:T(8,128)(2,1)} %get-tuple-element.118.refs_2_, bf16[1024,512]{1,0:T(8,128)(2,1)} %get-tuple-element.119.refs_3_), custom_call_target="tpu_custom_call" | custom-call | flops 6000000000 | bytes 3000000 | tf_op jit(solution)/shard_map/pallas_call | solution.py:72
  146.2 9.7 %shard_map.167 = (bf16[1024,512]{1,0:T(8,128)(2,1)}, f32[1024,512]{1,0:T(8,128)}) custom-call(s32[4]{0:T(128)} %pad_add_fusion.refs_0_, bf16[1024,512]{1,0:T(8,128)(2,1)} %get-tuple-element.117.refs_1_, bf16[1024,512]{1,0:T(8,128)(2,1)} %get-tuple-element.118.refs_2_, ...), custom_call_target="tpu_custom_call", output_to_operand_aliasing={{0}: (4, {}), {1}: (5, {})} | custom-call | flops 6000000000 | bytes 3000000 | tf_op jit(solution)/shard_map/pallas_call | solution.py:72
  157.4 8.1 %all-gather.7.cloned.1.call-done = bf16[5632,512]{1,0:T(8,128)(2,1)} async-done(((bf16[352,512]{1,0:T(8,128)(2,1)}), bf16[5632,512]{1,0:T(8,128)(2,1)}) %all-gather.7.cloned.1.call-update) | async-done | bytes 5767184 | tf_op jit(solution)/shard_map/all_gather | solution.py:848
  165.6 30.0 %shard_map.168 = (bf16[1024,512]{1,0:T(8,128)(2,1)}, f32[1024,512]{1,0:T(8,128)}, bf16[1024,512]{1,0:T(8,128)(2,1)}, bf16[1024,512]{1,0:T(8,128)(2,1)}, bf16[8,3...) custom-call(s32[4]{0:T(128)} %pad_add_fusion.refs_0_, bf16[1024,512]{1,0:T(8,128)(2,1)} %get-tuple-element.113.refs_1_, ...), custom_call_target="tpu_custom_call" | custom-call | flops 17716740096 | bytes 24000000 | tf_op jit(solution)/shard_map/pallas_call | solution.py:72
  197.6 7.6 %shard_map.169 = (bf16[1024,512]{1,0:T(8,128)(2,1)}, bf16[1024,512]{1,0:T(8,128)(2,1)}, bf16[1024,512]{1,0:T(8,128)(2,1)}) custom-call(s32[4]{0:T(128)} %pad_add_fusion.refs_0_, bf16[1024,512]{1,0:T(8,128)(2,1)} %get-tuple-element.117.refs_1_, bf16[1024,512]{1,0:T(8,128)(2,1)} %get-tuple-element.118.refs_2_, bf16[1024,512]{1,0:T(8,128)(2,1)} %get-tuple-element.119.refs_3_, ...), custom_call_target="tpu_custom_call" | custom-call | flops 5000000000 | bytes 5000000 | tf_op jit(solution)/shard_map/pallas_call | solution.py:72
  209.6 16.5 %shard_map.170 = (bf16[1024,512]{1,0:T(8,128)(2,1)}, bf16[1024,512]{1,0:T(8,128)(2,1)}, bf16[1024,512]{1,0:T(8,128)(2,1)}) custom-call(s32[4]{0:T(128)} %pad_add_fusion.refs_0_, bf16[1024,512]{1,0:T(8,128)(2,1)} %get-tuple-element.117.refs_1_, ...), custom_call_target="tpu_custom_call", output_to_operand_aliasing={{0}: (7, {}), {1}: (8, {}), {2}: (9, {})} | custom-call | flops 15000000512 | bytes 5000000 | tf_op jit(solution)/shard_map/pallas_call | solution.py:72
  226.1 6.4 %shard_map.171 = (bf16[2,4,96,512]{3,2,1,0:T(8,128)(2,1)}, bf16[2,4,96,512]{3,2,1,0:T(8,128)(2,1)}) custom-call(s32[4]{0:T(128)} %pad_add_fusion.refs_0_, bf16[1024,512]{1,0:T(8,128)(2,1)} %get-tuple-element.116.refs_2_.refs_7_.refs_1_, bf16[1024,512]{1,0:T(8,128)(2,1)} %get-tuple-element.134.refs_2_.refs_3_, ...), custom_call_target="tpu_custom_call" | custom-call | flops 1610612736 | bytes 9000000 | tf_op jit(solution)/shard_map/pallas_call | solution.py:72
  233.5 30.6 %shard_map.172 = (f32[1024,512]{1,0:T(8,128)}, bf16[1024,512]{1,0:T(8,128)(2,1)}, f32[1024,512]{1,0:T(8,128)}, bf16[1024,512]{1,0:T(8,128)(2,1)}, bf16[1024,512]...) custom-call(s32[4]{0:T(128)} %pad_add_fusion.refs_0_, ...), custom_call_target="tpu_custom_call" | custom-call | flops 13958643712 | bytes 40000000 | tf_op jit(solution)/shard_map/pallas_call | solution.py:72
  264.8 5.8 %collective-permute-done.16 = bf16[2,4,96,512]{3,2,1,0:T(8,128)(2,1)S(1)} collective-permute-done((bf16[2,4,96,512]{3,2,1,0:T(8,128)(2,1)S(1)}, bf16[2,4,96,512]{3,2,1,0:T(8,128)(2,1)S(1)}, u32[]{:S(2)}, u32[]{:S(2)}) %collective-permute-start.16) | collective-permute-done | bytes 786464 | tf_op jit(solution)/shard_map/ppermute | solution.py:587
  271.4 7.7 %shard_map.173 = (bf16[1024,512]{1,0:T(8,128)(2,1)}, bf16[1024,512]{1,0:T(8,128)(2,1)}, bf16[1024,512]{1,0:T(8,128)(2,1)}) custom-call(s32[4]{0:T(128)} %pad_add_fusion.refs_0_, bf16[1024,512]{1,0:T(8,128)(2,1)} %get-tuple-element.99.refs_1_, bf16[1024,512]{1,0:T(8,128)(2,1)} %get-tuple-element.100.refs_2_, bf16[1024,512]{1,0:T(8,128)(2,1)} %get-tuple-element.101.refs_3_, ...), custom_call_target="tpu_custom_call" | custom-call | flops 5000000000 | bytes 5000000 | tf_op jit(solution)/shard_map/pallas_call | solution.py:72
  286.1 16.3 %shard_map.174 = (bf16[1024,512]{1,0:T(8,128)(2,1)}, bf16[1024,512]{1,0:T(8,128)(2,1)}, bf16[1024,512]{1,0:T(8,128)(2,1)}) custom-call(s32[4]{0:T(128)} %pad_add_fusion.refs_0_, bf16[1024,512]{1,0:T(8,128)(2,1)} %get-tuple-element.99.refs_1_, ...), custom_call_target="tpu_custom_call", output_to_operand_aliasing={{0}: (7, {}), {1}: (8, {}), {2}: (9, {})} | custom-call | flops 15000000512 | bytes 5000000 | tf_op jit(solution)/shard_map/pallas_call | solution.py:72
  303.3 5.4 %collective-permute-done.17.refs_5_ = bf16[1024,512]{1,0:T(8,128)(2,1)S(1)} collective-permute-done((bf16[1024,512]{1,0:T(8,128)(2,1)}, bf16[1024,512]{1,0:T(8,128)(2,1)S(1)}, u32[]{:S(2)}, u32[]{:S(2)}) %collective-permute-start.17) | collective-permute-done | bytes 1048608 | tf_op jit(solution)/shard_map/ppermute | solution.py:591
  309.8 6.5 %shard_map.175 = (bf16[2,4,96,512]{3,2,1,0:T(8,128)(2,1)}, bf16[2,4,96,512]{3,2,1,0:T(8,128)(2,1)}) custom-call(s32[4]{0:T(128)} %pad_add_fusion.refs_0_, bf16[1024,512]{1,0:T(8,128)(2,1)} %get-tuple-element.98.refs_2_.refs_18_.refs_1_, bf16[1024,512]{1,0:T(8,128)(2,1)} %get-tuple-element.156.refs_2_.refs_3_, ...), custom_call_target="tpu_custom_call" | custom-call | flops 1610612736 | bytes 9000000 | tf_op jit(solution)/shard_map/pallas_call | solution.py:72
  322.9 9.6 %shard_map.176 = (f32[1024,512]{1,0:T(8,128)}, bf16[1024,512]{1,0:T(8,128)(2,1)}) custom-call(s32[4]{0:T(128)} %pad_add_fusion.refs_0_, bf16[1024,512]{1,0:T(8,128)(2,1)} %select_bitcast_fusion.4.refs_1_, f32[1024,512]{1,0:T(8,128)} %get-tuple-element.147.refs_2_, bf16[1024,512]{1,0:T(8,128)(2,1)} %get-tuple-element.156.refs_2_.refs_3_, ...), custom_call_target="tpu_custom_call" | custom-call | flops 2147483648 | bytes 12000000 | tf_op jit(solution)/shard_map/pallas_call | solution.py:72
  355.0 6.7 %collective-permute-done.25.refs_2_ = bf16[96,512]{1,0:T(8,128)(2,1)S(1)} collective-permute-done((bf16[96,512]{1,0:T(8,128)(2,1)S(1)}, bf16[96,512]{1,0:T(8,128)(2,1)S(1)}, u32[]{:S(2)}, u32[]{:S(2)}) %collective-permute-start.25) | collective-permute-done | bytes 98336 | tf_op jit(solution)/shard_map/ppermute | solution.py:591
  (165 shorter events, 107.8 us)
Async XLA Ops:
  7.2 99.8 %all-gather.5.cloned.1.call-start = ((), (), s32[]{:S(2)}) async-start(), calls=%async_computation.4 | async-start | bytes 6127616 | tf_op jit(solution)/shard_map/all_gather | solution.py:833
  12.2 11.6 %collective-permute-start.10 = (bf16[352,512]{1,0:T(8,128)(2,1)}, bf16[352,512]{1,0:T(8,128)(2,1)S(1)}, u32[]{:S(2)}, u32[]{:S(2)}) collective-permute-start(bf16[352,512]{1,0:T(8,128)(2,1)} %get-tuple-element.111), channel_id=1, source_target_pairs={{0,16},{16,0},{1,17},{17,1},{2,18},{18,2},{3,19},{19,3},{4,20},{20... | collective-permute-start | bytes 1081352 | tf_op jit(solution)/shard_map/ppermute | solution.py:591
  25.6 139.9 %all-gather.7.cloned.1.call-start = ((), (), s32[]{:S(2)}) async-start(), calls=%async_computation.5 | async-start | bytes 6127616 | tf_op jit(solution)/shard_map/all_gather | solution.py:848
  35.6 16.1 %collective-permute-start.2 = (bf16[112,512]{1,0:T(8,128)(2,1)S(1)}, bf16[112,512]{1,0:T(8,128)(2,1)S(1)}, u32[]{:S(2)}, u32[]{:S(2)}) collective-permute-start(bf16[112,512]{1,0:T(8,128)(2,1)S(1)} %get-tuple-element.215), channel_id=1, source_target_pairs={{0,8},{1,9},{2,10},{3,11},{4,12},{5,13},{6,14},{7,15},{8,0},{9,1},... | collective-permute-start | bytes 344072 | tf_op jit(solution)/shard_map/ppermute | solution.py:583
  35.6 16.1 %collective-permute-start.1 = (bf16[112,512]{1,0:T(8,128)(2,1)S(1)}, bf16[112,512]{1,0:T(8,128)(2,1)S(1)}, u32[]{:S(2)}, u32[]{:S(2)}) collective-permute-start(bf16[112,512]{1,0:T(8,128)(2,1)S(1)} %get-tuple-element.215), channel_id=1, source_target_pairs={{0,4},{1,5},{2,6},{3,7},{4,8},{5,9},{6,10},{7,11},{8,12},{9,13},{1... | collective-permute-start | bytes 344072 | tf_op jit(solution)/shard_map/ppermute | solution.py:583
  69.6 15.8 %collective-permute-start.9 = (bf16[112,512]{1,0:T(8,128)(2,1)S(1)}, bf16[112,512]{1,0:T(8,128)(2,1)S(1)}, u32[]{:S(2)}, u32[]{:S(2)}) collective-permute-start(bf16[112,512]{1,0:T(8,128)(2,1)S(1)} %get-tuple-element.105), channel_id=1, source_target_pairs={{0,12},{1,13},{2,14},{3,15},{4,0},{5,1},{6,2},{7,3},{8,4},{9,5},{1... | collective-permute-start | bytes 344072 | tf_op jit(solution)/shard_map/ppermute | solution.py:583
  69.7 27.0 %collective-permute-start.8 = (bf16[112,512]{1,0:T(8,128)(2,1)S(1)}, bf16[112,512]{1,0:T(8,128)(2,1)S(1)}, u32[]{:S(2)}, u32[]{:S(2)}) collective-permute-start(bf16[112,512]{1,0:T(8,128)(2,1)S(1)} %get-tuple-element.105), channel_id=1, source_target_pairs={{0,8},{1,9},{2,10},{3,11},{4,12},{5,13},{6,14},{7,15},{8,0},{9,1},... | collective-permute-start | bytes 344072 | tf_op jit(solution)/shard_map/ppermute | solution.py:583
  74.2 22.5 %collective-permute-start.7 = (bf16[112,512]{1,0:T(8,128)(2,1)S(1)}, bf16[112,512]{1,0:T(8,128)(2,1)S(1)}, u32[]{:S(2)}, u32[]{:S(2)}) collective-permute-start(bf16[112,512]{1,0:T(8,128)(2,1)S(1)} %get-tuple-element.105), channel_id=1, source_target_pairs={{0,4},{1,5},{2,6},{3,7},{4,8},{5,9},{6,10},{7,11},{8,12},{9,13},{1... | collective-permute-start | bytes 344072 | tf_op jit(solution)/shard_map/ppermute | solution.py:583
  107.0 233.8 %reduce-scatter.3.cloned.1.call-start = ((), (), s32[]{:S(2)}) async-start(), calls=%async_computation.2 | async-start | bytes 3391488 | tf_op jit(solution)/shard_map/reduce_scatter | solution.py:660
  107.2 19.3 %collective-permute-start.11 = (bf16[4,112,512]{2,1,0:T(8,128)(2,1)S(1)}, bf16[4,112,512]{2,1,0:T(8,128)(2,1)S(1)}, u32[]{:S(2)}, u32[]{:S(2)}) collective-permute-start(bf16[4,112,512]{2,1,0:T(8,128)(2,1)S(1)} %copy-done.16), channel_id=1, source_target_pairs={{0,2},{1,3},{2,0},{3,1},{4,6},{5,7},{6,4},{7,5},{8,10},{9,11},{10,... | collective-permute-start | bytes 1376264 | tf_op jit(solution)/shard_map/ppermute | solution.py:587
  127.2 28.7 %collective-permute-start.14 = (bf16[1024,512]{1,0:T(8,128)(2,1)S(1)}, bf16[1024,512]{1,0:T(8,128)(2,1)S(1)}, u32[]{:S(2)}, u32[]{:S(2)}) collective-permute-start(bf16[1024,512]{1,0:T(8,128)(2,1)S(1)} %select_bitcast_fusion.3), channel_id=1, source_target_pairs={{0,16},{16,0},{1,17},{17,1},{2,18},{18,2},{3,19},{19,3},{4,20},{20... | collective-permute-start | bytes 3145736 | tf_op jit(solution)/shard_map/ppermute | solution.py:591
  197.3 35.3 %collective-permute-start.15 = (bf16[1024,512]{1,0:T(8,128)(2,1)S(1)}, bf16[1024,512]{1,0:T(8,128)(2,1)S(1)}, u32[]{:S(2)}, u32[]{:S(2)}) collective-permute-start(bf16[1024,512]{1,0:T(8,128)(2,1)S(1)} %broadcast_select_fusion.1), channel_id=1, source_target_pairs={{0,16},{16,0},{1,17},{17,1},{2,18},{18,2},{3,19},{19,3},{4,20},{20... | collective-permute-start | bytes 3145736 | tf_op jit(solution)/shard_map/ppermute | solution.py:591
  209.5 152.8 %reduce-scatter.5.cloned.1.call-start = ((), (), s32[]{:S(2)}) async-start(), calls=%async_computation.3 | async-start | bytes 3391488 | tf_op jit(solution)/shard_map/reduce_scatter | solution.py:660
  264.2 14.9 %collective-permute-start.31 = (bf16[8,368,512]{2,1,0:T(8,128)(2,1)}, bf16[8,368,512]{2,1,0:T(8,128)(2,1)S(1)}, u32[]{:S(2)}, u32[]{:S(2)}) collective-permute-start(bf16[8,368,512]{2,1,0:T(8,128)(2,1)} %get-tuple-element.175), channel_id=1, source_target_pairs={{0,1},{1,0},{2,3},{3,2},{4,5},{5,4},{6,7},{7,6},{8,9},{9,8},{10,11... | collective-permute-start | bytes 9043976 | tf_op jit(solution)/shard_map/ppermute | solution.py:587
  281.6 27.1 %collective-permute-start.17 = (bf16[1024,512]{1,0:T(8,128)(2,1)}, bf16[1024,512]{1,0:T(8,128)(2,1)S(1)}, u32[]{:S(2)}, u32[]{:S(2)}) collective-permute-start(bf16[1024,512]{1,0:T(8,128)(2,1)} %get-tuple-element.151), channel_id=1, source_target_pairs={{0,16},{1,17},{2,18},{3,19},{4,20},{5,21},{6,22},{7,23},{8,24},{9,... | collective-permute-start | bytes 3145736 | tf_op jit(solution)/shard_map/ppermute | solution.py:591
  285.6 16.8 %collective-permute-start.18 = (bf16[4,96,512]{2,1,0:T(8,128)(2,1)S(1)}, bf16[4,96,512]{2,1,0:T(8,128)(2,1)S(1)}, u32[]{:S(2)}, u32[]{:S(2)}) collective-permute-start(bf16[4,96,512]{2,1,0:T(8,128)(2,1)S(1)} %copy-done.20), channel_id=1, source_target_pairs={{0,2},{1,3},{2,0},{3,1},{4,6},{5,7},{6,4},{7,5},{8,10},{9,11},{10,... | collective-permute-start | bytes 1179656 | tf_op jit(solution)/shard_map/ppermute | solution.py:587
  318.1 15.8 %collective-permute-start.28 = (bf16[96,512]{1,0:T(8,128)(2,1)S(1)}, bf16[96,512]{1,0:T(8,128)(2,1)S(1)}, u32[]{:S(2)}, u32[]{:S(2)}) collective-permute-start(bf16[96,512]{1,0:T(8,128)(2,1)S(1)} %copy-done.25), channel_id=1, source_target_pairs={{0,12},{1,13},{2,14},{3,15},{4,0},{5,1},{6,2},{7,3},{8,4},{9,5},{1... | collective-permute-start | bytes 294920 | tf_op jit(solution)/shard_map/ppermute | solution.py:583
  320.1 13.7 %collective-permute-start.27 = (bf16[96,512]{1,0:T(8,128)(2,1)S(1)}, bf16[96,512]{1,0:T(8,128)(2,1)S(1)}, u32[]{:S(2)}, u32[]{:S(2)}) collective-permute-start(bf16[96,512]{1,0:T(8,128)(2,1)S(1)} %copy-done.24), channel_id=1, source_target_pairs={{0,8},{1,9},{2,10},{3,11},{4,12},{5,13},{6,14},{7,15},{8,0},{9,1},... | collective-permute-start | bytes 294920 | tf_op jit(solution)/shard_map/ppermute | solution.py:583
  321.0 12.9 %collective-permute-start.26 = (bf16[96,512]{1,0:T(8,128)(2,1)S(1)}, bf16[96,512]{1,0:T(8,128)(2,1)S(1)}, u32[]{:S(2)}, u32[]{:S(2)}) collective-permute-start(bf16[96,512]{1,0:T(8,128)(2,1)S(1)} %copy-done.23), channel_id=1, source_target_pairs={{0,4},{1,5},{2,6},{3,7},{4,8},{5,9},{6,10},{7,11},{8,12},{9,13},{1... | collective-permute-start | bytes 294920 | tf_op jit(solution)/shard_map/ppermute | solution.py:583
  322.2 14.5 %collective-permute-start.21 = (bf16[4,96,512]{2,1,0:T(8,128)(2,1)S(1)}, bf16[4,96,512]{2,1,0:T(8,128)(2,1)S(1)}, u32[]{:S(2)}, u32[]{:S(2)}) collective-permute-start(bf16[4,96,512]{2,1,0:T(8,128)(2,1)S(1)} %fusion.1.refs_13_), channel_id=1, source_target_pairs={{0,2},{1,3},{2,0},{3,1},{4,6},{5,7},{6,4},{7,5},{8,10},{9,11},{10,... | collective-permute-start | bytes 1179656 | tf_op jit(solution)/shard_map/ppermute | solution.py:587
  332.6 29.0 %collective-permute-start.20 = (bf16[1024,512]{1,0:T(8,128)(2,1)}, bf16[1024,512]{1,0:T(8,128)(2,1)}, u32[]{:S(2)}, u32[]{:S(2)}) collective-permute-start(bf16[1024,512]{1,0:T(8,128)(2,1)} %get-tuple-element.165), channel_id=1, source_target_pairs={{16,0},{17,1},{18,2},{19,3},{20,4},{21,5},{22,6},{23,7},{24,8},{25... | collective-permute-start | bytes 3145736 | tf_op jit(solution)/shard_map/ppermute | solution.py:591
  341.8 19.9 %collective-permute-start.30 = (bf16[464,512]{1,0:T(8,128)(2,1)S(1)}, bf16[464,512]{1,0:T(8,128)(2,1)S(1)}, u32[]{:S(2)}, u32[]{:S(2)}) collective-permute-start(bf16[464,512]{1,0:T(8,128)(2,1)S(1)} %pad_maximum_fusion), channel_id=1, source_target_pairs={{0,16},{1,17},{2,18},{3,19},{4,20},{5,21},{6,22},{7,23},{8,24},{9,... | collective-permute-start | bytes 1425416 | tf_op jit(solution)/shard_map/ppermute | solution.py:591
  350.1 11.5 %collective-permute-start.25 = (bf16[96,512]{1,0:T(8,128)(2,1)S(1)}, bf16[96,512]{1,0:T(8,128)(2,1)S(1)}, u32[]{:S(2)}, u32[]{:S(2)}) collective-permute-start(bf16[96,512]{1,0:T(8,128)(2,1)S(1)} %get-tuple-element.196), channel_id=1, source_target_pairs={{16,0},{17,1},{18,2},{19,3},{20,4},{21,5},{22,6},{23,7},{24,8},{25... | collective-permute-start | bytes 294920 | tf_op jit(solution)/shard_map/ppermute | solution.py:591
  362.4 12.0 %collective-permute-start.32 = (bf16[368,512]{1,0:T(8,128)(2,1)}, bf16[368,512]{1,0:T(8,128)(2,1)S(1)}, u32[]{:S(2)}, u32[]{:S(2)}) collective-permute-start(bf16[368,512]{1,0:T(8,128)(2,1)} %bitcast.92), channel_id=1, source_target_pairs={{16,0},{17,1},{18,2},{19,3},{20,4},{21,5},{22,6},{23,7},{24,8},{25... | collective-permute-start | bytes 1130504 | tf_op jit(solution)/shard_map/ppermute | solution.py:591
  (43 other events, 390.1 us)
Sparse Core Ops, SparseCore 0:
  25.8 73.9 all-gather.4
  107.1 58.4 all-gather.6
  209.6 71.7 reduce-scatter.2
  285.9 76.4 reduce-scatter.4

commit v6 on v4

--- a/solution.py
+++ b/solution.py
@@ -315,13 +315,25 @@
 def turn_kernel(count, place, x_ref, n1_ref, o_ref, e_ref, vec_ref, o_cols, n1_cols, rest_ref,
                 y_ref, dm_ref, dza_ref, do_ref, keep, send, buf, h, du, slope, n2, df, dzf, da, dza, sums, sems):
     step = pl.program_id(0)
-    at_start([rest_copy(rest_ref, buf, sems.at[0], 0, REST, 0)])
+    near = rest_copy(rest_ref, buf, sems.at[0], 0, 3 * UNIT, 0)
+    far = rest_copy(rest_ref, buf, sems.at[1], 3 * UNIT, REST, 0)
+
+    @pl.when(step == 0)
+    def _():
+        near.start()
+        far.start()
+        near.wait()
 
     @pl.when(step < count)
     def _():
         at_rows = pl.ds(pl.multiple_of(step * ROWS, ROWS), ROWS)
         vec = vec_ref[...]
         middle, low, hat, scale, ga, ta = gated_rows(x_ref[...], n1_ref[...], o_ref[...], vec, buf)
+
+        @pl.when(step == 0)
+        def _():
+            far.wait()
+
         y, gf, tf = feed_rows(middle, low, vec, buf, h, slope, at_rows)
         y_ref[...] = y.astype(bf16)
         e = e_ref[...].astype(f32)
@@ -362,7 +374,7 @@
         + [pltpu.VMEM((length, wide), bf16)] * 2
         + [pltpu.VMEM((ROWS, wide), bf16)]
         + [tall] * 5
-        + [pltpu.VMEM((8, width), f32), pltpu.SemaphoreType.DMA((1,))],
+        + [pltpu.VMEM((8, width), f32), pltpu.SemaphoreType.DMA((2,))],
         flops=6 * length * width * (3 * width + 2 * wide),
         moved=24_000_000,
         waits=waits,

time: 388 us -> 388 us (level)
  no operation moved by 1% of the time
where the time goes in v6:
time: 388 us; the launch traced here: 380 us
  Pallas kernels  206 us (53%)
  waiting for transfers between devices  76.5 us (20%)
  starting transfers between devices  43.7 us (11%)
  other arithmetic  29.7 us (8%)
  between operations  14.5 us (4%)
  local copies, waits for them, and re-layouts  9.45 us (2%)
    pallas_call x18, Pallas kernels, run(): pl.pallas_call(body, grid_spec=pltpu.PrefetchScalarGridSpec(num_scalar_pr...  206 us
    ppermute x9, waiting for transfers between devices, crossed(): return lax.ppermute(value, 'section', [(s, 1 - s) for s in sources])  29.4 us
    ppermute x12, waiting for transfers between devices, moved_z(): lax.ppermute(value, 'dp', [(d, (d + 4 * steps) % count) for d in range(co...  20.4 us
    ppermute x9, starting transfers between devices, crossed(): return lax.ppermute(value, 'section', [(s, 1 - s) for s in sources])  18.9 us
    ppermute x12, starting transfers between devices, moved_z(): lax.ppermute(value, 'dp', [(d, (d + 4 * steps) % count) for d in range(co...  18.7 us
    ppermute x12, waiting for transfers between devices, swapped(): lax.ppermute(value, 'dp', [(d, d ^ bit) for d in range(lax.axis_size('dp'...  15.4 us
    all_gather x1, waiting for transfers between devices, run(): tail1 = lax.all_gather(after(tails[1], tail0), 'dp', axis=0)  9.53 us
  transfers between devices with their start and end apart: 37, of which 16 were waited for; matrix products, arithmetic and copies ran while one was open for 8% of the time, Pallas kernels for 45%

profile of v6, /device:TPU:0, one launch (start us, length us, event | category | flops | bytes accessed | tf_op | source)
XLA Modules:
  0.0 380.2 jit_solution(2804135160041690994)
XLA Ops:
  15.1 8.6 %collective-permute-done.10 = bf16[352,512]{1,0:T(8,128)(2,1)S(1)} collective-permute-done((bf16[352,512]{1,0:T(8,128)(2,1)}, bf16[352,512]{1,0:T(8,128)(2,1)S(1)}, u32[]{:S(2)}, u32[]{:S(2)}) %collective-permute-start.10) | collective-permute-done | bytes 360480 | tf_op jit(solution)/shard_map/ppermute | solution.py:603
  40.9 10.7 %collective-permute-done.2 = bf16[112,512]{1,0:T(8,128)(2,1)S(1)} collective-permute-done((bf16[112,512]{1,0:T(8,128)(2,1)S(1)}, bf16[112,512]{1,0:T(8,128)(2,1)S(1)}, u32[]{:S(2)}, u32[]{:S(2)}) %collective-permute-start.2) | collective-permute-done | bytes 114720 | tf_op jit(solution)/shard_map/ppermute | solution.py:595
  53.2 7.1 %collective-permute-done.4.refs_3_.refs_10_ = bf16[4,112,512]{2,1,0:T(8,128)(2,1)S(1)} collective-permute-done((bf16[4,112,512]{2,1,0:T(8,128)(2,1)S(1)}, bf16[4,112,512]{2,1,0:T(8,128)(2,1)S(1)}, u32[]{:S(2)}, u32[]{:S(2)}) %collective-permute-start.4) | collective-permute-done | bytes 458784 | tf_op jit(solution)/shard_map/ppermute | solution.py:599
  68.9 6.6 %shard_map.161 = (bf16[1024,512]{1,0:T(8,128)(2,1)}, bf16[1024,512]{1,0:T(8,128)(2,1)}, bf16[1024,512]{1,0:T(8,128)(2,1)}, bf16[1024,512]{1,0:T(8,128)(2,1)}, f32[16,512]{1,0:T(8,128)}) custom-call(s32[4]{0:T(128)} %pad_add_fusion.refs_0_, bf16[1024,512]{1,0:T(8,128)(2,1)} %select_bitcast_fusion.4.refs_1_, bf16[4,112,512]{2,1,0:T(8,128)(2,1)} %copy-done.9, ...), custom_call_target="tpu_custom_call" | custom-call | flops 1610612736 | bytes 8000000 | tf_op jit(solution)/shard_map/pallas_call | solution.py:72
  75.6 9.3 %shard_map.162 = (bf16[1024,512]{1,0:T(8,128)(2,1)}, f32[1024,512]{1,0:T(8,128)}) custom-call(s32[4]{0:T(128)} %pad_add_fusion.refs_0_, bf16[1024,512]{1,0:T(8,128)(2,1)} %get-tuple-element.99.refs_1_, bf16[1024,512]{1,0:T(8,128)(2,1)} %get-tuple-element.100.refs_2_, bf16[1024,512]{1,0:T(8,128)(2,1)} %get-tuple-element.101.refs_3_), custom_call_target="tpu_custom_call" | custom-call | flops 6000000000 | bytes 3000000 | tf_op jit(solution)/shard_map/pallas_call | solution.py:72
  89.3 9.4 %shard_map.163 = (bf16[1024,512]{1,0:T(8,128)(2,1)}, f32[1024,512]{1,0:T(8,128)}) custom-call(s32[4]{0:T(128)} %pad_add_fusion.refs_0_, bf16[1024,512]{1,0:T(8,128)(2,1)} %get-tuple-element.99.refs_1_, bf16[1024,512]{1,0:T(8,128)(2,1)} %get-tuple-element.100.refs_2_, ...), custom_call_target="tpu_custom_call", output_to_operand_aliasing={{0}: (4, {}), {1}: (5, {})} | custom-call | flops 6000000000 | bytes 3000000 | tf_op jit(solution)/shard_map/pallas_call | solution.py:72
  101.7 17.7 %shard_map.164 = (bf16[1024,512]{1,0:T(8,128)(2,1)}, bf16[1024,512]{1,0:T(8,128)(2,1)}, f32[1024,128]{1,0:T(8,128)}, bf16[1024,512]{1,0:T(8,128)(2,1)}, bf16[102...) custom-call(s32[4]{0:T(128)} %pad_add_fusion.refs_0_, ...), custom_call_target="tpu_custom_call" | custom-call | flops 5905580032 | bytes 24000000 | tf_op jit(solution)/shard_map/pallas_call | solution.py:72
  123.3 6.6 %shard_map.165 = (bf16[1024,512]{1,0:T(8,128)(2,1)}, bf16[1024,512]{1,0:T(8,128)(2,1)}, bf16[1024,512]{1,0:T(8,128)(2,1)}, bf16[1024,512]{1,0:T(8,128)(2,1)}, f32[16,512]{1,0:T(8,128)}) custom-call(s32[4]{0:T(128)} %pad_add_fusion.refs_0_, bf16[1024,512]{1,0:T(8,128)(2,1)} %get-tuple-element.113.refs_1_, ...), custom_call_target="tpu_custom_call" | custom-call | flops 1610612736 | bytes 8000000 | tf_op jit(solution)/shard_map/pallas_call | solution.py:72
  130.0 9.3 %shard_map.166 = (bf16[1024,512]{1,0:T(8,128)(2,1)}, f32[1024,512]{1,0:T(8,128)}) custom-call(s32[4]{0:T(128)} %pad_add_fusion.refs_0_, bf16[1024,512]{1,0:T(8,128)(2,1)} %get-tuple-element.117.refs_1_, bf16[1024,512]{1,0:T(8,128)(2,1)} %get-tuple-element.118.refs_2_, bf16[1024,512]{1,0:T(8,128)(2,1)} %get-tuple-element.119.refs_3_), custom_call_target="tpu_custom_call" | custom-call | flops 6000000000 | bytes 3000000 | tf_op jit(solution)/shard_map/pallas_call | solution.py:72
  139.3 9.7 %shard_map.167 = (bf16[1024,512]{1,0:T(8,128)(2,1)}, f32[1024,512]{1,0:T(8,128)}) custom-call(s32[4]{0:T(128)} %pad_add_fusion.refs_0_, bf16[1024,512]{1,0:T(8,128)(2,1)} %get-tuple-element.117.refs_1_, bf16[1024,512]{1,0:T(8,128)(2,1)} %get-tuple-element.118.refs_2_, ...), custom_call_target="tpu_custom_call", output_to_operand_aliasing={{0}: (4, {}), {1}: (5, {})} | custom-call | flops 6000000000 | bytes 3000000 | tf_op jit(solution)/shard_map/pallas_call | solution.py:72
  150.5 9.5 %all-gather.7.cloned.1.call-done = bf16[5632,512]{1,0:T(8,128)(2,1)} async-done(((bf16[352,512]{1,0:T(8,128)(2,1)}), bf16[5632,512]{1,0:T(8,128)(2,1)}) %all-gather.7.cloned.1.call-update) | async-done | bytes 5767184 | tf_op jit(solution)/shard_map/all_gather | solution.py:860
  160.0 29.4 %shard_map.168 = (bf16[1024,512]{1,0:T(8,128)(2,1)}, f32[1024,512]{1,0:T(8,128)}, bf16[1024,512]{1,0:T(8,128)(2,1)}, bf16[1024,512]{1,0:T(8,128)(2,1)}, bf16[8,3...) custom-call(s32[4]{0:T(128)} %pad_add_fusion.refs_0_, bf16[1024,512]{1,0:T(8,128)(2,1)} %get-tuple-element.113.refs_1_, ...), custom_call_target="tpu_custom_call" | custom-call | flops 17716740096 | bytes 24000000 | tf_op jit(solution)/shard_map/pallas_call | solution.py:72
  191.5 7.6 %shard_map.169 = (bf16[1024,512]{1,0:T(8,128)(2,1)}, bf16[1024,512]{1,0:T(8,128)(2,1)}, bf16[1024,512]{1,0:T(8,128)(2,1)}) custom-call(s32[4]{0:T(128)} %pad_add_fusion.refs_0_, bf16[1024,512]{1,0:T(8,128)(2,1)} %get-tuple-element.117.refs_1_, bf16[1024,512]{1,0:T(8,128)(2,1)} %get-tuple-element.118.refs_2_, bf16[1024,512]{1,0:T(8,128)(2,1)} %get-tuple-element.119.refs_3_, ...), custom_call_target="tpu_custom_call" | custom-call | flops 5000000000 | bytes 5000000 | tf_op jit(solution)/shard_map/pallas_call | solution.py:72
  203.5 16.5 %shard_map.170 = (bf16[1024,512]{1,0:T(8,128)(2,1)}, bf16[1024,512]{1,0:T(8,128)(2,1)}, bf16[1024,512]{1,0:T(8,128)(2,1)}) custom-call(s32[4]{0:T(128)} %pad_add_fusion.refs_0_, bf16[1024,512]{1,0:T(8,128)(2,1)} %get-tuple-element.117.refs_1_, ...), custom_call_target="tpu_custom_call", output_to_operand_aliasing={{0}: (7, {}), {1}: (8, {}), {2}: (9, {})} | custom-call | flops 15000000512 | bytes 5000000 | tf_op jit(solution)/shard_map/pallas_call | solution.py:72
  220.0 6.4 %shard_map.171 = (bf16[2,4,96,512]{3,2,1,0:T(8,128)(2,1)}, bf16[2,4,96,512]{3,2,1,0:T(8,128)(2,1)}) custom-call(s32[4]{0:T(128)} %pad_add_fusion.refs_0_, bf16[1024,512]{1,0:T(8,128)(2,1)} %get-tuple-element.116.refs_2_.refs_7_.refs_1_, bf16[1024,512]{1,0:T(8,128)(2,1)} %get-tuple-element.134.refs_2_.refs_3_, ...), custom_call_target="tpu_custom_call" | custom-call | flops 1610612736 | bytes 9000000 | tf_op jit(solution)/shard_map/pallas_call | solution.py:72
  227.4 30.6 %shard_map.172 = (f32[1024,512]{1,0:T(8,128)}, bf16[1024,512]{1,0:T(8,128)(2,1)}, f32[1024,512]{1,0:T(8,128)}, bf16[1024,512]{1,0:T(8,128)(2,1)}, bf16[1024,512]...) custom-call(s32[4]{0:T(128)} %pad_add_fusion.refs_0_, ...), custom_call_target="tpu_custom_call" | custom-call | flops 13958643712 | bytes 40000000 | tf_op jit(solution)/shard_map/pallas_call | solution.py:72
  258.6 5.8 %collective-permute-done.16 = bf16[2,4,96,512]{3,2,1,0:T(8,128)(2,1)S(1)} collective-permute-done((bf16[2,4,96,512]{3,2,1,0:T(8,128)(2,1)S(1)}, bf16[2,4,96,512]{3,2,1,0:T(8,128)(2,1)S(1)}, u32[]{:S(2)}, u32[]{:S(2)}) %collective-permute-start.16) | collective-permute-done | bytes 786464 | tf_op jit(solution)/shard_map/ppermute | solution.py:599
  265.3 7.7 %shard_map.173 = (bf16[1024,512]{1,0:T(8,128)(2,1)}, bf16[1024,512]{1,0:T(8,128)(2,1)}, bf16[1024,512]{1,0:T(8,128)(2,1)}) custom-call(s32[4]{0:T(128)} %pad_add_fusion.refs_0_, bf16[1024,512]{1,0:T(8,128)(2,1)} %get-tuple-element.99.refs_1_, bf16[1024,512]{1,0:T(8,128)(2,1)} %get-tuple-element.100.refs_2_, bf16[1024,512]{1,0:T(8,128)(2,1)} %get-tuple-element.101.refs_3_, ...), custom_call_target="tpu_custom_call" | custom-call | flops 5000000000 | bytes 5000000 | tf_op jit(solution)/shard_map/pallas_call | solution.py:72
  279.9 16.3 %shard_map.174 = (bf16[1024,512]{1,0:T(8,128)(2,1)}, bf16[1024,512]{1,0:T(8,128)(2,1)}, bf16[1024,512]{1,0:T(8,128)(2,1)}) custom-call(s32[4]{0:T(128)} %pad_add_fusion.refs_0_, bf16[1024,512]{1,0:T(8,128)(2,1)} %get-tuple-element.99.refs_1_, ...), custom_call_target="tpu_custom_call", output_to_operand_aliasing={{0}: (7, {}), {1}: (8, {}), {2}: (9, {})} | custom-call | flops 15000000512 | bytes 5000000 | tf_op jit(solution)/shard_map/pallas_call | solution.py:72
  297.1 5.4 %collective-permute-done.17.refs_5_ = bf16[1024,512]{1,0:T(8,128)(2,1)S(1)} collective-permute-done((bf16[1024,512]{1,0:T(8,128)(2,1)}, bf16[1024,512]{1,0:T(8,128)(2,1)S(1)}, u32[]{:S(2)}, u32[]{:S(2)}) %collective-permute-start.17) | collective-permute-done | bytes 1048608 | tf_op jit(solution)/shard_map/ppermute | solution.py:603
  303.6 6.5 %shard_map.175 = (bf16[2,4,96,512]{3,2,1,0:T(8,128)(2,1)}, bf16[2,4,96,512]{3,2,1,0:T(8,128)(2,1)}) custom-call(s32[4]{0:T(128)} %pad_add_fusion.refs_0_, bf16[1024,512]{1,0:T(8,128)(2,1)} %get-tuple-element.98.refs_2_.refs_18_.refs_1_, bf16[1024,512]{1,0:T(8,128)(2,1)} %get-tuple-element.156.refs_2_.refs_3_, ...), custom_call_target="tpu_custom_call" | custom-call | flops 1610612736 | bytes 9000000 | tf_op jit(solution)/shard_map/pallas_call | solution.py:72
  316.8 9.6 %shard_map.176 = (f32[1024,512]{1,0:T(8,128)}, bf16[1024,512]{1,0:T(8,128)(2,1)}) custom-call(s32[4]{0:T(128)} %pad_add_fusion.refs_0_, bf16[1024,512]{1,0:T(8,128)(2,1)} %select_bitcast_fusion.4.refs_1_, f32[1024,512]{1,0:T(8,128)} %get-tuple-element.147.refs_2_, bf16[1024,512]{1,0:T(8,128)(2,1)} %get-tuple-element.156.refs_2_.refs_3_, ...), custom_call_target="tpu_custom_call" | custom-call | flops 2147483648 | bytes 12000000 | tf_op jit(solution)/shard_map/pallas_call | solution.py:72
  348.5 6.9 %collective-permute-done.25.refs_2_ = bf16[96,512]{1,0:T(8,128)(2,1)S(1)} collective-permute-done((bf16[96,512]{1,0:T(8,128)(2,1)S(1)}, bf16[96,512]{1,0:T(8,128)(2,1)S(1)}, u32[]{:S(2)}, u32[]{:S(2)}) %collective-permute-start.25) | collective-permute-done | bytes 98336 | tf_op jit(solution)/shard_map/ppermute | solution.py:603
  363.1 5.1 %collective-permute-done.32.refs_6_ = bf16[368,512]{1,0:T(8,128)(2,1)S(1)} collective-permute-done((bf16[368,512]{1,0:T(8,128)(2,1)}, bf16[368,512]{1,0:T(8,128)(2,1)S(1)}, u32[]{:S(2)}, u32[]{:S(2)}) %collective-permute-start.32) | collective-permute-done | bytes 376864 | tf_op jit(solution)/shard_map/ppermute | solution.py:603
  (165 shorter events, 107.0 us)
Async XLA Ops:
  7.2 92.5 %all-gather.5.cloned.1.call-start = ((), (), s32[]{:S(2)}) async-start(), calls=%async_computation.4 | async-start | bytes 6127616 | tf_op jit(solution)/shard_map/all_gather | solution.py:845
  25.6 134.4 %all-gather.7.cloned.1.call-start = ((), (), s32[]{:S(2)}) async-start(), calls=%async_computation.5 | async-start | bytes 6127616 | tf_op jit(solution)/shard_map/all_gather | solution.py:860
  35.6 16.1 %collective-permute-start.2 = (bf16[112,512]{1,0:T(8,128)(2,1)S(1)}, bf16[112,512]{1,0:T(8,128)(2,1)S(1)}, u32[]{:S(2)}, u32[]{:S(2)}) collective-permute-start(bf16[112,512]{1,0:T(8,128)(2,1)S(1)} %get-tuple-element.215), channel_id=1, source_target_pairs={{0,8},{1,9},{2,10},{3,11},{4,12},{5,13},{6,14},{7,15},{8,0},{9,1},... | collective-permute-start | bytes 344072 | tf_op jit(solution)/shard_map/ppermute | solution.py:595
  35.6 16.1 %collective-permute-start.1 = (bf16[112,512]{1,0:T(8,128)(2,1)S(1)}, bf16[112,512]{1,0:T(8,128)(2,1)S(1)}, u32[]{:S(2)}, u32[]{:S(2)}) collective-permute-start(bf16[112,512]{1,0:T(8,128)(2,1)S(1)} %get-tuple-element.215), channel_id=1, source_target_pairs={{0,4},{1,5},{2,6},{3,7},{4,8},{5,9},{6,10},{7,11},{8,12},{9,13},{1... | collective-permute-start | bytes 344072 | tf_op jit(solution)/shard_map/ppermute | solution.py:595
  53.2 14.2 %collective-permute-start.5 = (bf16[4,112,512]{2,1,0:T(8,128)(2,1)S(1)}, bf16[4,112,512]{2,1,0:T(8,128)(2,1)S(1)}, u32[]{:S(2)}, u32[]{:S(2)}) collective-permute-start(bf16[4,112,512]{2,1,0:T(8,128)(2,1)S(1)} %pad_maximum_fusion.1.refs_2_.refs_9_), channel_id=1, source_target_pairs={{0,1},{1,0},{2,3},{3,2},{4,5},{5,4},{6,7},{7,6},{8,9},{9,8},{10,11... | collective-permute-start | bytes 1376264 | tf_op jit(solution)/shard_map/ppermute | solution.py:599
  61.4 23.4 %collective-permute-start.9 = (bf16[112,512]{1,0:T(8,128)(2,1)S(1)}, bf16[112,512]{1,0:T(8,128)(2,1)S(1)}, u32[]{:S(2)}, u32[]{:S(2)}) collective-permute-start(bf16[112,512]{1,0:T(8,128)(2,1)S(1)} %get-tuple-element.105), channel_id=1, source_target_pairs={{0,12},{1,13},{2,14},{3,15},{4,0},{5,1},{6,2},{7,3},{8,4},{9,5},{1... | collective-permute-start | bytes 344072 | tf_op jit(solution)/shard_map/ppermute | solution.py:595
  61.4 27.0 %collective-permute-start.8 = (bf16[112,512]{1,0:T(8,128)(2,1)S(1)}, bf16[112,512]{1,0:T(8,128)(2,1)S(1)}, u32[]{:S(2)}, u32[]{:S(2)}) collective-permute-start(bf16[112,512]{1,0:T(8,128)(2,1)S(1)} %get-tuple-element.105), channel_id=1, source_target_pairs={{0,8},{1,9},{2,10},{3,11},{4,12},{5,13},{6,14},{7,15},{8,0},{9,1},... | collective-permute-start | bytes 344072 | tf_op jit(solution)/shard_map/ppermute | solution.py:595
  65.3 23.1 %collective-permute-start.7 = (bf16[112,512]{1,0:T(8,128)(2,1)S(1)}, bf16[112,512]{1,0:T(8,128)(2,1)S(1)}, u32[]{:S(2)}, u32[]{:S(2)}) collective-permute-start(bf16[112,512]{1,0:T(8,128)(2,1)S(1)} %get-tuple-element.105), channel_id=1, source_target_pairs={{0,4},{1,5},{2,6},{3,7},{4,8},{5,9},{6,10},{7,11},{8,12},{9,13},{1... | collective-permute-start | bytes 344072 | tf_op jit(solution)/shard_map/ppermute | solution.py:595
  99.7 235.0 %reduce-scatter.3.cloned.1.call-start = ((), (), s32[]{:S(2)}) async-start(), calls=%async_computation.2 | async-start | bytes 3391488 | tf_op jit(solution)/shard_map/reduce_scatter | solution.py:672
  100.0 19.5 %collective-permute-start.11 = (bf16[4,112,512]{2,1,0:T(8,128)(2,1)S(1)}, bf16[4,112,512]{2,1,0:T(8,128)(2,1)S(1)}, u32[]{:S(2)}, u32[]{:S(2)}) collective-permute-start(bf16[4,112,512]{2,1,0:T(8,128)(2,1)S(1)} %copy-done.16), channel_id=1, source_target_pairs={{0,2},{1,3},{2,0},{3,1},{4,6},{5,7},{6,4},{7,5},{8,10},{9,11},{10,... | collective-permute-start | bytes 1376264 | tf_op jit(solution)/shard_map/ppermute | solution.py:599
  120.1 28.8 %collective-permute-start.14 = (bf16[1024,512]{1,0:T(8,128)(2,1)S(1)}, bf16[1024,512]{1,0:T(8,128)(2,1)S(1)}, u32[]{:S(2)}, u32[]{:S(2)}) collective-permute-start(bf16[1024,512]{1,0:T(8,128)(2,1)S(1)} %select_bitcast_fusion.3), channel_id=1, source_target_pairs={{0,16},{16,0},{1,17},{17,1},{2,18},{18,2},{3,19},{19,3},{4,20},{20... | collective-permute-start | bytes 3145736 | tf_op jit(solution)/shard_map/ppermute | solution.py:603
  191.1 35.3 %collective-permute-start.15 = (bf16[1024,512]{1,0:T(8,128)(2,1)S(1)}, bf16[1024,512]{1,0:T(8,128)(2,1)S(1)}, u32[]{:S(2)}, u32[]{:S(2)}) collective-permute-start(bf16[1024,512]{1,0:T(8,128)(2,1)S(1)} %broadcast_select_fusion.1), channel_id=1, source_target_pairs={{0,16},{16,0},{1,17},{17,1},{2,18},{18,2},{3,19},{19,3},{4,20},{20... | collective-permute-start | bytes 3145736 | tf_op jit(solution)/shard_map/ppermute | solution.py:603
  203.4 152.8 %reduce-scatter.5.cloned.1.call-start = ((), (), s32[]{:S(2)}) async-start(), calls=%async_computation.3 | async-start | bytes 3391488 | tf_op jit(solution)/shard_map/reduce_scatter | solution.py:672
  258.1 14.9 %collective-permute-start.31 = (bf16[8,368,512]{2,1,0:T(8,128)(2,1)}, bf16[8,368,512]{2,1,0:T(8,128)(2,1)S(1)}, u32[]{:S(2)}, u32[]{:S(2)}) collective-permute-start(bf16[8,368,512]{2,1,0:T(8,128)(2,1)} %get-tuple-element.175), channel_id=1, source_target_pairs={{0,1},{1,0},{2,3},{3,2},{4,5},{5,4},{6,7},{7,6},{8,9},{9,8},{10,11... | collective-permute-start | bytes 9043976 | tf_op jit(solution)/shard_map/ppermute | solution.py:599
  275.5 27.1 %collective-permute-start.17 = (bf16[1024,512]{1,0:T(8,128)(2,1)}, bf16[1024,512]{1,0:T(8,128)(2,1)S(1)}, u32[]{:S(2)}, u32[]{:S(2)}) collective-permute-start(bf16[1024,512]{1,0:T(8,128)(2,1)} %get-tuple-element.151), channel_id=1, source_target_pairs={{0,16},{1,17},{2,18},{3,19},{4,20},{5,21},{6,22},{7,23},{8,24},{9,... | collective-permute-start | bytes 3145736 | tf_op jit(solution)/shard_map/ppermute | solution.py:603
  279.4 16.8 %collective-permute-start.18 = (bf16[4,96,512]{2,1,0:T(8,128)(2,1)S(1)}, bf16[4,96,512]{2,1,0:T(8,128)(2,1)S(1)}, u32[]{:S(2)}, u32[]{:S(2)}) collective-permute-start(bf16[4,96,512]{2,1,0:T(8,128)(2,1)S(1)} %copy-done.20), channel_id=1, source_target_pairs={{0,2},{1,3},{2,0},{3,1},{4,6},{5,7},{6,4},{7,5},{8,10},{9,11},{10,... | collective-permute-start | bytes 1179656 | tf_op jit(solution)/shard_map/ppermute | solution.py:599
  311.9 15.8 %collective-permute-start.28 = (bf16[96,512]{1,0:T(8,128)(2,1)S(1)}, bf16[96,512]{1,0:T(8,128)(2,1)S(1)}, u32[]{:S(2)}, u32[]{:S(2)}) collective-permute-start(bf16[96,512]{1,0:T(8,128)(2,1)S(1)} %copy-done.25), channel_id=1, source_target_pairs={{0,12},{1,13},{2,14},{3,15},{4,0},{5,1},{6,2},{7,3},{8,4},{9,5},{1... | collective-permute-start | bytes 294920 | tf_op jit(solution)/shard_map/ppermute | solution.py:595
  314.0 13.8 %collective-permute-start.27 = (bf16[96,512]{1,0:T(8,128)(2,1)S(1)}, bf16[96,512]{1,0:T(8,128)(2,1)S(1)}, u32[]{:S(2)}, u32[]{:S(2)}) collective-permute-start(bf16[96,512]{1,0:T(8,128)(2,1)S(1)} %copy-done.24), channel_id=1, source_target_pairs={{0,8},{1,9},{2,10},{3,11},{4,12},{5,13},{6,14},{7,15},{8,0},{9,1},... | collective-permute-start | bytes 294920 | tf_op jit(solution)/shard_map/ppermute | solution.py:595
  314.9 12.8 %collective-permute-start.26 = (bf16[96,512]{1,0:T(8,128)(2,1)S(1)}, bf16[96,512]{1,0:T(8,128)(2,1)S(1)}, u32[]{:S(2)}, u32[]{:S(2)}) collective-permute-start(bf16[96,512]{1,0:T(8,128)(2,1)S(1)} %copy-done.23), channel_id=1, source_target_pairs={{0,4},{1,5},{2,6},{3,7},{4,8},{5,9},{6,10},{7,11},{8,12},{9,13},{1... | collective-permute-start | bytes 294920 | tf_op jit(solution)/shard_map/ppermute | solution.py:595
  316.0 14.7 %collective-permute-start.21 = (bf16[4,96,512]{2,1,0:T(8,128)(2,1)S(1)}, bf16[4,96,512]{2,1,0:T(8,128)(2,1)S(1)}, u32[]{:S(2)}, u32[]{:S(2)}) collective-permute-start(bf16[4,96,512]{2,1,0:T(8,128)(2,1)S(1)} %fusion.1.refs_13_), channel_id=1, source_target_pairs={{0,2},{1,3},{2,0},{3,1},{4,6},{5,7},{6,4},{7,5},{8,10},{9,11},{10,... | collective-permute-start | bytes 1179656 | tf_op jit(solution)/shard_map/ppermute | solution.py:599
  326.4 29.0 %collective-permute-start.20 = (bf16[1024,512]{1,0:T(8,128)(2,1)}, bf16[1024,512]{1,0:T(8,128)(2,1)}, u32[]{:S(2)}, u32[]{:S(2)}) collective-permute-start(bf16[1024,512]{1,0:T(8,128)(2,1)} %get-tuple-element.165), channel_id=1, source_target_pairs={{16,0},{17,1},{18,2},{19,3},{20,4},{21,5},{22,6},{23,7},{24,8},{25... | collective-permute-start | bytes 3145736 | tf_op jit(solution)/shard_map/ppermute | solution.py:603
  335.8 19.7 %collective-permute-start.30 = (bf16[464,512]{1,0:T(8,128)(2,1)S(1)}, bf16[464,512]{1,0:T(8,128)(2,1)S(1)}, u32[]{:S(2)}, u32[]{:S(2)}) collective-permute-start(bf16[464,512]{1,0:T(8,128)(2,1)S(1)} %pad_maximum_fusion), channel_id=1, source_target_pairs={{0,16},{1,17},{2,18},{3,19},{4,20},{5,21},{6,22},{7,23},{8,24},{9,... | collective-permute-start | bytes 1425416 | tf_op jit(solution)/shard_map/ppermute | solution.py:603
  343.7 11.7 %collective-permute-start.25 = (bf16[96,512]{1,0:T(8,128)(2,1)S(1)}, bf16[96,512]{1,0:T(8,128)(2,1)S(1)}, u32[]{:S(2)}, u32[]{:S(2)}) collective-permute-start(bf16[96,512]{1,0:T(8,128)(2,1)S(1)} %get-tuple-element.196), channel_id=1, source_target_pairs={{16,0},{17,1},{18,2},{19,3},{20,4},{21,5},{22,6},{23,7},{24,8},{25... | collective-permute-start | bytes 294920 | tf_op jit(solution)/shard_map/ppermute | solution.py:603
  356.3 12.0 %collective-permute-start.32 = (bf16[368,512]{1,0:T(8,128)(2,1)}, bf16[368,512]{1,0:T(8,128)(2,1)S(1)}, u32[]{:S(2)}, u32[]{:S(2)}) collective-permute-start(bf16[368,512]{1,0:T(8,128)(2,1)} %bitcast.92), channel_id=1, source_target_pairs={{16,0},{17,1},{18,2},{19,3},{20,4},{21,5},{22,6},{23,7},{24,8},{25... | collective-permute-start | bytes 1130504 | tf_op jit(solution)/shard_map/ppermute | solution.py:603
  (43 other events, 409.2 us)
Sparse Core Ops, SparseCore 0:
  25.8 73.9 all-gather.4
  102.0 58.0 all-gather.6
  203.5 71.4 reduce-scatter.2
  279.5 76.7 reduce-scatter.4
